TPU v7x, 32 devices: a whole 2x2x4 slice. The times are simulated.
32 devices in a mesh: feat: 8 (over z, y), ex: 4 (over x, core).
Axes of the slice: x: 2, y: 2, z: 4, core: 2. Of those that a mesh axis runs over, the one named last changes fastest.
Arguments:
- activations: bfloat16 [1024, 28672], P('ex', 'feat'), may hold values from -6 to 6
- out_grads: bfloat16 [1024, 8192], P('feat', 'ex'), may hold values from -6 to 6
- basis_in: bfloat16 [28672, 28672], P('feat', 'ex'), may hold values from -0.03125 to 0.03125
- basis_out: bfloat16 [8192, 8192], P('ex', 'feat'), may hold values from -0.0625 to 0.0625
Outputs:
- correction: float32 [8192, 28672], P('feat', 'ex')
All inputs are finite; a program needn't handle non-finite values.
Results may differ from a plain program's by a relative error of at most 0.0034.
Values may be sent and summed in bfloat16 or wider, within the bound.
No kernel may reach another device: no remote copies, remote signals or barrier semaphores. Data moves between devices by JAX's collectives and lax.ppermute only.
A program may use at most 192 MiB of HBM per device.

v0:
```python
import jax
import jax.numpy as jnp
from jax import lax
from jax.sharding import PartitionSpec as P

SEQ_LEN = 256


def per_device(activations, out_grads, basis_in, basis_out):
    partial_in = jnp.dot(
        lax.all_gather(activations, "ex", axis=0, tiled=True),
        basis_in,
        preferred_element_type=jnp.float32,
    )
    rotated_in = lax.psum(partial_in, "feat").astype(jnp.bfloat16)
    grad_all = lax.all_gather(out_grads, "feat", axis=0, tiled=True)
    out_share = lax.psum_scatter(
        jnp.dot(grad_all, basis_out, preferred_element_type=jnp.float32),
        "ex",
        scatter_dimension=0,
        tiled=True,
    )
    rotated_out = lax.all_gather(out_share.astype(jnp.bfloat16), "ex", axis=0, tiled=True)
    tokens_all = rotated_in.shape[0]
    seq_count = tokens_all // SEQ_LEN
    in_blocks = rotated_in.reshape(seq_count, SEQ_LEN, rotated_in.shape[1])
    out_blocks = rotated_out.reshape(seq_count, SEQ_LEN, rotated_out.shape[1])
    per_seq = jnp.einsum("nto,nti->noi", out_blocks, in_blocks, preferred_element_type=jnp.float32)
    total = jnp.sum(per_seq * per_seq, axis=0)
    return total / jnp.float32(tokens_all)


def solution(mesh):
    return jax.shard_map(
        per_device,
        mesh=mesh,
        in_specs=(P("ex", "feat"), P("feat", "ex"), P("feat", "ex"), P("ex", "feat")),
        out_specs=P("feat", "ex"),
        check_vma=False,
    )
```

profile of v0, /device:TPU:0, one launch (start us, length us, event | category | flops | bytes accessed | tf_op | source)
XLA Modules:
  0.0 1387.1 jit_solution(5466520336447878459)
XLA Ops:
  6.5 0.0 all-gather.4.cloned.1.call-start
  6.5 0.7 all-gather.4.cloned.1.call-update
  7.3 0.0 all-gather.8.cloned.1.call-start
  7.3 0.7 all-gather.8.cloned.1.call-update
  8.0 0.0 reduce-scatter.2.cloned.1.call-start
  8.1 77.6 %all-gather.4.cloned.1.call-done = bf16[1024,2048]{1,0:T(8,128)(2,1)} async-done(((bf16[128,2048]{1,0:T(8,128)(2,1)}), bf16[1024,2048]{1,0:T(8,128)(2,1)}) %all-gather.4.cloned.1.call-update) | async-done | bytes 4194320 | tf_op jit(solution)/shard_map/all_gather | solution.py:16
  85.6 10.0 fusion
  95.7 0.0 reduce-scatter.2.cloned.1.call-update
  95.7 0.0 all-gather.6.cloned.1.call-start
  95.7 42.1 %all-gather.8.cloned.1.call-done = bf16[1024,3584]{1,0:T(8,128)(2,1)} async-done(((bf16[256,3584]{1,0:T(8,128)(2,1)}), bf16[1024,3584]{1,0:T(8,128)(2,1)}) %all-gather.8.cloned.1.call-update) | async-done | bytes 7340048 | tf_op jit(solution)/shard_map/all_gather | solution.py:11
  137.8 61.3 %fusion.1 = f32[1024,7168]{1,0:T(8,128)} fusion(bf16[1024,3584]{1,0:T(8,128)(2,1)} %all-gather.8.cloned.1.call-done, bf16[3584,7168]{1,0:T(8,128)(2,1)} %param.6), kind=kOutput, calls=%fused_computation.3 | convolution fusion | flops 52613349376 | bytes 88080384 | tf_op jit(solution)/shard_map/dot_general | solution.py:10
  199.1 0.0 reduce-scatter.2.cloned.1.call-done
  199.1 2.1 convert_element_type.6
  201.2 0.0 all-gather.6.cloned.1.call-update
  201.3 1122.0 %all-reduce.1 = bf16[1024,7168]{1,0:T(8,128)(2,1)} all-reduce(f32[1024,7168]{1,0:T(8,128)} %fusion.1), channel_id=1, replica_groups=mesh['feat'=8,'ex'=4] {'feat'}, use_global_device_ids=true, to_apply=%region_1.0 | all-reduce | flops 7340032 | bytes 44040192 | tf_op jit(solution)/shard_map/psum | solution.py:15
  1323.2 0.0 all-gather.6.cloned.1.call-done
  1323.2 34.3 %multiply_reduce_fusion = f32[1024,7168]{1,0:T(8,128)} fusion(bf16[4,256,1024]{2,1,0:T(8,128)(2,1)} %bitcast.9, bf16[4,256,7168]{2,1,0:T(8,128)(2,1)} %bitcast.8), kind=kOutput, calls=%fused_computation | convolution fusion | flops 15083765760 | bytes 46137344 | tf_op jit(solution)/shard_map/nto,nti->noi/dot_general | solution.py:28
  1357.6 23.0 %broadcast_multiply_fusion = f32[1024,7168]{1,0:T(8,128)} fusion(f32[1024,7168]{1,0:T(8,128)} %multiply_reduce_fusion), kind=kLoop, calls=%fused_computation.1 | loop fusion | flops 7340032 | bytes 58720256 | tf_op jit(solution)/shard_map/div | solution.py:30
Async XLA Ops:
  6.5 79.1 %all-gather.4.cloned.1.call-start = ((), (), s32[]{:S(2)}) async-start(), calls=%async_computation.1 | async-start | bytes 4718592 | tf_op jit(solution)/shard_map/all_gather | solution.py:16
  7.3 130.5 %all-gather.8.cloned.1.call-start = ((), (), s32[]{:S(2)}) async-start(), calls=%async_computation.4 | async-start | bytes 9175040 | tf_op jit(solution)/shard_map/all_gather | solution.py:11
  8.0 191.1 %reduce-scatter.2.cloned.1.call-start = ((), (), s32[]{:S(2)}) async-start(), calls=%async_computation.2 | async-start | bytes 5242880 | tf_op jit(solution)/shard_map/reduce_scatter | solution.py:17
  95.7 1227.6 %all-gather.6.cloned.1.call-start = ((), (), s32[]{:S(2)}) async-start(), calls=%async_computation.3 | async-start | bytes 2621440 | tf_op jit(solution)/shard_map/all_gather | solution.py:23
Sparse Core Ops, SparseCore 0:
  9.5 76.0 all-gather.3
  87.2 50.5 all-gather.7
  140.3 44.4 reduce-scatter.1
  201.4 22.5 all-gather.5
where the time goes:
time: 1390 us
  blocking collectives  1120 us (81%)
  waiting for transfers between devices  121 us (9%)
  matrix products  106 us (8%)
  other arithmetic  25.1 us (2%)
    psum x1, blocking collectives, per_device(): rotated_in = lax.psum(partial_in, 'feat').astype(jnp.bfloat16)  1120 us
    all_gather x1, waiting for transfers between devices, per_device(): grad_all = lax.all_gather(out_grads, 'feat', axis=0, tiled=True)  77.6 us
    dot_general x1, matrix products, per_device(): jnp.dot(lax.all_gather(activations, 'ex', axis=0, tiled=True), basis_in,...  61.3 us
    all_gather x1, waiting for transfers between devices, per_device(): lax.all_gather(activations, 'ex', axis=0, tiled=True)  42.1 us
    dot_general x1, matrix products, per_device(): jnp.einsum('nto,nti->noi', out_blocks, in_blocks, preferred_element_type=...  34.3 us
  transfers between devices with their start and end apart: 4, of which 2 were waited for; matrix products, arithmetic and copies ran while one was open for 5% of the time, Pallas kernels for 0%

commit v1 on v0

v1 whole, which is shorter than its diff:
```python
import jax
import jax.numpy as jnp
from jax import lax
from jax.experimental import pallas as pl
from jax.experimental.pallas import tpu as pltpu
from jax.sharding import PartitionSpec as P

SEQ_LEN = 256
PARTS = 4
WIDTH = 256
BF16 = jnp.bfloat16
F32 = jnp.float32


def square_kernel(scale, out_t, p0, p1, p2, p3, *rest):
    result = rest[-1]
    total = None
    for n, piece in enumerate((p0, p1, p2, p3)):
        rows = piece.shape[0]
        for s in range(rows // SEQ_LEN):
            left = out_t[:, n * rows + s * SEQ_LEN : n * rows + (s + 1) * SEQ_LEN]
            right = piece[s * SEQ_LEN : (s + 1) * SEQ_LEN, :]
            product = jnp.dot(left, right, preferred_element_type=F32)
            total = product * product if total is None else total + product * product
    result[...] = total * scale


def square_into(buffer, out_t, pieces, first, width, full, scale):
    tile = 256
    rows = out_t.shape[0]
    depth = pieces[0].shape[0]
    offset = first // tile
    in_specs = [pl.BlockSpec(out_t.shape, lambda j: (0, 0))]
    in_specs += [pl.BlockSpec((depth, tile), lambda j: (0, j)) for _ in pieces]
    operands = [out_t, *pieces]
    aliases = {}
    if buffer is not None:
        in_specs.append(pl.BlockSpec(memory_space=pl.ANY))
        operands.append(buffer)
        aliases = {len(operands) - 1: 0}

    def body(*refs):
        square_kernel(scale, *refs)

    return pl.pallas_call(
        body,
        grid=(width // tile,),
        in_specs=in_specs,
        out_specs=pl.BlockSpec((rows, tile), lambda j: (0, offset + j)),
        out_shape=jax.ShapeDtypeStruct((rows, full), F32),
        input_output_aliases=aliases,
        compiler_params=pltpu.CompilerParams(vmem_limit_bytes=32 * 1024 * 1024),
        cost_estimate=pl.CostEstimate(
            flops=2 * rows * width * out_t.shape[1],
            bytes_accessed=rows * width * 4 + out_t.size * 2 + PARTS * depth * width * 2,
            transcendentals=0,
        ),
    )(*operands)


def call(kernel, flags, operands, in_specs, outputs, out_specs, grid, cost, aliases, vmem):
    return pl.pallas_call(
        kernel,
        grid_spec=pltpu.PrefetchScalarGridSpec(
            num_scalar_prefetch=1, grid=grid, in_specs=in_specs, out_specs=out_specs
        ),
        out_shape=outputs,
        input_output_aliases=aliases or {},
        compiler_params=pltpu.CompilerParams(vmem_limit_bytes=vmem * 1024 * 1024),
        cost_estimate=cost,
    )(flags, *operands)


def unit_list(count):
    lead = 6
    units = [[(0, i)] for i in range(4)] + [[(0, 4), (0, 5)]]
    units += [[(1, i), (1, i + 1)] for i in range(0, lead, 2)]
    rest = [(half, i) for i in range(lead, count) for half in (0, 1)]
    while rest:
        size = 2 if len(rest) > 8 else 1
        units.append(rest[:size])
        rest = rest[size:]
    return units


class Chain:
    def __init__(self, flags):
        self.flags = flags
        self.token = jnp.zeros((8, 128), F32)
        self.also = []

    def run(self, body, operands, in_specs, outputs, out_specs, grid, flops, size, aliases=None, vmem=12):
        waits = [self.token, *self.also]
        self.also = []
        count, made = len(operands), len(outputs)
        keep = pl.BlockSpec(memory_space=pl.ANY)

        def kernel(flags, *refs):
            refs[-1][...] = jnp.zeros((8, 128), F32)
            body(flags, refs[:count], refs[count + len(waits) : -1])

        results = call(
            kernel,
            self.flags,
            [*operands, *waits],
            [*in_specs, *[keep] * len(waits)],
            [*outputs, jax.ShapeDtypeStruct((8, 128), F32)],
            [*out_specs, pl.BlockSpec((8, 128), lambda *_: (0, 0))],
            grid,
            pl.CostEstimate(flops=flops, bytes_accessed=size, transcendentals=0),
            aliases,
            vmem,
        )
        self.token = results[made]
        return results[:made]


def multiply(chain, blocks, matrix, first, width, tile=256):
    rows = sum(block.shape[0] for block in blocks)
    inner = matrix.shape[0]
    base = first // tile

    def body(flags, ins, outs):
        (result,) = outs
        start = 0
        for block in ins[:-1]:
            here = slice(start, start + block.shape[0])
            start += block.shape[0]
            result[here, :] = jnp.dot(block[...], ins[-1][...], preferred_element_type=F32)

    return chain.run(
        body,
        [*blocks, matrix],
        [pl.BlockSpec(block.shape, lambda j, flags: (0, 0), pipeline_mode=pl.Buffered(1)) for block in blocks]
        + [pl.BlockSpec((inner, tile), lambda j, flags: (0, base + j))],
        [jax.ShapeDtypeStruct((rows, width), F32)],
        [pl.BlockSpec((rows, tile), lambda j, flags: (0, j))],
        (width // tile,),
        2 * rows * inner * width,
        2 * inner * (rows + width) + 4 * rows * width,
        vmem=18,
    )[0]


def relay(chain, value):
    tile = 128

    def body(flags, ins, outs):
        outs[0][...] = ins[0][...]

    spec = pl.BlockSpec((tile, value.shape[1]), lambda r, flags: (r, 0))
    shape = jax.ShapeDtypeStruct(value.shape, value.dtype)
    return chain.run(body, [value], [spec], [shape], [spec], (value.shape[0] // tile,), 0, 4 * value.size)[0]


def layout(parts):
    offsets, total = {}, 0
    for name, rows, present in parts:
        if present:
            offsets[name] = total
            total += rows
    return offsets, total


class Lane:
    def __init__(self, chain, units, permute):
        self.chain, self.units, self.permute = chain, units, permute
        self.sent, self.got, self.state, self.places, self.partials = {}, {}, {}, {}, {}

    def subs(self, u):
        return len(self.units[u]) if 0 <= u < len(self.units) else 0

    def advance(self, k, partials):
        half, n = SEQ_LEN, self.subs
        self.partials[k] = partials
        places, sizes = {}, {}
        for link, parts in (
            ("y", (("a1", half, n(k)), ("a5", half, n(k - 4)), ("b3", half, n(k - 2)))),
            ("z", (("za", half, max(n(k - 1), n(k - 3))), ("zb", 2 * half, max(n(k), n(k - 4))))),
            ("m", (("a3", half, n(k - 2)), ("b2", half, n(k - 1)), ("b4", half, n(k - 3)))),
        ):
            places[link], sizes[link] = layout([(name, rows * count, count) for name, rows, count in parts])
        before = self.places
        operands, in_specs, names, outputs, out_specs, out_names = [], [], [], [], [], []
        size = 0

        def read(name, array, rows=None, block=0, first=0):
            nonlocal size
            rows = rows or array.shape[0]
            base = first // 128
            operands.append(array)
            in_specs.append(pl.BlockSpec((rows, 128), lambda j, flags: (block, base + j)))
            names.append(name)
            size += rows * WIDTH * array.dtype.itemsize

        def write(name, rows, dtype):
            nonlocal size
            outputs.append(jax.ShapeDtypeStruct((rows, WIDTH), dtype))
            out_specs.append(pl.BlockSpec((rows, 128), lambda j, flags: (0, j)))
            out_names.append(name)
            size += rows * WIDTH * jnp.dtype(dtype).itemsize

        for link, array in self.got.items():
            read("got_" + link, array)
        for link, array in self.sent.items():
            if (link == "z" and (n(k - 4) or n(k - 5))) or (link == "m" and n(k - 4)):
                read("sent_" + link, array)
        for age in (0, 1):
            for s in range(n(k - age)):
                array, block, first = self.partials[k - age][s]
                read(f"p{age}a{s}", array, 2 * half, block, first)
                read(f"p{age}b{s}", array, 2 * half, block, first + WIDTH)
        for name, u in (("a1", k - 2), ("b1", k - 2), ("a2", k - 3), ("b2", k - 3)):
            if n(u):
                read("old_" + name, self.state[name])
        for link, rows in sizes.items():
            if rows:
                write("out_" + link, rows, BF16)
        for name, u in (("a1", k - 1), ("b1", k - 1), ("a2", k - 2), ("b2", k - 2)):
            if n(u):
                write("new_" + name, half * n(u), F32)
        if n(k - 5):
            write("final", 2 * half * n(k - 5), BF16)

        def body(flags, ins, outs):
            refs = dict(zip(names + out_names, (*ins, *outs)))
            y, side, outer = flags[0], flags[1], flags[2] == 1

            def rows(start, count=half):
                return pl.ds(pl.multiple_of(start, 16), count)

            def put(link, part, value, extra=0):
                start = places[link][part] + extra
                refs["out_" + link][start : start + value.shape[0], :] = value.astype(BF16)

            def take(kind, link, part, extra=0, count=half):
                return refs[kind + "_" + link][rows(before[link][part] + extra, count), :]

            for s in range(n(k)):
                put("y", "a1", refs[f"p0a{s}"][rows((1 - y) * half), :], s * half)
            for s in range(n(k - 1)):
                total = refs[f"p1a{s}"][rows(y * half), :] + take("got", "y", "a1", s * half).astype(F32)
                refs["new_a1"][s * half : (s + 1) * half, :] = total

            @pl.when(outer)
            def _():
                for s in range(n(k)):
                    put("z", "zb", refs[f"p0b{s}"][...], s * 2 * half)
                if n(k - 1):
                    put("z", "za", refs["new_a1"][...])
                if n(k - 4):
                    put("y", "a5", take("got", "z", "za", 0, half * n(k - 4)))
                if n(k - 5):
                    refs["final"][...] = take("got", "z", "zb", 0, 2 * half * n(k - 5))

            @pl.when(jnp.logical_not(outer))
            def _():
                for s in range(n(k - 1)):
                    for keep, start in ((False, (1 - side) * half), (True, side * half)):
                        value = refs[f"p1b{s}"][rows(start), :]
                        value += take("got", "z", "zb", start + s * 2 * half).astype(F32)
                        if keep:
                            refs["new_b1"][s * half : (s + 1) * half, :] = value
                        else:
                            put("m", "b2", value, s * half)
                if n(k - 2):
                    whole = half * n(k - 2)
                    total = refs["old_a1"][...] + take("got", "z", "za", 0, whole).astype(F32)
                    put("m", "a3", total)
                    refs["new_a2"][...] = total
                    total = refs["old_b1"][...] + take("got", "m", "b2", 0, whole).astype(F32)
                    put("y", "b3", total)
                    refs["new_b2"][...] = total
                if n(k - 3):
                    whole = half * n(k - 3)
                    put("z", "za", refs["old_a2"][...] + take("got", "m", "a3", 0, whole).astype(F32))
                    put("m", "b4", refs["old_b2"][...] + take("got", "y", "b3", 0, whole).astype(F32))
                if n(k - 4):
                    put("y", "a5", take("sent", "z", "za", 0, half * n(k - 4)))
                for s in range(n(k - 4)):
                    put("z", "zb", take("sent", "m", "b4", s * half), s * 2 * half)
                    put("z", "zb", take("got", "m", "b4", s * half), s * 2 * half + half)
                if n(k - 5):
                    refs["final"][...] = take("sent", "z", "zb", 0, 2 * half * n(k - 5))

        made = self.chain.run(body, operands, in_specs, outputs, out_specs, (WIDTH // 128,), 0, size, vmem=4 + size // 2**20 * 5 // 4)
        made = dict(zip(out_names, made))
        ready = []
        for s in range(n(k - 5)):
            place = before["y"]["a5"] // half + s
            ready.append((self.units[k - 5][s], (self.sent["y"], self.got["y"], place, made["final"], s)))
        self.places = places
        self.sent = {link: made["out_" + link] for link in sizes if sizes[link]}
        self.got = {link: self.permute[link](value) for link, value in self.sent.items()}
        self.state = {name[4:]: value for name, value in made.items() if name.startswith("new_")}
        return ready


def square_chunk(chain, buffer, out_t, pair, index, full, scale):
    rows = out_t.shape[1]
    tile = 512
    operands, in_specs = [out_t], [pl.BlockSpec((PARTS, tile, SEQ_LEN), lambda r, flags: (0, r, 0))]
    for own, other, place, _, _ in pair:
        for array in (own, other):
            operands.append(array)
            in_specs.append(pl.BlockSpec((SEQ_LEN, WIDTH), lambda r, flags, place=place: (place, 0)))
    for *_, final, s in pair:
        operands.append(final)
        in_specs.append(pl.BlockSpec((2 * SEQ_LEN, WIDTH), lambda r, flags, s=s: (s, 0)))
    aliases = {}
    if buffer is not None:
        in_specs.append(pl.BlockSpec(memory_space=pl.ANY))
        operands.append(buffer)
        aliases = {len(operands): 0}

    def body(flags, ins, outs):
        y, side = flags[0], flags[1]
        left, a, b = ins[0], ins[1:5], ins[5:7]
        (result,) = outs

        def square(seq, right):
            product = jnp.dot(left[seq], right, preferred_element_type=F32)
            return product * product

        total = square(y, a[0][...]) + square(1 - y, a[1][...])
        total += square(2 + y, a[2][...]) + square(3 - y, a[3][...])
        result[:, :WIDTH] = total * scale
        total = square(side, b[0][:SEQ_LEN, :]) + square(1 - side, b[0][SEQ_LEN:, :])
        total += square(2 + side, b[1][:SEQ_LEN, :]) + square(3 - side, b[1][SEQ_LEN:, :])
        result[:, WIDTH:] = total * scale

    return chain.run(
        body,
        operands,
        in_specs,
        [jax.ShapeDtypeStruct((rows, full), F32)],
        [pl.BlockSpec((tile, 2 * WIDTH), lambda r, flags: (r, index))],
        (rows // tile,),
        4 * rows * WIDTH * PARTS * SEQ_LEN,
        rows * WIDTH * 8 + out_t.size * 2 + PARTS * SEQ_LEN * WIDTH * 4,
        aliases,
    )[0]


def make_per_device(feat, ex):
    depth = feat // 2
    mid = depth // 2

    def along_z(pairs):
        return [(a * 2 + y, b * 2 + y) for a, b in pairs for y in (0, 1)]

    inward = [along_z([(k, k + 1), (depth - 1 - k, depth - 2 - k)]) for k in range(mid - 1)]
    outward = [along_z([(k + 1, k), (depth - 2 - k, depth - 1 - k)]) for k in reversed(range(mid - 1))]
    middle = along_z([(mid - 1, mid), (mid, mid - 1)])
    y_swap = [(i, i ^ 1) for i in range(feat)]
    y_middle = [(i, i ^ 1) for i in range(feat) if i // 2 in (mid - 1, mid)]

    def swap_ex(value, bit):
        return lax.ppermute(value, "ex", [(i, i ^ bit) for i in range(ex)])

    def send(value, pairs):
        return lax.ppermute(value.astype(BF16), "feat", pairs)

    def gather_low(block):
        bit = 1
        while bit < ex // 2:
            block = jnp.concatenate([block, swap_ex(block, bit)], axis=0)
            bit *= 2
        return block

    def spread(value, z):
        for step, pairs in enumerate(outward):
            level = mid - 2 - step
            here = (z == level) | (z == depth - 1 - level)
            value = jnp.where(here, lax.ppermute(value, "feat", pairs), value)
        return value

    def tree_a(partial, y, z):
        half = partial.shape[0] // 2
        away = lax.dynamic_slice_in_dim(partial, (1 - y) * half, half, 0)
        total = lax.dynamic_slice_in_dim(partial, y * half, half, 0)
        total = total + send(away, y_swap).astype(F32)
        for pairs in inward:
            total = total + send(total, pairs).astype(F32)
        total = (total + send(total, middle).astype(F32)).astype(BF16)
        total = spread(total, z)
        return [total, lax.ppermute(total, "feat", y_swap)]

    def tree_b(partial, side, z):
        half = partial.shape[0] // 2
        for pairs in inward:
            partial = partial + send(partial, pairs).astype(F32)
        away = lax.dynamic_slice_in_dim(partial, (1 - side) * half, half, 0)
        total = lax.dynamic_slice_in_dim(partial, side * half, half, 0)
        total = total + send(away, middle).astype(F32)
        total = (total + send(total, y_middle).astype(F32)).astype(BF16)
        other = lax.ppermute(total, "feat", middle)
        return [spread(total, z), spread(other, z)]

    def pipelined(activations, out_grads, basis_in, basis_out, flags, ordered):
        columns = basis_in.shape[1]
        chain = Chain(flags)
        stay = [(k, k) for k in range(feat) if k // 2 in (0, depth - 1)]
        permute = {
            "y": lambda v: lax.ppermute(v, "feat", y_swap),
            "z": lambda v: lax.ppermute(v, "feat", inward[0] + outward[0]),
            "m": lambda v: lax.ppermute(v, "feat", middle + stay),
        }
        near = [activations, swap_ex(activations, 1)]
        far = swap_ex(activations, 2)
        grad_all = lax.all_gather(out_grads, "feat", axis=0, tiled=True)
        tokens_all = PARTS * activations.shape[0]
        tokens = [near, None]

        count = columns // (2 * WIDTH)
        units = unit_list(count)
        lanes = [Lane(chain, units[p::2], permute) for p in (0, 1)]
        finished, made = {}, {}
        result = rotated_out = out_t = None
        for j in range(len(units) + 12):
            lane, k = lanes[j % 2], j // 2
            if k >= len(lane.units) + 6:
                continue
            partials = None
            if lane.subs(k):
                unit = lane.units[k]
                if tokens[1] is None and j == 4:
                    far = relay(chain, far)
                    tokens[1] = [far, swap_ex(far, 1)]
                if unit[0] not in made:
                    group = list(unit)
                    if j + 1 < len(units) and len({half for half, _ in unit + units[j + 1]}) == len(unit) == 2:
                        if len({i for _, i in unit}) == 1:
                            group += units[j + 1]
                    halves = sorted({half for half, _ in group})
                    chunks = sorted({i for _, i in group})
                    blocks = [block for half in halves for block in tokens[half]]
                    wide = 2 * WIDTH * len(chunks)
                    array = multiply(chain, blocks, basis_in, chunks[0] * 2 * WIDTH, wide)
                    for half, i in group:
                        made[half, i] = (array, halves.index(half), chunks.index(i) * 2 * WIDTH)
                partials = [made[sub] for sub in unit]
            ready = lane.advance(k, partials)
            other = lanes[1 - j % 2].got
            if len(other) == 3 and len(lane.got) == 3:
                chain.also.append(other["m"])
            if j == 6:
                share = multiply(chain, [grad_all], basis_out, 0, basis_out.shape[1])
                share = lax.psum_scatter(share, "ex", scatter_dimension=0, tiled=True)
                rotated_out = lax.all_gather(share.astype(BF16), "ex", axis=0, tiled=True)
            if j == 14:
                out_t = ordered(rotated_out, 0).reshape(-1, PARTS, SEQ_LEN).transpose(1, 0, 2)
                chain.also.append(out_t)
            for (half, i), value in ready:
                finished[half, i] = value
                if (1 - half, i) in finished:
                    pair = (finished[0, i], finished[1, i])
                    result = square_chunk(chain, result, out_t, pair, i, columns, 1.0 / tokens_all)
        return result

    def per_device(activations, out_grads, basis_in, basis_out):
        place = lax.axis_index("feat")
        e = lax.axis_index("ex")
        y, z = place % 2, place // 2
        side = (z >= mid).astype(jnp.int32)
        columns = basis_in.shape[1]

        block = activations.shape[0]

        def ordered(rotated_out, flip):
            turned = []
            for q in range(PARTS):
                for r in range(ex // PARTS):
                    source = e ^ ((q ^ flip) * (ex // PARTS) + r)
                    turned.append(lax.dynamic_slice_in_dim(rotated_out, source * block, block, 0))
            return jnp.concatenate(turned, axis=0).T

        if depth == 4 and ex == PARTS and block == SEQ_LEN and columns % (2 * WIDTH) == 0:
            outer = ((z == 0) | (z == depth - 1)).astype(jnp.int32)
            flags = jnp.stack([y.astype(jnp.int32), side, outer])
            return pipelined(activations, out_grads, basis_in, basis_out, flags, ordered)

        far = swap_ex(activations, ex // 2)
        tokens_half = [gather_low(activations), gather_low(far)]
        tokens_all = 2 * tokens_half[0].shape[0]
        scale = 1.0 / tokens_all
        grad_all = lax.all_gather(out_grads, "feat", axis=0, tiled=True)
        out_share = lax.psum_scatter(
            jnp.dot(grad_all, basis_out, preferred_element_type=F32),
            "ex",
            scatter_dimension=0,
            tiled=True,
        )
        rotated_out = lax.all_gather(out_share.astype(BF16), "ex", axis=0, tiled=True)
        out_a, out_b = ordered(rotated_out, y), ordered(rotated_out, side)

        width = 512
        chunks = list(range(0, columns, width))
        lead = 4
        order = [(0, i) for i in range(min(lead, len(chunks)))]
        for i in range(len(chunks)):
            order.append((1, i))
            if i + lead < len(chunks):
                order.append((0, i + lead))
        pieces = {}
        result = None
        for half, i in order:
            first = chunks[i]
            partial = jnp.dot(tokens_half[half], basis_in[:, first : first + width], preferred_element_type=F32)
            if i % 2 == 0:
                pieces[half, i] = tree_a(partial, y, z)
            else:
                pieces[half, i] = tree_b(partial, side, z)
            if half == 1:
                result = square_into(
                    result, out_a if i % 2 == 0 else out_b, pieces[0, i] + pieces[1, i], first, width, columns, scale
                )
        return result

    return per_device


def solution(mesh):
    return jax.shard_map(
        make_per_device(mesh.shape["feat"], mesh.shape["ex"]),
        mesh=mesh,
        in_specs=(P("ex", "feat"), P("feat", "ex"), P("feat", "ex"), P("ex", "feat")),
        out_specs=P("feat", "ex"),
        check_vma=False,
    )
```

time: 1390 us -> 512 us (0.37)
  blocking collectives: 1120 us -> 0 us
  Pallas kernels: 0 us -> 221 us
  starting transfers between devices: 0.12 us -> 153 us
  matrix products: 106 us -> 0 us
  waiting for transfers between devices: 121 us -> 55.8 us
  local copies, waits for them, and re-layouts: 0 us -> 54.2 us
  other arithmetic: 25.1 us -> 3.71 us
    psum x1 -> x0, blocking collectives: 1120 us -> none  [per_device(): rotated_in = lax.psum(partial_in, 'feat').astype(jnp.bfloat16)]
    pallas_call x0 -> x64, Pallas kernels: none -> 221 us  [call(): pl.pallas_call(kernel, grid_spec=pltpu.PrefetchScalarGridSpec(num_scalar_...]
    ppermute x0 -> x83, starting transfers between devices: none -> 152 us  [the longest x28 78 us: pipelined(): lax.ppermute(v, 'feat', inward[0] + outward[0])]
    all_gather x3 -> x2, waiting for transfers between devices: 120 us -> 0.01 us  [the longest x1 0.01 us: pipelined(): grad_all = lax.all_gather(out_grads, 'feat', axis=0, tiled=True)]
    dot_general x3 -> x0, matrix products: 106 us -> none  [the longest x1 61.3 us: per_device(): jnp.dot(lax.all_gather(activations, 'ex', axis=0, tiled=True), basis_in,...]
    ppermute x0 -> x83, waiting for transfers between devices: none -> 55 us  [the longest x28 39 us: pipelined(): lax.ppermute(v, 'feat', inward[0] + outward[0])]
    unnamed x0 -> x252, local copies, waits for them, and re-layouts: none -> 49.7 us
    div x1 -> x0, other arithmetic: 23 us -> none  [per_device(): return total / jnp.float32(tokens_all)]
  transfers between devices with their start and end apart: 4 -> 86, of which waited for: 2 -> 15; matrix products, arithmetic and copies ran while one was open for 5% -> 2% of each run, Pallas kernels for 0% -> 42%
where the time goes in v1:
time: 512 us; the launch traced here: 502 us
  Pallas kernels  221 us (43%)
  starting transfers between devices  153 us (30%)
  waiting for transfers between devices  55.8 us (11%)
  local copies, waits for them, and re-layouts  54.2 us (11%)
  between operations  15.3 us (3%)
    pallas_call x64, Pallas kernels, call(): pl.pallas_call(kernel, grid_spec=pltpu.PrefetchScalarGridSpec(num_scalar_...  221 us
    ppermute x28, starting transfers between devices, pipelined(): lax.ppermute(v, 'feat', inward[0] + outward[0])  78 us
    unnamed x252, local copies, waits for them, and re-layouts  49.7 us
    ppermute x24, starting transfers between devices, pipelined(): lax.ppermute(v, 'feat', middle + stay)  39.1 us
    ppermute x28, waiting for transfers between devices, pipelined(): lax.ppermute(v, 'feat', inward[0] + outward[0])  39 us
    ppermute x28, starting transfers between devices, pipelined(): lax.ppermute(v, 'feat', y_swap)  32.3 us
    ppermute x28, waiting for transfers between devices, pipelined(): lax.ppermute(v, 'feat', y_swap)  15 us
  transfers between devices with their start and end apart: 86, of which 15 were waited for; matrix products, arithmetic and copies ran while one was open for 2% of the time, Pallas kernels for 42%

profile of v1, /device:TPU:0, one launch (start us, length us, event | category | flops | bytes accessed | tf_op | source)
XLA Modules:
  0.0 502.3 jit_solution(304316841214843539)
XLA Ops:
  13.6 4.3 shard_map.46
  18.8 3.0 collective-permute-start.2
  23.4 4.4 shard_map.48
  29.3 4.4 shard_map.50
  33.6 6.4 %collective-permute-done.2.refs_1_ = bf16[512,256]{1,0:T(8,128)(2,1)S(1)} collective-permute-done((bf16[512,256]{1,0:T(8,128)(2,1)S(1)}, bf16[512,256]{1,0:T(8,128)(2,1)S(1)}, u32[]{:S(2)}, u32[]{:S(2)}) %collective-permute-start.2) | collective-permute-done | bytes 262176 | tf_op jit(solution)/shard_map/ppermute | solution.py:406
  42.0 4.4 shard_map.52
  46.4 4.3 collective-permute-done.8.refs_1_
  57.6 4.5 collective-permute-start.14
  62.0 7.1 %shard_map.55 = (f32[512,1024]{1,0:T(8,128)S(1)}, f32[8,128]{1,0:T(8,128)S(1)}) custom-call(s32[3]{0:T(128)S(1)} %pad_add_fusion.flags, bf16[256,3584]{1,0:T(8,128)(2,1)S(1)} %copy-done.3, bf16[256,3584]{1,0:T(8,128)(2,1)S(1)} %collective-permute-done.refs_1_, bf16[3584,7168]{1,0:T(8,128)(2,1)} %refs_2_.31, f32[8,128]{1,0:T(8,128)S(1)} %get-tuple-element.301.refs_3_), custom_call_target="tpu_custom_call" | custom-call | flops 3758096384 | bytes 13107200 | tf_op jit(solution)/shard_map/pallas_call | solution.py:62
  69.7 13.0 %collective-permute-done.4.refs_1_ = bf16[768,256]{1,0:T(8,128)(2,1)S(1)} collective-permute-done((bf16[768,256]{1,0:T(8,128)(2,1)S(1)}, bf16[768,256]{1,0:T(8,128)(2,1)S(1)}, u32[]{:S(2)}, u32[]{:S(2)}) %collective-permute-start.4) | collective-permute-done | bytes 393248 | tf_op jit(solution)/shard_map/ppermute | solution.py:406
  85.2 5.1 %collective-permute-start.10 = (bf16[1280,256]{1,0:T(8,128)(2,1)S(1)}, bf16[1280,256]{1,0:T(8,128)(2,1)S(1)}, u32[]{:S(2)}, u32[]{:S(2)}) collective-permute-start(bf16[1280,256]{1,0:T(8,128)(2,1)S(1)} %get-tuple-element.307), channel_id=1, source_target_pairs={{0,8},{4,12},{24,16},{28,20},{8,0},{12,4},{16,24},{20,28},{1,9},{5... | collective-permute-start | bytes 1966088 | tf_op jit(solution)/shard_map/ppermute | solution.py:406
  91.9 7.1 %shard_map.57 = (f32[512,1024]{1,0:T(8,128)S(1)}, f32[8,128]{1,0:T(8,128)S(1)}) custom-call(s32[3]{0:T(128)S(1)} %pad_add_fusion.flags, bf16[256,3584]{1,0:T(8,128)(2,1)S(1)} %get-tuple-element.309.refs_0_.refs_2_, bf16[256,3584]{1,0:T(8,128)(2,1)S(1)} %collective-permute-done.12.refs_1_.refs_3_, bf16[3584,7168]{1,0:T(8,128)(2,1)} %refs_2_.31, ...), custom_call_target="tpu_custom_call" | custom-call | flops 3758096384 | bytes 13107200 | tf_op jit(solution)/shard_map/pallas_call | solution.py:62
  99.0 6.2 %collective-permute-done.14.refs_1_ = bf16[768,256]{1,0:T(8,128)(2,1)S(1)} collective-permute-done((bf16[768,256]{1,0:T(8,128)(2,1)S(1)}, bf16[768,256]{1,0:T(8,128)(2,1)S(1)}, u32[]{:S(2)}, u32[]{:S(2)}) %collective-permute-start.14) | collective-permute-done | bytes 393248 | tf_op jit(solution)/shard_map/ppermute | solution.py:406
  112.2 7.1 %shard_map.59 = (f32[512,1024]{1,0:T(8,128)S(1)}, f32[8,128]{1,0:T(8,128)S(1)}) custom-call(s32[3]{0:T(128)S(1)} %pad_add_fusion.flags, bf16[256,3584]{1,0:T(8,128)(2,1)S(1)} %get-tuple-element.309.refs_0_.refs_2_, bf16[256,3584]{1,0:T(8,128)(2,1)S(1)} %collective-permute-done.12.refs_1_.refs_3_, bf16[3584,7168]{1,0:T(8,128)(2,1)} %refs_2_.31, ...), custom_call_target="tpu_custom_call" | custom-call | flops 3758096384 | bytes 13107200 | tf_op jit(solution)/shard_map/pallas_call | solution.py:62
  131.6 6.4 %shard_map.61 = (f32[1024,1024]{1,0:T(8,128)S(1)}, f32[8,128]{1,0:T(8,128)S(1)}) custom-call(s32[3]{0:T(128)S(1)} %pad_add_fusion.flags, bf16[1024,2048]{1,0:T(8,128)(2,1)S(1)} %copy-done.121, bf16[2048,1024]{1,0:T(8,128)(2,1)S(1)} %copy-done.120, f32[8,128]{1,0:T(8,128)S(1)} %get-tuple-element.325.refs_2_, ...), custom_call_target="tpu_custom_call" | custom-call | flops 4294967296 | bytes 12582912 | tf_op jit(solution)/shard_map/pallas_call | solution.py:62
  140.8 3.2 collective-permute-start.21
  151.7 7.6 %shard_map.62 = (f32[512,1024]{1,0:T(8,128)S(1)}, f32[8,128]{1,0:T(8,128)S(1)}) custom-call(s32[3]{0:T(128)S(1)} %pad_add_fusion.flags, bf16[256,3584]{1,0:T(8,128)(2,1)S(1)} %copy-done.12, bf16[256,3584]{1,0:T(8,128)(2,1)S(1)} %copy-done.18, bf16[3584,7168]{1,0:T(8,128)(2,1)} %refs_2_.31, f32[8,128]{1,0:T(8,128)S(1)} %get-tuple-element.333.refs_3_), custom_call_target="tpu_custom_call" | custom-call | flops 3758096384 | bytes 13107200 | tf_op jit(solution)/shard_map/pallas_call | solution.py:62
  160.0 2.9 shard_map.63
  168.2 11.0 %shard_map.64 = (f32[1024,1024]{1,0:T(8,128)S(1)}, f32[8,128]{1,0:T(8,128)S(1)}) custom-call(s32[3]{0:T(128)S(1)} %pad_add_fusion.flags, bf16[256,3584]{1,0:T(8,128)(2,1)S(1)} %copy-done.4, bf16[256,3584]{1,0:T(8,128)(2,1)S(1)} %copy-done.7, bf16[256,3584]{1,0:T(8,128)(2,1)S(1)} %copy-done.13, bf16[256,3584]{1,0:T(8,128)(2,1)S(1)} %copy-done.19, ...), custom_call_target="tpu_custom_call" | custom-call | flops 7516192768 | bytes 18874368 | tf_op jit(solution)/shard_map/pallas_call | solution.py:62
  179.3 3.2 shard_map.65
  197.4 5.7 %collective-permute-done.25.refs_0_ = bf16[768,256]{1,0:T(8,128)(2,1)S(1)} collective-permute-done((bf16[768,256]{1,0:T(8,128)(2,1)}, bf16[768,256]{1,0:T(8,128)(2,1)S(1)}, u32[]{:S(2)}, u32[]{:S(2)}) %collective-permute-start.25) | collective-permute-done | bytes 393248 | tf_op jit(solution)/shard_map/ppermute | solution.py:405
  212.6 3.3 shard_map.66
  215.9 10.4 %collective-permute-start.32 = (bf16[1536,256]{1,0:T(8,128)(2,1)S(1)}, bf16[1536,256]{1,0:T(8,128)(2,1)S(1)}, u32[]{:S(2)}, u32[]{:S(2)}) collective-permute-start(bf16[1536,256]{1,0:T(8,128)(2,1)S(1)} %get-tuple-element.369.refs_3_), channel_id=1, source_target_pairs={{0,8},{4,12},{24,16},{28,20},{8,0},{12,4},{16,24},{20,28},{1,9},{5... | collective-permute-start | bytes 2359304 | tf_op jit(solution)/shard_map/ppermute | solution.py:406
  228.9 10.9 %shard_map.67 = (f32[1024,1024]{1,0:T(8,128)S(1)}, f32[8,128]{1,0:T(8,128)S(1)}) custom-call(s32[3]{0:T(128)S(1)} %pad_add_fusion.flags, bf16[256,3584]{1,0:T(8,128)(2,1)S(1)} %copy-done.4, bf16[256,3584]{1,0:T(8,128)(2,1)S(1)} %copy-done.8, bf16[256,3584]{1,0:T(8,128)(2,1)S(1)} %copy-done.14, bf16[256,3584]{1,0:T(8,128)(2,1)S(1)} %copy-done.20, ...), custom_call_target="tpu_custom_call" | custom-call | flops 7516192768 | bytes 18874368 | tf_op jit(solution)/shard_map/pallas_call | solution.py:62
  239.9 2.9 shard_map.68
  244.3 4.7 collective-permute-start.29
  256.9 4.4 shard_map.70
  261.3 5.3 %collective-permute-done.28.refs_0_.refs_2_ = bf16[1280,256]{1,0:T(8,128)(2,1)S(1)} collective-permute-done((bf16[1280,256]{1,0:T(8,128)(2,1)S(1)}, bf16[1280,256]{1,0:T(8,128)(2,1)S(1)}, u32[]{:S(2)}, u32[]{:S(2)}) %collective-permute-start.28) | collective-permute-done | bytes 655392 | tf_op jit(solution)/shard_map/ppermute | solution.py:405
  267.4 3.4 shard_map.71
  270.8 7.5 %collective-permute-start.36 = (bf16[1536,256]{1,0:T(8,128)(2,1)}, bf16[1536,256]{1,0:T(8,128)(2,1)}, u32[]{:S(2)}, u32[]{:S(2)}) collective-permute-start(bf16[1536,256]{1,0:T(8,128)(2,1)} %get-tuple-element.385.refs_4_), channel_id=1, source_target_pairs={{8,16},{12,20},{16,8},{20,12},{0,0},{4,4},{24,24},{28,28},{9,17},{... | collective-permute-start | bytes 2359304 | tf_op jit(solution)/shard_map/ppermute | solution.py:407
  281.3 4.4 shard_map.72
  285.8 3.3 shard_map.73
  293.9 7.4 %collective-permute-start.45 = (bf16[1536,256]{1,0:T(8,128)(2,1)}, bf16[1536,256]{1,0:T(8,128)(2,1)}, u32[]{:S(2)}, u32[]{:S(2)}) collective-permute-start(bf16[1536,256]{1,0:T(8,128)(2,1)} %get-tuple-element.409.refs_4_), channel_id=1, source_target_pairs={{8,16},{12,20},{16,8},{20,12},{0,0},{4,4},{24,24},{28,28},{9,17},{... | collective-permute-start | bytes 2359304 | tf_op jit(solution)/shard_map/ppermute | solution.py:407
  304.5 4.6 shard_map.74
  309.2 3.7 shard_map.75
  317.6 6.5 %collective-permute-start.42 = (bf16[1280,256]{1,0:T(8,128)(2,1)}, bf16[1280,256]{1,0:T(8,128)(2,1)}, u32[]{:S(2)}, u32[]{:S(2)}) collective-permute-start(bf16[1280,256]{1,0:T(8,128)(2,1)} %get-tuple-element.405.refs_4_), channel_id=1, source_target_pairs={{8,16},{12,20},{16,8},{20,12},{0,0},{4,4},{24,24},{28,28},{9,17},{... | collective-permute-start | bytes 1966088 | tf_op jit(solution)/shard_map/ppermute | solution.py:407
  333.8 4.4 shard_map.76
  338.3 3.1 shard_map.77
  342.3 4.0 collective-permute-start.50
  347.8 4.0 shard_map.78
  351.8 4.3 shard_map.79
  356.1 4.5 shard_map.80
  364.5 2.9 collective-permute-start.47
  368.0 3.1 shard_map.82
  371.1 3.1 shard_map.83
  374.3 4.4 shard_map.84
  385.4 4.0 shard_map.86
  389.5 4.0 shard_map.87
  393.5 4.4 shard_map.88
  400.9 3.0 collective-permute-start.53
  404.3 3.1 shard_map.90
  407.4 4.4 shard_map.91
  416.6 3.1 shard_map.93
  422.6 6.5 %collective-permute-start.59 = (bf16[768,256]{1,0:T(8,128)(2,1)S(1)}, bf16[768,256]{1,0:T(8,128)(2,1)S(1)}, u32[]{:S(2)}, u32[]{:S(2)}) collective-permute-start(bf16[768,256]{1,0:T(8,128)(2,1)S(1)} %get-tuple-element.487.refs_3_), channel_id=1, source_target_pairs={{0,8},{4,12},{24,16},{28,20},{8,0},{12,4},{16,24},{20,28},{1,9},{5... | collective-permute-start | bytes 1179656 | tf_op jit(solution)/shard_map/ppermute | solution.py:406
  429.5 3.1 shard_map.95
  437.6 3.1 shard_map.97
  442.7 6.0 %collective-permute-start.65 = (bf16[768,256]{1,0:T(8,128)(2,1)S(1)}, bf16[768,256]{1,0:T(8,128)(2,1)S(1)}, u32[]{:S(2)}, u32[]{:S(2)}) collective-permute-start(bf16[768,256]{1,0:T(8,128)(2,1)S(1)} %get-tuple-element.509.refs_3_), channel_id=1, source_target_pairs={{0,8},{4,12},{24,16},{28,20},{8,0},{12,4},{16,24},{20,28},{1,9},{5... | collective-permute-start | bytes 1179656 | tf_op jit(solution)/shard_map/ppermute | solution.py:406
  453.3 3.2 shard_map.100
  456.5 3.1 collective-permute-done.64.refs_0_.refs_2_
  462.4 4.6 collective-permute-done.74.refs_1_
  471.7 3.2 shard_map.103
  476.4 6.8 %collective-permute-start.81 = (bf16[512,256]{1,0:T(8,128)(2,1)S(1)}, bf16[512,256]{1,0:T(8,128)(2,1)S(1)}, u32[]{:S(2)}, u32[]{:S(2)}) collective-permute-start(bf16[512,256]{1,0:T(8,128)(2,1)S(1)} %get-tuple-element.546.refs_2_), channel_id=1, source_target_pairs={{0,8},{4,12},{24,16},{28,20},{8,0},{12,4},{16,24},{20,28},{1,9},{5... | collective-permute-start | bytes 786440 | tf_op jit(solution)/shard_map/ppermute | solution.py:406
  487.0 3.2 shard_map.106
  492.2 3.2 shard_map.109
  (433 shorter events, 172.9 us)
Async XLA Ops:
  6.5 120.7 %all-gather.3.cloned.1.call-start = ((), (), s32[]{:S(2)}) async-start(), calls=%async_computation.1 | async-start | bytes 4718592 | tf_op jit(solution)/shard_map/all_gather | solution.py:411
  7.3 183.8 %reduce-scatter.2.cloned.1.call-start = ((), (), s32[]{:S(2)}) async-start(), calls=%async_computation.2 | async-start | bytes 5242880 | tf_op jit(solution)/shard_map/reduce_scatter | solution.py:449
  7.8 44.1 %collective-permute-start.6 = (bf16[256,3584]{1,0:T(8,128)(2,1)}, bf16[256,3584]{1,0:T(8,128)(2,1)}, u32[]{:S(2)}, u32[]{:S(2)}) collective-permute-start(bf16[256,3584]{1,0:T(8,128)(2,1)} %refs_0_.21), channel_id=1, source_target_pairs={{0,2},{1,3},{2,0},{3,1},{4,6},{5,7},{6,4},{7,5},{8,10},{9,11},{10,... | collective-permute-start | bytes 5505032 | tf_op jit(solution)/shard_map/ppermute | solution.py:359
  18.8 21.2 %collective-permute-start.2 = (bf16[512,256]{1,0:T(8,128)(2,1)S(1)}, bf16[512,256]{1,0:T(8,128)(2,1)S(1)}, u32[]{:S(2)}, u32[]{:S(2)}) collective-permute-start(bf16[512,256]{1,0:T(8,128)(2,1)S(1)} %get-tuple-element.285), channel_id=1, source_target_pairs={{0,8},{4,12},{24,16},{28,20},{8,0},{12,4},{16,24},{20,28},{1,9},{5... | collective-permute-start | bytes 786440 | tf_op jit(solution)/shard_map/ppermute | solution.py:406
  28.6 22.0 %collective-permute-start.8 = (bf16[512,256]{1,0:T(8,128)(2,1)S(1)}, bf16[512,256]{1,0:T(8,128)(2,1)S(1)}, u32[]{:S(2)}, u32[]{:S(2)}) collective-permute-start(bf16[512,256]{1,0:T(8,128)(2,1)S(1)} %get-tuple-element.296), channel_id=1, source_target_pairs={{0,8},{4,12},{24,16},{28,20},{8,0},{12,4},{16,24},{20,28},{1,9},{5... | collective-permute-start | bytes 786440 | tf_op jit(solution)/shard_map/ppermute | solution.py:406
  29.1 17.2 %collective-permute-start.7 = (bf16[256,256]{1,0:T(8,128)(2,1)S(1)}, bf16[256,256]{1,0:T(8,128)(2,1)S(1)}, u32[]{:S(2)}, u32[]{:S(2)}) collective-permute-start(bf16[256,256]{1,0:T(8,128)(2,1)S(1)} %get-tuple-element.295), channel_id=1, source_target_pairs={{0,4},{4,0},{8,12},{12,8},{16,20},{20,16},{24,28},{28,24},{1,5},{5... | collective-permute-start | bytes 393224 | tf_op jit(solution)/shard_map/ppermute | solution.py:405
  54.0 36.3 %collective-permute-start.12 = (bf16[256,3584]{1,0:T(8,128)(2,1)S(1)}, bf16[256,3584]{1,0:T(8,128)(2,1)S(1)}, u32[]{:S(2)}, u32[]{:S(2)}) collective-permute-start(bf16[256,3584]{1,0:T(8,128)(2,1)S(1)} %get-tuple-element.309.refs_0_.refs_2_), channel_id=1, source_target_pairs={{0,1},{1,0},{2,3},{3,2},{4,5},{5,4},{6,7},{7,6},{8,9},{9,8},{10,11... | collective-permute-start | bytes 5505032 | tf_op jit(solution)/shard_map/ppermute | solution.py:359
  54.1 28.7 %collective-permute-start.4 = (bf16[768,256]{1,0:T(8,128)(2,1)S(1)}, bf16[768,256]{1,0:T(8,128)(2,1)S(1)}, u32[]{:S(2)}, u32[]{:S(2)}) collective-permute-start(bf16[768,256]{1,0:T(8,128)(2,1)S(1)} %get-tuple-element.293), channel_id=1, source_target_pairs={{0,8},{4,12},{24,16},{28,20},{8,0},{12,4},{16,24},{20,28},{1,9},{5... | collective-permute-start | bytes 1179656 | tf_op jit(solution)/shard_map/ppermute | solution.py:406
  56.9 28.3 %collective-permute-start.15 = (bf16[256,256]{1,0:T(8,128)(2,1)S(1)}, bf16[256,256]{1,0:T(8,128)(2,1)S(1)}, u32[]{:S(2)}, u32[]{:S(2)}) collective-permute-start(bf16[256,256]{1,0:T(8,128)(2,1)S(1)} %get-tuple-element.312), channel_id=1, source_target_pairs={{8,16},{12,20},{16,8},{20,12},{0,0},{4,4},{24,24},{28,28},{9,17},{... | collective-permute-start | bytes 393224 | tf_op jit(solution)/shard_map/ppermute | solution.py:407
  57.6 47.6 %collective-permute-start.14 = (bf16[768,256]{1,0:T(8,128)(2,1)S(1)}, bf16[768,256]{1,0:T(8,128)(2,1)S(1)}, u32[]{:S(2)}, u32[]{:S(2)}) collective-permute-start(bf16[768,256]{1,0:T(8,128)(2,1)S(1)} %get-tuple-element.311), channel_id=1, source_target_pairs={{0,8},{4,12},{24,16},{28,20},{8,0},{12,4},{16,24},{20,28},{1,9},{5... | collective-permute-start | bytes 1179656 | tf_op jit(solution)/shard_map/ppermute | solution.py:406
  69.2 29.9 %collective-permute-start.13 = (bf16[256,256]{1,0:T(8,128)(2,1)S(1)}, bf16[256,256]{1,0:T(8,128)(2,1)S(1)}, u32[]{:S(2)}, u32[]{:S(2)}) collective-permute-start(bf16[256,256]{1,0:T(8,128)(2,1)S(1)} %get-tuple-element.310), channel_id=1, source_target_pairs={{0,4},{4,0},{8,12},{12,8},{16,20},{20,16},{24,28},{28,24},{1,5},{5... | collective-permute-start | bytes 393224 | tf_op jit(solution)/shard_map/ppermute | solution.py:405
  84.5 27.6 %collective-permute-start.11 = (bf16[512,256]{1,0:T(8,128)(2,1)S(1)}, bf16[512,256]{1,0:T(8,128)(2,1)S(1)}, u32[]{:S(2)}, u32[]{:S(2)}) collective-permute-start(bf16[512,256]{1,0:T(8,128)(2,1)S(1)} %get-tuple-element.308), channel_id=1, source_target_pairs={{8,16},{12,20},{16,8},{20,12},{0,0},{4,4},{24,24},{28,28},{9,17},{... | collective-permute-start | bytes 786440 | tf_op jit(solution)/shard_map/ppermute | solution.py:407
  85.2 36.6 %collective-permute-start.10 = (bf16[1280,256]{1,0:T(8,128)(2,1)S(1)}, bf16[1280,256]{1,0:T(8,128)(2,1)S(1)}, u32[]{:S(2)}, u32[]{:S(2)}) collective-permute-start(bf16[1280,256]{1,0:T(8,128)(2,1)S(1)} %get-tuple-element.307), channel_id=1, source_target_pairs={{0,8},{4,12},{24,16},{28,20},{8,0},{12,4},{16,24},{20,28},{1,9},{5... | collective-permute-start | bytes 1966088 | tf_op jit(solution)/shard_map/ppermute | solution.py:406
  90.3 29.0 %collective-permute-start.9 = (bf16[768,256]{1,0:T(8,128)(2,1)S(1)}, bf16[768,256]{1,0:T(8,128)(2,1)S(1)}, u32[]{:S(2)}, u32[]{:S(2)}) collective-permute-start(bf16[768,256]{1,0:T(8,128)(2,1)S(1)} %get-tuple-element.306), channel_id=1, source_target_pairs={{0,4},{4,0},{8,12},{12,8},{16,20},{20,16},{24,28},{28,24},{1,5},{5... | collective-permute-start | bytes 1179656 | tf_op jit(solution)/shard_map/ppermute | solution.py:405
  111.5 15.7 %collective-permute-start.16 = (bf16[512,256]{1,0:T(8,128)(2,1)S(1)}, bf16[512,256]{1,0:T(8,128)(2,1)S(1)}, u32[]{:S(2)}, u32[]{:S(2)}) collective-permute-start(bf16[512,256]{1,0:T(8,128)(2,1)S(1)} %get-tuple-element.326), channel_id=1, source_target_pairs={{8,16},{12,20},{16,8},{20,12},{0,0},{4,4},{24,24},{28,28},{9,17},{... | collective-permute-start | bytes 786440 | tf_op jit(solution)/shard_map/ppermute | solution.py:407
  140.8 183.4 %all-gather.5.cloned.1.call-start = ((), (), s32[]{:S(2)}) async-start(), calls=%async_computation.3 | async-start | bytes 2621440 | tf_op jit(solution)/shard_map/all_gather | solution.py:450
  140.8 19.1 %collective-permute-start.21 = (bf16[1280,256]{1,0:T(8,128)(2,1)}, bf16[1280,256]{1,0:T(8,128)(2,1)S(1)}, u32[]{:S(2)}, u32[]{:S(2)}) collective-permute-start(bf16[1280,256]{1,0:T(8,128)(2,1)} %copy-done.122), channel_id=1, source_target_pairs={{0,8},{4,12},{24,16},{28,20},{8,0},{12,4},{16,24},{20,28},{1,9},{5... | collective-permute-start | bytes 1966088 | tf_op jit(solution)/shard_map/ppermute | solution.py:406
  144.1 24.1 %collective-permute-start.19 = (bf16[1024,256]{1,0:T(8,128)(2,1)S(1)}, bf16[1024,256]{1,0:T(8,128)(2,1)S(1)}, u32[]{:S(2)}, u32[]{:S(2)}) collective-permute-start(bf16[1024,256]{1,0:T(8,128)(2,1)S(1)} %get-tuple-element.330.refs_4_), channel_id=1, source_target_pairs={{8,16},{12,20},{16,8},{20,12},{0,0},{4,4},{24,24},{28,28},{9,17},{... | collective-permute-start | bytes 1572872 | tf_op jit(solution)/shard_map/ppermute | solution.py:407
  145.2 14.1 %collective-permute-start.20 = (bf16[768,256]{1,0:T(8,128)(2,1)}, bf16[768,256]{1,0:T(8,128)(2,1)S(1)}, u32[]{:S(2)}, u32[]{:S(2)}) collective-permute-start(bf16[768,256]{1,0:T(8,128)(2,1)} %copy-done.124), channel_id=1, source_target_pairs={{0,4},{4,0},{8,12},{12,8},{16,20},{20,16},{24,28},{28,24},{1,5},{5... | collective-permute-start | bytes 1179656 | tf_op jit(solution)/shard_map/ppermute | solution.py:405
  146.9 32.3 %collective-permute-start.18 = (bf16[1536,256]{1,0:T(8,128)(2,1)S(1)}, bf16[1536,256]{1,0:T(8,128)(2,1)S(1)}, u32[]{:S(2)}, u32[]{:S(2)}) collective-permute-start(bf16[1536,256]{1,0:T(8,128)(2,1)S(1)} %get-tuple-element.329.refs_3_), channel_id=1, source_target_pairs={{0,8},{4,12},{24,16},{28,20},{8,0},{12,4},{16,24},{20,28},{1,9},{5... | collective-permute-start | bytes 2359304 | tf_op jit(solution)/shard_map/ppermute | solution.py:406
  149.2 30.0 %collective-permute-start.17 = (bf16[768,256]{1,0:T(8,128)(2,1)}, bf16[768,256]{1,0:T(8,128)(2,1)S(1)}, u32[]{:S(2)}, u32[]{:S(2)}) collective-permute-start(bf16[768,256]{1,0:T(8,128)(2,1)} %copy-done.123), channel_id=1, source_target_pairs={{0,4},{4,0},{8,12},{12,8},{16,20},{20,16},{24,28},{28,24},{1,5},{5... | collective-permute-start | bytes 1179656 | tf_op jit(solution)/shard_map/ppermute | solution.py:405
  166.0 38.7 %collective-permute-start.26 = (bf16[1536,256]{1,0:T(8,128)(2,1)}, bf16[1536,256]{1,0:T(8,128)(2,1)}, u32[]{:S(2)}, u32[]{:S(2)}) collective-permute-start(bf16[1536,256]{1,0:T(8,128)(2,1)} %get-tuple-element.351.refs_3_), channel_id=1, source_target_pairs={{0,8},{4,12},{24,16},{28,20},{8,0},{12,4},{16,24},{20,28},{1,9},{5... | collective-permute-start | bytes 2359304 | tf_op jit(solution)/shard_map/ppermute | solution.py:406
  187.6 40.5 %collective-permute-start.24 = (bf16[1280,256]{1,0:T(8,128)(2,1)}, bf16[1280,256]{1,0:T(8,128)(2,1)S(1)}, u32[]{:S(2)}, u32[]{:S(2)}) collective-permute-start(bf16[1280,256]{1,0:T(8,128)(2,1)} %get-tuple-element.349.refs_4_), channel_id=1, source_target_pairs={{8,16},{12,20},{16,8},{20,12},{0,0},{4,4},{24,24},{28,28},{9,17},{... | collective-permute-start | bytes 1966088 | tf_op jit(solution)/shard_map/ppermute | solution.py:407
  189.3 15.4 %collective-permute-start.27 = (bf16[1024,256]{1,0:T(8,128)(2,1)}, bf16[1024,256]{1,0:T(8,128)(2,1)S(1)}, u32[]{:S(2)}, u32[]{:S(2)}) collective-permute-start(bf16[1024,256]{1,0:T(8,128)(2,1)} %get-tuple-element.352.refs_4_), channel_id=1, source_target_pairs={{8,16},{12,20},{16,8},{20,12},{0,0},{4,4},{24,24},{28,28},{9,17},{... | collective-permute-start | bytes 1572872 | tf_op jit(solution)/shard_map/ppermute | solution.py:407
  194.8 45.0 %collective-permute-start.23 = (bf16[1536,256]{1,0:T(8,128)(2,1)}, bf16[1536,256]{1,0:T(8,128)(2,1)S(1)}, u32[]{:S(2)}, u32[]{:S(2)}) collective-permute-start(bf16[1536,256]{1,0:T(8,128)(2,1)} %copy-done.48), channel_id=1, source_target_pairs={{0,8},{4,12},{24,16},{28,20},{8,0},{12,4},{16,24},{20,28},{1,9},{5... | collective-permute-start | bytes 2359304 | tf_op jit(solution)/shard_map/ppermute | solution.py:406
  203.2 36.6 %collective-permute-start.22 = (bf16[1280,256]{1,0:T(8,128)(2,1)}, bf16[1280,256]{1,0:T(8,128)(2,1)S(1)}, u32[]{:S(2)}, u32[]{:S(2)}) collective-permute-start(bf16[1280,256]{1,0:T(8,128)(2,1)} %copy-done.50), channel_id=1, source_target_pairs={{0,4},{4,0},{8,12},{12,8},{16,20},{20,16},{24,28},{28,24},{1,5},{5... | collective-permute-start | bytes 1966088 | tf_op jit(solution)/shard_map/ppermute | solution.py:405
  215.9 33.3 %collective-permute-start.32 = (bf16[1536,256]{1,0:T(8,128)(2,1)S(1)}, bf16[1536,256]{1,0:T(8,128)(2,1)S(1)}, u32[]{:S(2)}, u32[]{:S(2)}) collective-permute-start(bf16[1536,256]{1,0:T(8,128)(2,1)S(1)} %get-tuple-element.369.refs_3_), channel_id=1, source_target_pairs={{0,8},{4,12},{24,16},{28,20},{8,0},{12,4},{16,24},{20,28},{1,9},{5... | collective-permute-start | bytes 2359304 | tf_op jit(solution)/shard_map/ppermute | solution.py:406
  226.4 22.6 %collective-permute-start.31 = (bf16[1280,256]{1,0:T(8,128)(2,1)S(1)}, bf16[1280,256]{1,0:T(8,128)(2,1)S(1)}, u32[]{:S(2)}, u32[]{:S(2)}) collective-permute-start(bf16[1280,256]{1,0:T(8,128)(2,1)S(1)} %get-tuple-element.368.refs_1_), channel_id=1, source_target_pairs={{0,4},{4,0},{8,12},{12,8},{16,20},{20,16},{24,28},{28,24},{1,5},{5... | collective-permute-start | bytes 1966088 | tf_op jit(solution)/shard_map/ppermute | solution.py:405
  228.1 21.2 %collective-permute-start.33 = (bf16[1280,256]{1,0:T(8,128)(2,1)S(1)}, bf16[1280,256]{1,0:T(8,128)(2,1)S(1)}, u32[]{:S(2)}, u32[]{:S(2)}) collective-permute-start(bf16[1280,256]{1,0:T(8,128)(2,1)S(1)} %get-tuple-element.370.refs_4_), channel_id=1, source_target_pairs={{8,16},{12,20},{16,8},{20,12},{0,0},{4,4},{24,24},{28,28},{9,17},{... | collective-permute-start | bytes 1966088 | tf_op jit(solution)/shard_map/ppermute | solution.py:407
  244.3 23.1 %collective-permute-start.29 = (bf16[1536,256]{1,0:T(8,128)(2,1)S(1)}, bf16[1536,256]{1,0:T(8,128)(2,1)S(1)}, u32[]{:S(2)}, u32[]{:S(2)}) collective-permute-start(bf16[1536,256]{1,0:T(8,128)(2,1)S(1)} %get-tuple-element.366.refs_3_), channel_id=1, source_target_pairs={{0,8},{4,12},{24,16},{28,20},{8,0},{12,4},{16,24},{20,28},{1,9},{5... | collective-permute-start | bytes 2359304 | tf_op jit(solution)/shard_map/ppermute | solution.py:406
  248.9 17.7 %collective-permute-start.28 = (bf16[1280,256]{1,0:T(8,128)(2,1)S(1)}, bf16[1280,256]{1,0:T(8,128)(2,1)S(1)}, u32[]{:S(2)}, u32[]{:S(2)}) collective-permute-start(bf16[1280,256]{1,0:T(8,128)(2,1)S(1)} %get-tuple-element.365.refs_1_), channel_id=1, source_target_pairs={{0,4},{4,0},{8,12},{12,8},{16,20},{20,16},{24,28},{28,24},{1,5},{5... | collective-permute-start | bytes 1966088 | tf_op jit(solution)/shard_map/ppermute | solution.py:405
  252.2 27.4 %collective-permute-start.39 = (bf16[1536,256]{1,0:T(8,128)(2,1)S(1)}, bf16[1536,256]{1,0:T(8,128)(2,1)S(1)}, u32[]{:S(2)}, u32[]{:S(2)}) collective-permute-start(bf16[1536,256]{1,0:T(8,128)(2,1)S(1)} %get-tuple-element.388.refs_4_), channel_id=1, source_target_pairs={{8,16},{12,20},{16,8},{20,12},{0,0},{4,4},{24,24},{28,28},{9,17},{... | collective-permute-start | bytes 2359304 | tf_op jit(solution)/shard_map/ppermute | solution.py:407
  253.1 32.7 %collective-permute-start.38 = (bf16[1536,256]{1,0:T(8,128)(2,1)S(1)}, bf16[1536,256]{1,0:T(8,128)(2,1)S(1)}, u32[]{:S(2)}, u32[]{:S(2)}) collective-permute-start(bf16[1536,256]{1,0:T(8,128)(2,1)S(1)} %get-tuple-element.387.refs_3_), channel_id=1, source_target_pairs={{0,8},{4,12},{24,16},{28,20},{8,0},{12,4},{16,24},{20,28},{1,9},{5... | collective-permute-start | bytes 2359304 | tf_op jit(solution)/shard_map/ppermute | solution.py:406
  255.4 30.4 %collective-permute-start.37 = (bf16[1280,256]{1,0:T(8,128)(2,1)S(1)}, bf16[1280,256]{1,0:T(8,128)(2,1)S(1)}, u32[]{:S(2)}, u32[]{:S(2)}) collective-permute-start(bf16[1280,256]{1,0:T(8,128)(2,1)S(1)} %get-tuple-element.386.refs_1_), channel_id=1, source_target_pairs={{0,4},{4,0},{8,12},{12,8},{16,20},{20,16},{24,28},{28,24},{1,5},{5... | collective-permute-start | bytes 1966088 | tf_op jit(solution)/shard_map/ppermute | solution.py:405
  270.8 30.5 %collective-permute-start.36 = (bf16[1536,256]{1,0:T(8,128)(2,1)}, bf16[1536,256]{1,0:T(8,128)(2,1)}, u32[]{:S(2)}, u32[]{:S(2)}) collective-permute-start(bf16[1536,256]{1,0:T(8,128)(2,1)} %get-tuple-element.385.refs_4_), channel_id=1, source_target_pairs={{8,16},{12,20},{16,8},{20,12},{0,0},{4,4},{24,24},{28,28},{9,17},{... | collective-permute-start | bytes 2359304 | tf_op jit(solution)/shard_map/ppermute | solution.py:407
  278.3 30.8 %collective-permute-start.35 = (bf16[1536,256]{1,0:T(8,128)(2,1)}, bf16[1536,256]{1,0:T(8,128)(2,1)}, u32[]{:S(2)}, u32[]{:S(2)}) collective-permute-start(bf16[1536,256]{1,0:T(8,128)(2,1)} %get-tuple-element.384.refs_3_), channel_id=1, source_target_pairs={{0,8},{4,12},{24,16},{28,20},{8,0},{12,4},{16,24},{20,28},{1,9},{5... | collective-permute-start | bytes 2359304 | tf_op jit(solution)/shard_map/ppermute | solution.py:406
  279.6 29.5 %collective-permute-start.34 = (bf16[1280,256]{1,0:T(8,128)(2,1)}, bf16[1280,256]{1,0:T(8,128)(2,1)}, u32[]{:S(2)}, u32[]{:S(2)}) collective-permute-start(bf16[1280,256]{1,0:T(8,128)(2,1)} %get-tuple-element.383.refs_1_), channel_id=1, source_target_pairs={{0,4},{4,0},{8,12},{12,8},{16,20},{20,16},{24,28},{28,24},{1,5},{5... | collective-permute-start | bytes 1966088 | tf_op jit(solution)/shard_map/ppermute | solution.py:405
  293.9 36.3 %collective-permute-start.45 = (bf16[1536,256]{1,0:T(8,128)(2,1)}, bf16[1536,256]{1,0:T(8,128)(2,1)}, u32[]{:S(2)}, u32[]{:S(2)}) collective-permute-start(bf16[1536,256]{1,0:T(8,128)(2,1)} %get-tuple-element.409.refs_4_), channel_id=1, source_target_pairs={{8,16},{12,20},{16,8},{20,12},{0,0},{4,4},{24,24},{28,28},{9,17},{... | collective-permute-start | bytes 2359304 | tf_op jit(solution)/shard_map/ppermute | solution.py:407
  301.3 36.9 %collective-permute-start.44 = (bf16[1536,256]{1,0:T(8,128)(2,1)}, bf16[1536,256]{1,0:T(8,128)(2,1)}, u32[]{:S(2)}, u32[]{:S(2)}) collective-permute-start(bf16[1536,256]{1,0:T(8,128)(2,1)} %get-tuple-element.408.refs_3_), channel_id=1, source_target_pairs={{0,8},{4,12},{24,16},{28,20},{8,0},{12,4},{16,24},{20,28},{1,9},{5... | collective-permute-start | bytes 2359304 | tf_op jit(solution)/shard_map/ppermute | solution.py:406
  301.3 36.9 %collective-permute-start.43 = (bf16[1280,256]{1,0:T(8,128)(2,1)}, bf16[1280,256]{1,0:T(8,128)(2,1)}, u32[]{:S(2)}, u32[]{:S(2)}) collective-permute-start(bf16[1280,256]{1,0:T(8,128)(2,1)} %copy-done.40), channel_id=1, source_target_pairs={{0,4},{4,0},{8,12},{12,8},{16,20},{20,16},{24,28},{28,24},{1,5},{5... | collective-permute-start | bytes 1966088 | tf_op jit(solution)/shard_map/ppermute | solution.py:405
  317.6 28.6 %collective-permute-start.42 = (bf16[1280,256]{1,0:T(8,128)(2,1)}, bf16[1280,256]{1,0:T(8,128)(2,1)}, u32[]{:S(2)}, u32[]{:S(2)}) collective-permute-start(bf16[1280,256]{1,0:T(8,128)(2,1)} %get-tuple-element.405.refs_4_), channel_id=1, source_target_pairs={{8,16},{12,20},{16,8},{20,12},{0,0},{4,4},{24,24},{28,28},{9,17},{... | collective-permute-start | bytes 1966088 | tf_op jit(solution)/shard_map/ppermute | solution.py:407
  324.2 36.5 %collective-permute-start.41 = (bf16[1536,256]{1,0:T(8,128)(2,1)}, bf16[1536,256]{1,0:T(8,128)(2,1)}, u32[]{:S(2)}, u32[]{:S(2)}) collective-permute-start(bf16[1536,256]{1,0:T(8,128)(2,1)} %get-tuple-element.404.refs_3_), channel_id=1, source_target_pairs={{0,8},{4,12},{24,16},{28,20},{8,0},{12,4},{16,24},{20,28},{1,9},{5... | collective-permute-start | bytes 2359304 | tf_op jit(solution)/shard_map/ppermute | solution.py:406
  330.2 30.5 %collective-permute-start.40 = (bf16[1280,256]{1,0:T(8,128)(2,1)}, bf16[1280,256]{1,0:T(8,128)(2,1)S(1)}, u32[]{:S(2)}, u32[]{:S(2)}) collective-permute-start(bf16[1280,256]{1,0:T(8,128)(2,1)} %copy-done.44), channel_id=1, source_target_pairs={{0,4},{4,0},{8,12},{12,8},{16,20},{20,16},{24,28},{28,24},{1,5},{5... | collective-permute-start | bytes 1966088 | tf_op jit(solution)/shard_map/ppermute | solution.py:405
  341.4 26.0 %collective-permute-start.51 = (bf16[1280,256]{1,0:T(8,128)(2,1)S(1)}, bf16[1280,256]{1,0:T(8,128)(2,1)S(1)}, u32[]{:S(2)}, u32[]{:S(2)}) collective-permute-start(bf16[1280,256]{1,0:T(8,128)(2,1)S(1)} %get-tuple-element.435.refs_4_), channel_id=1, source_target_pairs={{8,16},{12,20},{16,8},{20,12},{0,0},{4,4},{24,24},{28,28},{9,17},{... | collective-permute-start | bytes 1966088 | tf_op jit(solution)/shard_map/ppermute | solution.py:407
  342.3 36.4 %collective-permute-start.50 = (bf16[1536,256]{1,0:T(8,128)(2,1)S(1)}, bf16[1536,256]{1,0:T(8,128)(2,1)S(1)}, u32[]{:S(2)}, u32[]{:S(2)}) collective-permute-start(bf16[1536,256]{1,0:T(8,128)(2,1)S(1)} %get-tuple-element.434.refs_3_), channel_id=1, source_target_pairs={{0,8},{4,12},{24,16},{28,20},{8,0},{12,4},{16,24},{20,28},{1,9},{5... | collective-permute-start | bytes 2359304 | tf_op jit(solution)/shard_map/ppermute | solution.py:406
  346.3 32.4 %collective-permute-start.49 = (bf16[1280,256]{1,0:T(8,128)(2,1)S(1)}, bf16[1280,256]{1,0:T(8,128)(2,1)S(1)}, u32[]{:S(2)}, u32[]{:S(2)}) collective-permute-start(bf16[1280,256]{1,0:T(8,128)(2,1)S(1)} %get-tuple-element.432.refs_3_), channel_id=1, source_target_pairs={{0,4},{4,0},{8,12},{12,8},{16,20},{20,16},{24,28},{28,24},{1,5},{5... | collective-permute-start | bytes 1966088 | tf_op jit(solution)/shard_map/ppermute | solution.py:405
  363.6 20.3 %collective-permute-start.48 = (bf16[1024,256]{1,0:T(8,128)(2,1)S(1)}, bf16[1024,256]{1,0:T(8,128)(2,1)S(1)}, u32[]{:S(2)}, u32[]{:S(2)}) collective-permute-start(bf16[1024,256]{1,0:T(8,128)(2,1)S(1)} %get-tuple-element.431.refs_4_), channel_id=1, source_target_pairs={{8,16},{12,20},{16,8},{20,12},{0,0},{4,4},{24,24},{28,28},{9,17},{... | collective-permute-start | bytes 1572872 | tf_op jit(solution)/shard_map/ppermute | solution.py:407
  364.5 33.4 %collective-permute-start.47 = (bf16[1536,256]{1,0:T(8,128)(2,1)S(1)}, bf16[1536,256]{1,0:T(8,128)(2,1)S(1)}, u32[]{:S(2)}, u32[]{:S(2)}) collective-permute-start(bf16[1536,256]{1,0:T(8,128)(2,1)S(1)} %get-tuple-element.430.refs_3_), channel_id=1, source_target_pairs={{0,8},{4,12},{24,16},{28,20},{8,0},{12,4},{16,24},{20,28},{1,9},{5... | collective-permute-start | bytes 2359304 | tf_op jit(solution)/shard_map/ppermute | solution.py:406
  367.5 30.4 %collective-permute-start.46 = (bf16[1024,256]{1,0:T(8,128)(2,1)S(1)}, bf16[1024,256]{1,0:T(8,128)(2,1)S(1)}, u32[]{:S(2)}, u32[]{:S(2)}) collective-permute-start(bf16[1024,256]{1,0:T(8,128)(2,1)S(1)} %get-tuple-element.429.refs_1_.refs_3_), channel_id=1, source_target_pairs={{0,4},{4,0},{8,12},{12,8},{16,20},{20,16},{24,28},{28,24},{1,5},{5... | collective-permute-start | bytes 1572872 | tf_op jit(solution)/shard_map/ppermute | solution.py:405
  381.1 22.7 %collective-permute-start.57 = (bf16[1024,256]{1,0:T(8,128)(2,1)S(1)}, bf16[1024,256]{1,0:T(8,128)(2,1)S(1)}, u32[]{:S(2)}, u32[]{:S(2)}) collective-permute-start(bf16[1024,256]{1,0:T(8,128)(2,1)S(1)} %get-tuple-element.471.refs_4_), channel_id=1, source_target_pairs={{8,16},{12,20},{16,8},{20,12},{0,0},{4,4},{24,24},{28,28},{9,17},{... | collective-permute-start | bytes 1572872 | tf_op jit(solution)/shard_map/ppermute | solution.py:407
  381.8 30.0 %collective-permute-start.56 = (bf16[1536,256]{1,0:T(8,128)(2,1)S(1)}, bf16[1536,256]{1,0:T(8,128)(2,1)S(1)}, u32[]{:S(2)}, u32[]{:S(2)}) collective-permute-start(bf16[1536,256]{1,0:T(8,128)(2,1)S(1)} %get-tuple-element.470.refs_3_), channel_id=1, source_target_pairs={{0,8},{4,12},{24,16},{28,20},{8,0},{12,4},{16,24},{20,28},{1,9},{5... | collective-permute-start | bytes 2359304 | tf_op jit(solution)/shard_map/ppermute | solution.py:406
  383.9 27.9 %collective-permute-start.55 = (bf16[1024,256]{1,0:T(8,128)(2,1)S(1)}, bf16[1024,256]{1,0:T(8,128)(2,1)S(1)}, u32[]{:S(2)}, u32[]{:S(2)}) collective-permute-start(bf16[1024,256]{1,0:T(8,128)(2,1)S(1)} %get-tuple-element.469.refs_1_.refs_3_), channel_id=1, source_target_pairs={{0,4},{4,0},{8,12},{12,8},{16,20},{20,16},{24,28},{28,24},{1,5},{5... | collective-permute-start | bytes 1572872 | tf_op jit(solution)/shard_map/ppermute | solution.py:405
  400.2 15.7 %collective-permute-start.54 = (bf16[768,256]{1,0:T(8,128)(2,1)S(1)}, bf16[768,256]{1,0:T(8,128)(2,1)S(1)}, u32[]{:S(2)}, u32[]{:S(2)}) collective-permute-start(bf16[768,256]{1,0:T(8,128)(2,1)S(1)} %get-tuple-element.464.refs_4_), channel_id=1, source_target_pairs={{8,16},{12,20},{16,8},{20,12},{0,0},{4,4},{24,24},{28,28},{9,17},{... | collective-permute-start | bytes 1179656 | tf_op jit(solution)/shard_map/ppermute | solution.py:407
  400.9 18.9 %collective-permute-start.53 = (bf16[1280,256]{1,0:T(8,128)(2,1)S(1)}, bf16[1280,256]{1,0:T(8,128)(2,1)S(1)}, u32[]{:S(2)}, u32[]{:S(2)}) collective-permute-start(bf16[1280,256]{1,0:T(8,128)(2,1)S(1)} %get-tuple-element.463.refs_3_), channel_id=1, source_target_pairs={{0,8},{4,12},{24,16},{28,20},{8,0},{12,4},{16,24},{20,28},{1,9},{5... | collective-permute-start | bytes 1966088 | tf_op jit(solution)/shard_map/ppermute | solution.py:406
  403.8 15.9 %collective-permute-start.52 = (bf16[1024,256]{1,0:T(8,128)(2,1)S(1)}, bf16[1024,256]{1,0:T(8,128)(2,1)S(1)}, u32[]{:S(2)}, u32[]{:S(2)}) collective-permute-start(bf16[1024,256]{1,0:T(8,128)(2,1)S(1)} %get-tuple-element.462.refs_1_.refs_3_), channel_id=1, source_target_pairs={{0,4},{4,0},{8,12},{12,8},{16,20},{20,16},{24,28},{28,24},{1,5},{5... | collective-permute-start | bytes 1572872 | tf_op jit(solution)/shard_map/ppermute | solution.py:405
  414.1 18.6 %collective-permute-start.62 = (bf16[1280,256]{1,0:T(8,128)(2,1)S(1)}, bf16[1280,256]{1,0:T(8,128)(2,1)S(1)}, u32[]{:S(2)}, u32[]{:S(2)}) collective-permute-start(bf16[1280,256]{1,0:T(8,128)(2,1)S(1)} %get-tuple-element.494.refs_3_), channel_id=1, source_target_pairs={{0,8},{4,12},{24,16},{28,20},{8,0},{12,4},{16,24},{20,28},{1,9},{5... | collective-permute-start | bytes 1966088 | tf_op jit(solution)/shard_map/ppermute | solution.py:406
  414.4 18.3 %collective-permute-start.61 = (bf16[1024,256]{1,0:T(8,128)(2,1)S(1)}, bf16[1024,256]{1,0:T(8,128)(2,1)S(1)}, u32[]{:S(2)}, u32[]{:S(2)}) collective-permute-start(bf16[1024,256]{1,0:T(8,128)(2,1)S(1)} %get-tuple-element.493.refs_1_.refs_3_), channel_id=1, source_target_pairs={{0,4},{4,0},{8,12},{12,8},{16,20},{20,16},{24,28},{28,24},{1,5},{5... | collective-permute-start | bytes 1572872 | tf_op jit(solution)/shard_map/ppermute | solution.py:405
  422.6 18.1 %collective-permute-start.59 = (bf16[768,256]{1,0:T(8,128)(2,1)S(1)}, bf16[768,256]{1,0:T(8,128)(2,1)S(1)}, u32[]{:S(2)}, u32[]{:S(2)}) collective-permute-start(bf16[768,256]{1,0:T(8,128)(2,1)S(1)} %get-tuple-element.487.refs_3_), channel_id=1, source_target_pairs={{0,8},{4,12},{24,16},{28,20},{8,0},{12,4},{16,24},{20,28},{1,9},{5... | collective-permute-start | bytes 1179656 | tf_op jit(solution)/shard_map/ppermute | solution.py:406
  434.5 14.3 %collective-permute-start.68 = (bf16[768,256]{1,0:T(8,128)(2,1)S(1)}, bf16[768,256]{1,0:T(8,128)(2,1)S(1)}, u32[]{:S(2)}, u32[]{:S(2)}) collective-permute-start(bf16[768,256]{1,0:T(8,128)(2,1)S(1)} %get-tuple-element.515.refs_3_), channel_id=1, source_target_pairs={{0,8},{4,12},{24,16},{28,20},{8,0},{12,4},{16,24},{20,28},{1,9},{5... | collective-permute-start | bytes 1179656 | tf_op jit(solution)/shard_map/ppermute | solution.py:406
  434.8 14.0 %collective-permute-start.69 = (bf16[768,256]{1,0:T(8,128)(2,1)S(1)}, bf16[768,256]{1,0:T(8,128)(2,1)S(1)}, u32[]{:S(2)}, u32[]{:S(2)}) collective-permute-start(bf16[768,256]{1,0:T(8,128)(2,1)S(1)} %get-tuple-element.516.refs_4_), channel_id=1, source_target_pairs={{8,16},{12,20},{16,8},{20,12},{0,0},{4,4},{24,24},{28,28},{9,17},{... | collective-permute-start | bytes 1179656 | tf_op jit(solution)/shard_map/ppermute | solution.py:407
  442.7 16.9 %collective-permute-start.65 = (bf16[768,256]{1,0:T(8,128)(2,1)S(1)}, bf16[768,256]{1,0:T(8,128)(2,1)S(1)}, u32[]{:S(2)}, u32[]{:S(2)}) collective-permute-start(bf16[768,256]{1,0:T(8,128)(2,1)S(1)} %get-tuple-element.509.refs_3_), channel_id=1, source_target_pairs={{0,8},{4,12},{24,16},{28,20},{8,0},{12,4},{16,24},{20,28},{1,9},{5... | collective-permute-start | bytes 1179656 | tf_op jit(solution)/shard_map/ppermute | solution.py:406
  450.2 16.8 %collective-permute-start.74 = (bf16[768,256]{1,0:T(8,128)(2,1)S(1)}, bf16[768,256]{1,0:T(8,128)(2,1)S(1)}, u32[]{:S(2)}, u32[]{:S(2)}) collective-permute-start(bf16[768,256]{1,0:T(8,128)(2,1)S(1)} %get-tuple-element.531.refs_3_), channel_id=1, source_target_pairs={{0,8},{4,12},{24,16},{28,20},{8,0},{12,4},{16,24},{20,28},{1,9},{5... | collective-permute-start | bytes 1179656 | tf_op jit(solution)/shard_map/ppermute | solution.py:406
  460.8 14.6 %collective-permute-start.71 = (bf16[768,256]{1,0:T(8,128)(2,1)S(1)}, bf16[768,256]{1,0:T(8,128)(2,1)S(1)}, u32[]{:S(2)}, u32[]{:S(2)}) collective-permute-start(bf16[768,256]{1,0:T(8,128)(2,1)S(1)} %get-tuple-element.527.refs_3_), channel_id=1, source_target_pairs={{0,8},{4,12},{24,16},{28,20},{8,0},{12,4},{16,24},{20,28},{1,9},{5... | collective-permute-start | bytes 1179656 | tf_op jit(solution)/shard_map/ppermute | solution.py:406
  468.2 15.1 %collective-permute-start.78 = (bf16[768,256]{1,0:T(8,128)(2,1)S(1)}, bf16[768,256]{1,0:T(8,128)(2,1)S(1)}, u32[]{:S(2)}, u32[]{:S(2)}) collective-permute-start(bf16[768,256]{1,0:T(8,128)(2,1)S(1)} %get-tuple-element.542.refs_3_), channel_id=1, source_target_pairs={{0,8},{4,12},{24,16},{28,20},{8,0},{12,4},{16,24},{20,28},{1,9},{5... | collective-permute-start | bytes 1179656 | tf_op jit(solution)/shard_map/ppermute | solution.py:406
  (148 other events, 1006.0 us)
Sparse Core Ops, SparseCore 0:
  9.5 111.1 all-gather.2
  140.9 45.4 reduce-scatter.1
  193.3 23.2 all-gather.4

commit v2 on v1

--- a/solution.py
+++ b/solution.py
@@ -6,6 +6,7 @@
 from jax.sharding import PartitionSpec as P
 
 SEQ_LEN = 256
+EXTRA = {0: 1, 1: 1, 2: 1, 3: 1, 4: 1, 9: 1, 10: 1, 11: 1, 12: 1, 13: 2, 14: 1}
 PARTS = 4
 WIDTH = 256
 BF16 = jnp.bfloat16
@@ -73,11 +74,11 @@
 
 def unit_list(count):
     lead = 6
-    units = [[(0, i)] for i in range(4)] + [[(0, 4), (0, 5)]]
+    units = [[(0, i)] for i in range(lead)]
     units += [[(1, i), (1, i + 1)] for i in range(0, lead, 2)]
     rest = [(half, i) for i in range(lead, count) for half in (0, 1)]
     while rest:
-        size = 2 if len(rest) > 8 else 1
+        size = 2 if len(rest) > 4 else 1
         units.append(rest[:size])
         rest = rest[size:]
     return units
@@ -89,7 +90,7 @@
         self.token = jnp.zeros((8, 128), F32)
         self.also = []
 
-    def run(self, body, operands, in_specs, outputs, out_specs, grid, flops, size, aliases=None, vmem=12):
+    def run(self, body, operands, in_specs, outputs, out_specs, grid, flops, size, aliases=None, vmem=10):
         waits = [self.token, *self.also]
         self.also = []
         count, made = len(operands), len(outputs)
@@ -115,7 +116,7 @@
         return results[:made]
 
 
-def multiply(chain, blocks, matrix, first, width, tile=256):
+def multiply(chain, blocks, matrix, first, width, dtype, vmem, tile=256):
     rows = sum(block.shape[0] for block in blocks)
     inner = matrix.shape[0]
     base = first // tile
@@ -126,19 +127,19 @@
         for block in ins[:-1]:
             here = slice(start, start + block.shape[0])
             start += block.shape[0]
-            result[here, :] = jnp.dot(block[...], ins[-1][...], preferred_element_type=F32)
+            result[here, :] = jnp.dot(block[...], ins[-1][...], preferred_element_type=F32).astype(dtype)
 
     return chain.run(
         body,
         [*blocks, matrix],
         [pl.BlockSpec(block.shape, lambda j, flags: (0, 0), pipeline_mode=pl.Buffered(1)) for block in blocks]
         + [pl.BlockSpec((inner, tile), lambda j, flags: (0, base + j))],
-        [jax.ShapeDtypeStruct((rows, width), F32)],
+        [jax.ShapeDtypeStruct((rows, width), dtype)],
         [pl.BlockSpec((rows, tile), lambda j, flags: (0, j))],
         (width // tile,),
         2 * rows * inner * width,
         2 * inner * (rows + width) + 4 * rows * width,
-        vmem=18,
+        vmem=vmem,
     )[0]
 
 
@@ -151,6 +152,75 @@
     spec = pl.BlockSpec((tile, value.shape[1]), lambda r, flags: (r, 0))
     shape = jax.ShapeDtypeStruct(value.shape, value.dtype)
     return chain.run(body, [value], [spec], [shape], [spec], (value.shape[0] // tile,), 0, 4 * value.size)[0]
+
+
+def rotate_out(chain, grads, basis):
+    inner, width = basis.shape
+    tile = 256
+
+    def body(flags, ins, outs):
+        for q in range(PARTS):
+            rows = pl.ds(pl.multiple_of((flags[3] ^ q) * SEQ_LEN, SEQ_LEN), SEQ_LEN)
+            product = jnp.dot(ins[0][rows, :], ins[1][...], preferred_element_type=F32)
+            outs[q % 2][q // 2 * SEQ_LEN : (q // 2 + 1) * SEQ_LEN, :] = product
+
+    half = jax.ShapeDtypeStruct((2 * SEQ_LEN, width), F32)
+    return chain.run(
+        body,
+        [grads, basis],
+        [
+            pl.BlockSpec(grads.shape, lambda j, flags: (0, 0), pipeline_mode=pl.Buffered(1)),
+            pl.BlockSpec((inner, tile), lambda j, flags: (0, j)),
+        ],
+        [half, half],
+        [pl.BlockSpec((2 * SEQ_LEN, tile), lambda j, flags: (0, j))] * 2,
+        (width // tile,),
+        2 * grads.size * width,
+        2 * (grads.size + basis.size) + 4 * PARTS * SEQ_LEN * width,
+        vmem=14,
+    )
+
+
+def add_rows(chain, mine, other, dtype):
+    rows, width = mine.shape
+    tile = 256
+    count = rows // SEQ_LEN
+
+    def body(flags, ins, outs):
+        for n in range(count):
+            here = slice(n * SEQ_LEN, (n + 1) * SEQ_LEN)
+            outs[n][...] = (ins[0][here, :] + ins[1][here, :]).astype(dtype)
+
+    return chain.run(
+        body,
+        [mine, other],
+        [pl.BlockSpec((rows, tile), lambda j, flags: (0, j))] * 2,
+        [jax.ShapeDtypeStruct((SEQ_LEN, width), dtype)] * count,
+        [pl.BlockSpec((SEQ_LEN, tile), lambda j, flags: (0, j))] * count,
+        (width // tile,),
+        0,
+        12 * rows * width,
+    )
+
+
+def turn(chain, pieces):
+    rows, width = pieces[0].shape
+    tile = 256
+
+    def body(flags, ins, outs):
+        for q in range(len(pieces)):
+            outs[0][q] = ins[q][...].T
+
+    return chain.run(
+        body,
+        pieces,
+        [pl.BlockSpec((rows, tile), lambda j, flags: (0, j))] * len(pieces),
+        [jax.ShapeDtypeStruct((len(pieces), width, rows), pieces[0].dtype)],
+        [pl.BlockSpec((len(pieces), tile, rows), lambda j, flags: (0, j, 0))],
+        (width // tile,),
+        0,
+        4 * len(pieces) * rows * width,
+    )[0]
 
 
 def layout(parts):
@@ -239,7 +309,7 @@
             for s in range(n(k)):
                 put("y", "a1", refs[f"p0a{s}"][rows((1 - y) * half), :], s * half)
             for s in range(n(k - 1)):
-                total = refs[f"p1a{s}"][rows(y * half), :] + take("got", "y", "a1", s * half).astype(F32)
+                total = refs[f"p1a{s}"][rows(y * half), :].astype(F32) + take("got", "y", "a1", s * half).astype(F32)
                 refs["new_a1"][s * half : (s + 1) * half, :] = total
 
             @pl.when(outer)
@@ -257,7 +327,7 @@
             def _():
                 for s in range(n(k - 1)):
                     for keep, start in ((False, (1 - side) * half), (True, side * half)):
-                        value = refs[f"p1b{s}"][rows(start), :]
+                        value = refs[f"p1b{s}"][rows(start), :].astype(F32)
                         value += take("got", "z", "zb", start + s * 2 * half).astype(F32)
                         if keep:
                             refs["new_b1"][s * half : (s + 1) * half, :] = value
@@ -283,7 +353,7 @@
                 if n(k - 5):
                     refs["final"][...] = take("sent", "z", "zb", 0, 2 * half * n(k - 5))
 
-        made = self.chain.run(body, operands, in_specs, outputs, out_specs, (WIDTH // 128,), 0, size, vmem=4 + size // 2**20 * 5 // 4)
+        made = self.chain.run(body, operands, in_specs, outputs, out_specs, (WIDTH // 128,), 0, size, vmem=4 + size // 2**20)
         made = dict(zip(out_names, made))
         ready = []
         for s in range(n(k - 5)):
@@ -397,7 +467,7 @@
         other = lax.ppermute(total, "feat", middle)
         return [spread(total, z), spread(other, z)]
 
-    def pipelined(activations, out_grads, basis_in, basis_out, flags, ordered):
+    def pipelined(activations, out_grads, basis_in, basis_out, flags):
         columns = basis_in.shape[1]
         chain = Chain(flags)
         stay = [(k, k) for k in range(feat) if k // 2 in (0, depth - 1)]
@@ -415,8 +485,13 @@
         count = columns // (2 * WIDTH)
         units = unit_list(count)
         lanes = [Lane(chain, units[p::2], permute) for p in (0, 1)]
-        finished, made = {}, {}
-        result = rotated_out = out_t = None
+        finished, made, waiting = {}, {}, []
+
+        def square(result, i):
+            pair = (finished[0, i], finished[1, i])
+            return square_chunk(chain, result, out_t, pair, i, columns, 1.0 / tokens_all)
+
+        result = out_t = None
         for j in range(len(units) + 12):
             lane, k = lanes[j % 2], j // 2
             if k >= len(lane.units) + 6:
@@ -436,26 +511,34 @@
                     chunks = sorted({i for _, i in group})
                     blocks = [block for half in halves for block in tokens[half]]
                     wide = 2 * WIDTH * len(chunks)
-                    array = multiply(chain, blocks, basis_in, chunks[0] * 2 * WIDTH, wide)
+                    array = multiply(chain, blocks, basis_in, chunks[0] * 2 * WIDTH, wide, BF16, 8 if len(blocks) == 2 else 14)
                     for half, i in group:
                         made[half, i] = (array, halves.index(half), chunks.index(i) * 2 * WIDTH)
                 partials = [made[sub] for sub in unit]
             ready = lane.advance(k, partials)
             other = lanes[1 - j % 2].got
-            if len(other) == 3 and len(lane.got) == 3:
-                chain.also.append(other["m"])
-            if j == 6:
-                share = multiply(chain, [grad_all], basis_out, 0, basis_out.shape[1])
-                share = lax.psum_scatter(share, "ex", scatter_dimension=0, tiled=True)
-                rotated_out = lax.all_gather(share.astype(BF16), "ex", axis=0, tiled=True)
-            if j == 14:
-                out_t = ordered(rotated_out, 0).reshape(-1, PARTS, SEQ_LEN).transpose(1, 0, 2)
-                chain.also.append(out_t)
+            spare = len(lane.got) + len(other) + EXTRA.get(j, 0) - 5
+            chain.also += [other[link] for link in "myz" if link in other][: max(spare, 0)]
+            if j == 9:
+                keep, away = rotate_out(chain, grad_all, basis_out)
+                away = swap_ex(away, 1)
+            if j == 10:
+                keep, away = add_rows(chain, keep, away, F32)
+                away = swap_ex(away, 2)
+            if j == 13:
+                (own,) = add_rows(chain, keep, away, BF16)
+                across = swap_ex(own, 2)
+                beside = [swap_ex(own, 1), swap_ex(across, 1)]
+            if j == 15:
+                out_t = turn(chain, [own, beside[0], across, beside[1]])
             for (half, i), value in ready:
                 finished[half, i] = value
                 if (1 - half, i) in finished:
-                    pair = (finished[0, i], finished[1, i])
-                    result = square_chunk(chain, result, out_t, pair, i, columns, 1.0 / tokens_all)
+                    waiting.append(i)
+            if waiting and out_t is not None:
+                result = square(result, waiting.pop(0))
+        for i in waiting:
+            result = square(result, i)
         return result
 
     def per_device(activations, out_grads, basis_in, basis_out):
@@ -477,8 +560,8 @@
 
         if depth == 4 and ex == PARTS and block == SEQ_LEN and columns % (2 * WIDTH) == 0:
             outer = ((z == 0) | (z == depth - 1)).astype(jnp.int32)
-            flags = jnp.stack([y.astype(jnp.int32), side, outer])
-            return pipelined(activations, out_grads, basis_in, basis_out, flags, ordered)
+            flags = jnp.stack([y.astype(jnp.int32), side, outer, e.astype(jnp.int32)])
+            return pipelined(activations, out_grads, basis_in, basis_out, flags)
 
         far = swap_ex(activations, ex // 2)
         tokens_half = [gather_low(activations), gather_low(far)]

time: 512 us -> 496 us (0.969)
  waiting for transfers between devices: 55.8 us -> 94.2 us
  local copies, waits for them, and re-layouts: 54.2 us -> 25 us
  Pallas kernels: 221 us -> 207 us
  starting transfers between devices: 153 us -> 146 us
    ppermute x28 -> x27, waiting for transfers between devices: 39 us -> 71.2 us  [pipelined(): lax.ppermute(v, 'feat', inward[0] + outward[0])]
    unnamed x252 -> x90, local copies, waits for them, and re-layouts: 49.7 us -> 25 us
    ppermute x24 -> x23, starting transfers between devices: 39.1 us -> 18.2 us  [pipelined(): lax.ppermute(v, 'feat', middle + stay)]
    ppermute x28 -> x27, starting transfers between devices: 78 us -> 93.6 us  [pipelined(): lax.ppermute(v, 'feat', inward[0] + outward[0])]
    pallas_call x64 -> x65, Pallas kernels: 221 us -> 207 us  [call(): pl.pallas_call(kernel, grid_spec=pltpu.PrefetchScalarGridSpec(num_scalar_...]
    ppermute x28 -> x27, starting transfers between devices: 32.3 us -> 29.3 us  [pipelined(): lax.ppermute(v, 'feat', y_swap)]
    ppermute x28 -> x27, waiting for transfers between devices: 15 us -> 16.2 us  [pipelined(): lax.ppermute(v, 'feat', y_swap)]
  transfers between devices with their start and end apart: 86 -> 86, of which waited for: 15 -> 15; matrix products, arithmetic and copies ran while one was open for 2% -> 0% of each run, Pallas kernels for 42% -> 40%
where the time goes in v2:
time: 496 us; the launch traced here: 488 us
  Pallas kernels  207 us (42%)
  starting transfers between devices  146 us (29%)
  waiting for transfers between devices  94.2 us (19%)
  local copies, waits for them, and re-layouts  25 us (5%)
  between operations  15.1 us (3%)
    pallas_call x65, Pallas kernels, call(): pl.pallas_call(kernel, grid_spec=pltpu.PrefetchScalarGridSpec(num_scalar_...  207 us
    ppermute x27, starting transfers between devices, pipelined(): lax.ppermute(v, 'feat', inward[0] + outward[0])  93.6 us
    ppermute x27, waiting for transfers between devices, pipelined(): lax.ppermute(v, 'feat', inward[0] + outward[0])  71.2 us
    ppermute x27, starting transfers between devices, pipelined(): lax.ppermute(v, 'feat', y_swap)  29.3 us
    unnamed x90, local copies, waits for them, and re-layouts  25 us
    ppermute x23, starting transfers between devices, pipelined(): lax.ppermute(v, 'feat', middle + stay)  18.2 us
    ppermute x27, waiting for transfers between devices, pipelined(): lax.ppermute(v, 'feat', y_swap)  16.2 us
  transfers between devices with their start and end apart: 86, of which 15 were waited for; matrix products, arithmetic and copies ran while one was open for 0% of the time, Pallas kernels for 40%

profile of v2, /device:TPU:0, one launch (start us, length us, event | category | flops | bytes accessed | tf_op | source)
XLA Modules:
  0.0 487.8 jit_solution(16841011423054094877)
XLA Ops:
  7.8 2.6 collective-permute-start.11
  13.6 4.3 shard_map.46
  18.7 3.0 collective-permute-start.4
  23.2 4.3 shard_map.48
  29.1 4.3 shard_map.50
  33.4 6.6 %collective-permute-done.4.refs_1_ = bf16[512,256]{1,0:T(8,128)(2,1)S(1)} collective-permute-done((bf16[512,256]{1,0:T(8,128)(2,1)S(1)}, bf16[512,256]{1,0:T(8,128)(2,1)S(1)}, u32[]{:S(2)}, u32[]{:S(2)}) %collective-permute-start.4) | collective-permute-done | bytes 262176 | tf_op jit(solution)/shard_map/ppermute | solution.py:476
  43.6 4.3 shard_map.52
  47.9 2.6 collective-permute-done.2.refs_1_
  57.5 4.5 collective-permute-start.6
  62.0 4.3 shard_map.55
  66.3 16.0 %collective-permute-done.9.refs_1_ = bf16[768,256]{1,0:T(8,128)(2,1)S(1)} collective-permute-done((bf16[768,256]{1,0:T(8,128)(2,1)S(1)}, bf16[768,256]{1,0:T(8,128)(2,1)S(1)}, u32[]{:S(2)}, u32[]{:S(2)}) %collective-permute-start.9) | collective-permute-done | bytes 393248 | tf_op jit(solution)/shard_map/ppermute | solution.py:476
  84.4 5.6 %collective-permute-start.17 = (bf16[768,256]{1,0:T(8,128)(2,1)S(1)}, bf16[768,256]{1,0:T(8,128)(2,1)S(1)}, u32[]{:S(2)}, u32[]{:S(2)}) collective-permute-start(bf16[768,256]{1,0:T(8,128)(2,1)S(1)} %get-tuple-element.314), channel_id=1, source_target_pairs={{0,8},{4,12},{24,16},{28,20},{8,0},{12,4},{16,24},{20,28},{1,9},{5... | collective-permute-start | bytes 1179656 | tf_op jit(solution)/shard_map/ppermute | solution.py:476
  91.6 4.3 shard_map.57
  96.0 8.9 %collective-permute-done.6.refs_1_ = bf16[768,256]{1,0:T(8,128)(2,1)S(1)} collective-permute-done((bf16[768,256]{1,0:T(8,128)(2,1)S(1)}, bf16[768,256]{1,0:T(8,128)(2,1)S(1)}, u32[]{:S(2)}, u32[]{:S(2)}) %collective-permute-start.6) | collective-permute-done | bytes 393248 | tf_op jit(solution)/shard_map/ppermute | solution.py:476
  106.9 6.1 %collective-permute-start.13 = (bf16[768,256]{1,0:T(8,128)(2,1)S(1)}, bf16[768,256]{1,0:T(8,128)(2,1)S(1)}, u32[]{:S(2)}, u32[]{:S(2)}) collective-permute-start(bf16[768,256]{1,0:T(8,128)(2,1)S(1)} %get-tuple-element.310), channel_id=1, source_target_pairs={{0,8},{4,12},{24,16},{28,20},{8,0},{12,4},{16,24},{20,28},{1,9},{5... | collective-permute-start | bytes 1179656 | tf_op jit(solution)/shard_map/ppermute | solution.py:476
  114.6 7.0 %shard_map.59 = (bf16[512,1024]{1,0:T(8,128)(2,1)S(1)}, f32[8,128]{1,0:T(8,128)S(1)}) custom-call(s32[4]{0:T(128)S(1)} %pad_add_fusion.flags, bf16[256,3584]{1,0:T(8,128)(2,1)S(1)} %get-tuple-element.312.refs_0_.refs_2_, bf16[256,3584]{1,0:T(8,128)(2,1)S(1)} %collective-permute-done.15.refs_1_.refs_3_, bf16[3584,7168]{1,0:T(8,128)(2,1)} %refs_2_.25, ...), custom_call_target="tpu_custom_call" | custom-call | flops 3758096384 | bytes 13107200 | tf_op jit(solution)/shard_map/pallas_call | solution.py:63
  127.2 7.1 %shard_map.61 = (bf16[512,1024]{1,0:T(8,128)(2,1)S(1)}, f32[8,128]{1,0:T(8,128)S(1)}) custom-call(s32[4]{0:T(128)S(1)} %pad_add_fusion.flags, bf16[256,3584]{1,0:T(8,128)(2,1)S(1)} %get-tuple-element.312.refs_0_.refs_2_, bf16[256,3584]{1,0:T(8,128)(2,1)S(1)} %collective-permute-done.15.refs_1_.refs_3_, bf16[3584,7168]{1,0:T(8,128)(2,1)} %refs_2_.25, ...), custom_call_target="tpu_custom_call" | custom-call | flops 3758096384 | bytes 13107200 | tf_op jit(solution)/shard_map/pallas_call | solution.py:63
  141.4 7.1 %shard_map.63 = (bf16[512,1024]{1,0:T(8,128)(2,1)S(1)}, f32[8,128]{1,0:T(8,128)S(1)}) custom-call(s32[4]{0:T(128)S(1)} %pad_add_fusion.flags, bf16[256,3584]{1,0:T(8,128)(2,1)S(1)} %get-tuple-element.312.refs_0_.refs_2_, bf16[256,3584]{1,0:T(8,128)(2,1)S(1)} %collective-permute-done.15.refs_1_.refs_3_, bf16[3584,7168]{1,0:T(8,128)(2,1)} %refs_2_.25, ...), custom_call_target="tpu_custom_call" | custom-call | flops 3758096384 | bytes 13107200 | tf_op jit(solution)/shard_map/pallas_call | solution.py:63
  153.1 10.5 %shard_map.65 = (bf16[1024,1024]{1,0:T(8,128)(2,1)S(1)}, f32[8,128]{1,0:T(8,128)S(1)}) custom-call(s32[4]{0:T(128)S(1)} %pad_add_fusion.flags, bf16[256,3584]{1,0:T(8,128)(2,1)S(1)} %copy-done.1, bf16[256,3584]{1,0:T(8,128)(2,1)S(1)} %copy-done.4, bf16[256,3584]{1,0:T(8,128)(2,1)S(1)} %get-tuple-element.312.refs_0_.refs_2_, ...), custom_call_target="tpu_custom_call" | custom-call | flops 7516192768 | bytes 18874368 | tf_op jit(solution)/shard_map/pallas_call | solution.py:63
  179.9 6.5 %shard_map.67 = (f32[512,1024]{1,0:T(8,128)S(1)}, f32[512,1024]{1,0:T(8,128)S(1)}, f32[8,128]{1,0:T(8,128)S(1)}) custom-call(s32[4]{0:T(128)S(1)} %pad_add_fusion.flags, bf16[1024,2048]{1,0:T(8,128)(2,1)S(1)} %copy-done.44, bf16[2048,1024]{1,0:T(8,128)(2,1)S(1)} %copy-done.43, f32[8,128]{1,0:T(8,128)S(1)} %get-tuple-element.350.refs_2_, ...), custom_call_target="tpu_custom_call" | custom-call | flops 4294967296 | bytes 12582912 | tf_op jit(solution)/shard_map/pallas_call | solution.py:63
  186.5 2.8 collective-permute-start.28
  193.8 14.1 %collective-permute-done.28.refs_1_ = bf16[1536,256]{1,0:T(8,128)(2,1)S(1)} collective-permute-done((bf16[1536,256]{1,0:T(8,128)(2,1)}, bf16[1536,256]{1,0:T(8,128)(2,1)S(1)}, u32[]{:S(2)}, u32[]{:S(2)}) %collective-permute-start.28) | collective-permute-done | bytes 786464 | tf_op jit(solution)/shard_map/ppermute | solution.py:476
  216.1 2.8 shard_map.68
  224.8 10.7 %shard_map.70 = (bf16[1024,1024]{1,0:T(8,128)(2,1)S(1)}, f32[8,128]{1,0:T(8,128)S(1)}) custom-call(s32[4]{0:T(128)S(1)} %pad_add_fusion.flags, bf16[256,3584]{1,0:T(8,128)(2,1)S(1)} %copy-done.2, bf16[256,3584]{1,0:T(8,128)(2,1)S(1)} %copy-done.5, bf16[256,3584]{1,0:T(8,128)(2,1)S(1)} %copy-done.7, bf16[256,3584]{1,0:T(8,128)(2,1)S(1)} %copy-done.9, ...), custom_call_target="tpu_custom_call" | custom-call | flops 7516192768 | bytes 18874368 | tf_op jit(solution)/shard_map/pallas_call | solution.py:63
  235.5 2.8 shard_map.71
  239.7 4.8 collective-permute-start.34
  244.5 2.8 shard_map.72
  250.6 3.1 collective-permute-done.33.refs_7_.refs_0_.refs_2_
  255.6 10.5 %shard_map.73 = (bf16[1024,1024]{1,0:T(8,128)(2,1)S(1)}, f32[8,128]{1,0:T(8,128)S(1)}) custom-call(s32[4]{0:T(128)S(1)} %pad_add_fusion.flags, bf16[256,3584]{1,0:T(8,128)(2,1)S(1)} %copy-done.2, bf16[256,3584]{1,0:T(8,128)(2,1)S(1)} %copy-done.5, bf16[256,3584]{1,0:T(8,128)(2,1)S(1)} %copy-done.7, bf16[256,3584]{1,0:T(8,128)(2,1)S(1)} %copy-done.9, ...), custom_call_target="tpu_custom_call" | custom-call | flops 7516192768 | bytes 18874368 | tf_op jit(solution)/shard_map/pallas_call | solution.py:63
  266.2 2.9 shard_map.74
  271.4 9.3 %collective-permute-start.46 = (bf16[1536,256]{1,0:T(8,128)(2,1)S(1)}, bf16[1536,256]{1,0:T(8,128)(2,1)S(1)}, u32[]{:S(2)}, u32[]{:S(2)}) collective-permute-start(bf16[1536,256]{1,0:T(8,128)(2,1)S(1)} %get-tuple-element.398.refs_3_), channel_id=1, source_target_pairs={{0,8},{4,12},{24,16},{28,20},{8,0},{12,4},{16,24},{20,28},{1,9},{5... | collective-permute-start | bytes 2359304 | tf_op jit(solution)/shard_map/ppermute | solution.py:476
  282.2 2.9 shard_map.76
  285.9 5.0 %collective-permute-done.43.refs_2_ = bf16[256,1024]{1,0:T(8,128)(2,1)S(1)} collective-permute-done((bf16[256,1024]{1,0:T(8,128)(2,1)S(1)}, bf16[256,1024]{1,0:T(8,128)(2,1)S(1)}, u32[]{:S(2)}, u32[]{:S(2)}) %collective-permute-start.43) | collective-permute-done | bytes 524320 | tf_op jit(solution)/shard_map/ppermute | solution.py:429
  295.0 4.3 shard_map.77
  299.3 2.7 shard_map.78
  302.8 8.1 %collective-permute-start.50 = (bf16[1536,256]{1,0:T(8,128)(2,1)S(1)}, bf16[1536,256]{1,0:T(8,128)(2,1)S(1)}, u32[]{:S(2)}, u32[]{:S(2)}) collective-permute-start(bf16[1536,256]{1,0:T(8,128)(2,1)S(1)} %get-tuple-element.416.refs_3_), channel_id=1, source_target_pairs={{0,8},{4,12},{24,16},{28,20},{8,0},{12,4},{16,24},{20,28},{1,9},{5... | collective-permute-start | bytes 2359304 | tf_op jit(solution)/shard_map/ppermute | solution.py:476
  312.8 4.3 shard_map.80
  317.2 2.8 shard_map.81
  321.0 2.6 collective-permute-start.59
  325.4 3.1 shard_map.82
  328.5 4.3 shard_map.83
  336.0 6.1 %collective-permute-start.55 = (bf16[1536,256]{1,0:T(8,128)(2,1)S(1)}, bf16[1536,256]{1,0:T(8,128)(2,1)S(1)}, u32[]{:S(2)}, u32[]{:S(2)}) collective-permute-start(bf16[1536,256]{1,0:T(8,128)(2,1)S(1)} %get-tuple-element.438.refs_3_), channel_id=1, source_target_pairs={{0,8},{4,12},{24,16},{28,20},{8,0},{12,4},{16,24},{20,28},{1,9},{5... | collective-permute-start | bytes 2359304 | tf_op jit(solution)/shard_map/ppermute | solution.py:476
  342.9 3.1 shard_map.85
  346.1 4.3 shard_map.86
  352.9 3.3 collective-permute-start.65
  357.6 3.1 shard_map.88
  365.9 4.5 collective-permute-start.61
  370.4 3.1 shard_map.90
  373.5 6.4 %collective-permute-done.65.refs_1_ = bf16[1536,256]{1,0:T(8,128)(2,1)S(1)} collective-permute-done((bf16[1536,256]{1,0:T(8,128)(2,1)S(1)}, bf16[1536,256]{1,0:T(8,128)(2,1)S(1)}, u32[]{:S(2)}, u32[]{:S(2)}) %collective-permute-start.65) | collective-permute-done | bytes 786464 | tf_op jit(solution)/shard_map/ppermute | solution.py:476
  387.3 3.1 shard_map.92
  390.5 6.9 %collective-permute-done.60.refs_0_.refs_2_.refs_4_ = bf16[768,256]{1,0:T(8,128)(2,1)S(1)} collective-permute-done((bf16[768,256]{1,0:T(8,128)(2,1)S(1)}, bf16[768,256]{1,0:T(8,128)(2,1)S(1)}, u32[]{:S(2)}, u32[]{:S(2)}) %collective-permute-start.60) | collective-permute-done | bytes 393248 | tf_op jit(solution)/shard_map/ppermute | solution.py:475
  401.5 3.1 shard_map.94
  404.6 8.9 %collective-permute-done.71.refs_1_ = bf16[1536,256]{1,0:T(8,128)(2,1)S(1)} collective-permute-done((bf16[1536,256]{1,0:T(8,128)(2,1)S(1)}, bf16[1536,256]{1,0:T(8,128)(2,1)S(1)}, u32[]{:S(2)}, u32[]{:S(2)}) %collective-permute-start.71) | collective-permute-done | bytes 786464 | tf_op jit(solution)/shard_map/ppermute | solution.py:476
  420.9 3.1 shard_map.96
  424.1 6.2 %collective-permute-done.66.refs_0_.refs_2_.refs_4_ = bf16[768,256]{1,0:T(8,128)(2,1)S(1)} collective-permute-done((bf16[768,256]{1,0:T(8,128)(2,1)S(1)}, bf16[768,256]{1,0:T(8,128)(2,1)S(1)}, u32[]{:S(2)}, u32[]{:S(2)}) %collective-permute-start.66) | collective-permute-done | bytes 393248 | tf_op jit(solution)/shard_map/ppermute | solution.py:475
  434.0 3.1 shard_map.98
  437.2 4.5 collective-permute-done.77.refs_1_
  448.9 3.1 shard_map.100
  453.0 6.4 %collective-permute-start.83 = (bf16[512,256]{1,0:T(8,128)(2,1)S(1)}, bf16[512,256]{1,0:T(8,128)(2,1)S(1)}, u32[]{:S(2)}, u32[]{:S(2)}) collective-permute-start(bf16[512,256]{1,0:T(8,128)(2,1)S(1)} %get-tuple-element.530.refs_2_), channel_id=1, source_target_pairs={{0,8},{4,12},{24,16},{28,20},{8,0},{12,4},{16,24},{20,28},{1,9},{5... | collective-permute-start | bytes 786440 | tf_op jit(solution)/shard_map/ppermute | solution.py:476
  459.4 3.1 shard_map.102
  465.7 3.1 shard_map.104
  469.6 3.1 shard_map.106
  473.6 3.2 shard_map.108
  477.3 3.2 shard_map.110
  (266 shorter events, 147.7 us)
Async XLA Ops:
  6.5 166.2 %all-gather.2.cloned.1.call-start = ((), (), s32[]{:S(2)}) async-start(), calls=%async_computation | async-start | bytes 4718592 | tf_op jit(solution)/shard_map/all_gather | solution.py:481
  7.8 43.9 %collective-permute-start.11 = (bf16[256,3584]{1,0:T(8,128)(2,1)}, bf16[256,3584]{1,0:T(8,128)(2,1)}, u32[]{:S(2)}, u32[]{:S(2)}) collective-permute-start(bf16[256,3584]{1,0:T(8,128)(2,1)} %refs_0_.21), channel_id=1, source_target_pairs={{0,2},{1,3},{2,0},{3,1},{4,6},{5,7},{6,4},{7,5},{8,10},{9,11},{10,... | collective-permute-start | bytes 5505032 | tf_op jit(solution)/shard_map/ppermute | solution.py:429
  18.7 21.3 %collective-permute-start.4 = (bf16[512,256]{1,0:T(8,128)(2,1)S(1)}, bf16[512,256]{1,0:T(8,128)(2,1)S(1)}, u32[]{:S(2)}, u32[]{:S(2)}) collective-permute-start(bf16[512,256]{1,0:T(8,128)(2,1)S(1)} %get-tuple-element.285), channel_id=1, source_target_pairs={{0,8},{4,12},{24,16},{28,20},{8,0},{12,4},{16,24},{20,28},{1,9},{5... | collective-permute-start | bytes 786440 | tf_op jit(solution)/shard_map/ppermute | solution.py:476
  29.0 21.5 %collective-permute-start.2 = (bf16[512,256]{1,0:T(8,128)(2,1)S(1)}, bf16[512,256]{1,0:T(8,128)(2,1)S(1)}, u32[]{:S(2)}, u32[]{:S(2)}) collective-permute-start(bf16[512,256]{1,0:T(8,128)(2,1)S(1)} %get-tuple-element.283), channel_id=1, source_target_pairs={{0,8},{4,12},{24,16},{28,20},{8,0},{12,4},{16,24},{20,28},{1,9},{5... | collective-permute-start | bytes 786440 | tf_op jit(solution)/shard_map/ppermute | solution.py:476
  53.8 59.2 %collective-permute-start.15 = (bf16[256,3584]{1,0:T(8,128)(2,1)S(1)}, bf16[256,3584]{1,0:T(8,128)(2,1)S(1)}, u32[]{:S(2)}, u32[]{:S(2)}) collective-permute-start(bf16[256,3584]{1,0:T(8,128)(2,1)S(1)} %get-tuple-element.312.refs_0_.refs_2_), channel_id=1, source_target_pairs={{0,1},{1,0},{2,3},{3,2},{4,5},{5,4},{6,7},{7,6},{8,9},{9,8},{10,11... | collective-permute-start | bytes 5505032 | tf_op jit(solution)/shard_map/ppermute | solution.py:429
  53.9 28.5 %collective-permute-start.9 = (bf16[768,256]{1,0:T(8,128)(2,1)S(1)}, bf16[768,256]{1,0:T(8,128)(2,1)S(1)}, u32[]{:S(2)}, u32[]{:S(2)}) collective-permute-start(bf16[768,256]{1,0:T(8,128)(2,1)S(1)} %get-tuple-element.296), channel_id=1, source_target_pairs={{0,8},{4,12},{24,16},{28,20},{8,0},{12,4},{16,24},{20,28},{1,9},{5... | collective-permute-start | bytes 1179656 | tf_op jit(solution)/shard_map/ppermute | solution.py:476
  55.4 29.1 %collective-permute-start.5 = (bf16[256,256]{1,0:T(8,128)(2,1)S(1)}, bf16[256,256]{1,0:T(8,128)(2,1)S(1)}, u32[]{:S(2)}, u32[]{:S(2)}) collective-permute-start(bf16[256,256]{1,0:T(8,128)(2,1)S(1)} %get-tuple-element.292), channel_id=1, source_target_pairs={{0,4},{4,0},{8,12},{12,8},{16,20},{20,16},{24,28},{28,24},{1,5},{5... | collective-permute-start | bytes 393224 | tf_op jit(solution)/shard_map/ppermute | solution.py:475
  56.9 33.2 %collective-permute-start.7 = (bf16[256,256]{1,0:T(8,128)(2,1)S(1)}, bf16[256,256]{1,0:T(8,128)(2,1)S(1)}, u32[]{:S(2)}, u32[]{:S(2)}) collective-permute-start(bf16[256,256]{1,0:T(8,128)(2,1)S(1)} %get-tuple-element.294), channel_id=1, source_target_pairs={{8,16},{12,20},{16,8},{20,12},{0,0},{4,4},{24,24},{28,28},{9,17},{... | collective-permute-start | bytes 393224 | tf_op jit(solution)/shard_map/ppermute | solution.py:477
  57.5 47.3 %collective-permute-start.6 = (bf16[768,256]{1,0:T(8,128)(2,1)S(1)}, bf16[768,256]{1,0:T(8,128)(2,1)S(1)}, u32[]{:S(2)}, u32[]{:S(2)}) collective-permute-start(bf16[768,256]{1,0:T(8,128)(2,1)S(1)} %get-tuple-element.293), channel_id=1, source_target_pairs={{0,8},{4,12},{24,16},{28,20},{8,0},{12,4},{16,24},{20,28},{1,9},{5... | collective-permute-start | bytes 1179656 | tf_op jit(solution)/shard_map/ppermute | solution.py:476
  83.7 23.2 %collective-permute-start.18 = (bf16[512,256]{1,0:T(8,128)(2,1)S(1)}, bf16[512,256]{1,0:T(8,128)(2,1)S(1)}, u32[]{:S(2)}, u32[]{:S(2)}) collective-permute-start(bf16[512,256]{1,0:T(8,128)(2,1)S(1)} %get-tuple-element.315), channel_id=1, source_target_pairs={{8,16},{12,20},{16,8},{20,12},{0,0},{4,4},{24,24},{28,28},{9,17},{... | collective-permute-start | bytes 786440 | tf_op jit(solution)/shard_map/ppermute | solution.py:477
  84.4 37.2 %collective-permute-start.17 = (bf16[768,256]{1,0:T(8,128)(2,1)S(1)}, bf16[768,256]{1,0:T(8,128)(2,1)S(1)}, u32[]{:S(2)}, u32[]{:S(2)}) collective-permute-start(bf16[768,256]{1,0:T(8,128)(2,1)S(1)} %get-tuple-element.314), channel_id=1, source_target_pairs={{0,8},{4,12},{24,16},{28,20},{8,0},{12,4},{16,24},{20,28},{1,9},{5... | collective-permute-start | bytes 1179656 | tf_op jit(solution)/shard_map/ppermute | solution.py:476
  90.1 31.6 %collective-permute-start.16 = (bf16[512,256]{1,0:T(8,128)(2,1)S(1)}, bf16[512,256]{1,0:T(8,128)(2,1)S(1)}, u32[]{:S(2)}, u32[]{:S(2)}) collective-permute-start(bf16[512,256]{1,0:T(8,128)(2,1)S(1)} %get-tuple-element.313), channel_id=1, source_target_pairs={{0,4},{4,0},{8,12},{12,8},{16,20},{20,16},{24,28},{28,24},{1,5},{5... | collective-permute-start | bytes 786440 | tf_op jit(solution)/shard_map/ppermute | solution.py:475
  106.2 20.6 %collective-permute-start.14 = (bf16[512,256]{1,0:T(8,128)(2,1)S(1)}, bf16[512,256]{1,0:T(8,128)(2,1)S(1)}, u32[]{:S(2)}, u32[]{:S(2)}) collective-permute-start(bf16[512,256]{1,0:T(8,128)(2,1)S(1)} %get-tuple-element.311), channel_id=1, source_target_pairs={{8,16},{12,20},{16,8},{20,12},{0,0},{4,4},{24,24},{28,28},{9,17},{... | collective-permute-start | bytes 786440 | tf_op jit(solution)/shard_map/ppermute | solution.py:477
  106.9 27.4 %collective-permute-start.13 = (bf16[768,256]{1,0:T(8,128)(2,1)S(1)}, bf16[768,256]{1,0:T(8,128)(2,1)S(1)}, u32[]{:S(2)}, u32[]{:S(2)}) collective-permute-start(bf16[768,256]{1,0:T(8,128)(2,1)S(1)} %get-tuple-element.310), channel_id=1, source_target_pairs={{0,8},{4,12},{24,16},{28,20},{8,0},{12,4},{16,24},{20,28},{1,9},{5... | collective-permute-start | bytes 1179656 | tf_op jit(solution)/shard_map/ppermute | solution.py:476
  113.0 21.3 %collective-permute-start.12 = (bf16[512,256]{1,0:T(8,128)(2,1)S(1)}, bf16[512,256]{1,0:T(8,128)(2,1)S(1)}, u32[]{:S(2)}, u32[]{:S(2)}) collective-permute-start(bf16[512,256]{1,0:T(8,128)(2,1)S(1)} %get-tuple-element.309), channel_id=1, source_target_pairs={{0,4},{4,0},{8,12},{12,8},{16,20},{20,16},{24,28},{28,24},{1,5},{5... | collective-permute-start | bytes 786440 | tf_op jit(solution)/shard_map/ppermute | solution.py:475
  123.5 16.3 %collective-permute-start.24 = (bf16[768,256]{1,0:T(8,128)(2,1)S(1)}, bf16[768,256]{1,0:T(8,128)(2,1)S(1)}, u32[]{:S(2)}, u32[]{:S(2)}) collective-permute-start(bf16[768,256]{1,0:T(8,128)(2,1)S(1)} %get-tuple-element.335.refs_4_), channel_id=1, source_target_pairs={{8,16},{12,20},{16,8},{20,12},{0,0},{4,4},{24,24},{28,28},{9,17},{... | collective-permute-start | bytes 1179656 | tf_op jit(solution)/shard_map/ppermute | solution.py:477
  124.2 24.2 %collective-permute-start.23 = (bf16[1280,256]{1,0:T(8,128)(2,1)S(1)}, bf16[1280,256]{1,0:T(8,128)(2,1)S(1)}, u32[]{:S(2)}, u32[]{:S(2)}) collective-permute-start(bf16[1280,256]{1,0:T(8,128)(2,1)S(1)} %get-tuple-element.334.refs_3_), channel_id=1, source_target_pairs={{0,8},{4,12},{24,16},{28,20},{8,0},{12,4},{16,24},{20,28},{1,9},{5... | collective-permute-start | bytes 1966088 | tf_op jit(solution)/shard_map/ppermute | solution.py:476
  126.8 21.7 %collective-permute-start.22 = (bf16[768,256]{1,0:T(8,128)(2,1)S(1)}, bf16[768,256]{1,0:T(8,128)(2,1)S(1)}, u32[]{:S(2)}, u32[]{:S(2)}) collective-permute-start(bf16[768,256]{1,0:T(8,128)(2,1)S(1)} %get-tuple-element.333), channel_id=1, source_target_pairs={{0,4},{4,0},{8,12},{12,8},{16,20},{20,16},{24,28},{28,24},{1,5},{5... | collective-permute-start | bytes 1179656 | tf_op jit(solution)/shard_map/ppermute | solution.py:475
  136.1 17.0 %collective-permute-start.21 = (bf16[768,256]{1,0:T(8,128)(2,1)S(1)}, bf16[768,256]{1,0:T(8,128)(2,1)S(1)}, u32[]{:S(2)}, u32[]{:S(2)}) collective-permute-start(bf16[768,256]{1,0:T(8,128)(2,1)S(1)} %get-tuple-element.332.refs_4_), channel_id=1, source_target_pairs={{8,16},{12,20},{16,8},{20,12},{0,0},{4,4},{24,24},{28,28},{9,17},{... | collective-permute-start | bytes 1179656 | tf_op jit(solution)/shard_map/ppermute | solution.py:477
  137.3 26.4 %collective-permute-start.20 = (bf16[1280,256]{1,0:T(8,128)(2,1)S(1)}, bf16[1280,256]{1,0:T(8,128)(2,1)S(1)}, u32[]{:S(2)}, u32[]{:S(2)}) collective-permute-start(bf16[1280,256]{1,0:T(8,128)(2,1)S(1)} %get-tuple-element.331.refs_3_), channel_id=1, source_target_pairs={{0,8},{4,12},{24,16},{28,20},{8,0},{12,4},{16,24},{20,28},{1,9},{5... | collective-permute-start | bytes 1966088 | tf_op jit(solution)/shard_map/ppermute | solution.py:476
  139.8 23.9 %collective-permute-start.19 = (bf16[768,256]{1,0:T(8,128)(2,1)S(1)}, bf16[768,256]{1,0:T(8,128)(2,1)S(1)}, u32[]{:S(2)}, u32[]{:S(2)}) collective-permute-start(bf16[768,256]{1,0:T(8,128)(2,1)S(1)} %get-tuple-element.330), channel_id=1, source_target_pairs={{0,4},{4,0},{8,12},{12,8},{16,20},{20,16},{24,28},{28,24},{1,5},{5... | collective-permute-start | bytes 1179656 | tf_op jit(solution)/shard_map/ppermute | solution.py:475
  151.9 19.2 %collective-permute-start.25 = (bf16[1024,256]{1,0:T(8,128)(2,1)S(1)}, bf16[1024,256]{1,0:T(8,128)(2,1)S(1)}, u32[]{:S(2)}, u32[]{:S(2)}) collective-permute-start(bf16[1024,256]{1,0:T(8,128)(2,1)S(1)} %get-tuple-element.351.refs_4_), channel_id=1, source_target_pairs={{8,16},{12,20},{16,8},{20,12},{0,0},{4,4},{24,24},{28,28},{9,17},{... | collective-permute-start | bytes 1572872 | tf_op jit(solution)/shard_map/ppermute | solution.py:477
  152.6 19.3 %collective-permute-start.26 = (bf16[1024,256]{1,0:T(8,128)(2,1)S(1)}, bf16[1024,256]{1,0:T(8,128)(2,1)S(1)}, u32[]{:S(2)}, u32[]{:S(2)}) collective-permute-start(bf16[1024,256]{1,0:T(8,128)(2,1)S(1)} %get-tuple-element.352.refs_1_), channel_id=1, source_target_pairs={{0,4},{4,0},{8,12},{12,8},{16,20},{20,16},{24,28},{28,24},{1,5},{5... | collective-permute-start | bytes 1572872 | tf_op jit(solution)/shard_map/ppermute | solution.py:475
  186.4 37.0 %collective-permute-start.27 = (f32[512,1024]{1,0:T(8,128)S(1)}, f32[512,1024]{1,0:T(8,128)S(1)}, u32[]{:S(2)}, u32[]{:S(2)}) collective-permute-start(f32[512,1024]{1,0:T(8,128)S(1)} %get-tuple-element.354), channel_id=1, source_target_pairs={{0,1},{1,0},{2,3},{3,2},{4,5},{5,4},{6,7},{7,6},{8,9},{9,8},{10,11... | collective-permute-start | bytes 6291464 | tf_op jit(solution)/shard_map/ppermute | solution.py:429
  186.5 21.4 %collective-permute-start.28 = (bf16[1536,256]{1,0:T(8,128)(2,1)}, bf16[1536,256]{1,0:T(8,128)(2,1)S(1)}, u32[]{:S(2)}, u32[]{:S(2)}) collective-permute-start(bf16[1536,256]{1,0:T(8,128)(2,1)} %copy-done.16), channel_id=1, source_target_pairs={{0,8},{4,12},{24,16},{28,20},{8,0},{12,4},{16,24},{20,28},{1,9},{5... | collective-permute-start | bytes 2359304 | tf_op jit(solution)/shard_map/ppermute | solution.py:476
  189.2 31.8 %collective-permute-start.29 = (bf16[1024,256]{1,0:T(8,128)(2,1)}, bf16[1024,256]{1,0:T(8,128)(2,1)S(1)}, u32[]{:S(2)}, u32[]{:S(2)}) collective-permute-start(bf16[1024,256]{1,0:T(8,128)(2,1)} %copy-done.22), channel_id=1, source_target_pairs={{8,16},{12,20},{16,8},{20,12},{0,0},{4,4},{24,24},{28,28},{9,17},{... | collective-permute-start | bytes 1572872 | tf_op jit(solution)/shard_map/ppermute | solution.py:477
  190.9 31.7 %collective-permute-start.30 = (bf16[1024,256]{1,0:T(8,128)(2,1)}, bf16[1024,256]{1,0:T(8,128)(2,1)S(1)}, u32[]{:S(2)}, u32[]{:S(2)}) collective-permute-start(bf16[1024,256]{1,0:T(8,128)(2,1)} %copy-done.18), channel_id=1, source_target_pairs={{0,4},{4,0},{8,12},{12,8},{16,20},{20,16},{24,28},{28,24},{1,5},{5... | collective-permute-start | bytes 1572872 | tf_op jit(solution)/shard_map/ppermute | solution.py:475
  192.5 43.0 %collective-permute-start.32 = (bf16[1536,256]{1,0:T(8,128)(2,1)}, bf16[1536,256]{1,0:T(8,128)(2,1)S(1)}, u32[]{:S(2)}, u32[]{:S(2)}) collective-permute-start(bf16[1536,256]{1,0:T(8,128)(2,1)} %copy-done.14), channel_id=1, source_target_pairs={{0,8},{4,12},{24,16},{28,20},{8,0},{12,4},{16,24},{20,28},{1,9},{5... | collective-permute-start | bytes 2359304 | tf_op jit(solution)/shard_map/ppermute | solution.py:476
  218.8 25.7 %collective-permute-start.37 = (bf16[1536,256]{1,0:T(8,128)(2,1)S(1)}, bf16[1536,256]{1,0:T(8,128)(2,1)S(1)}, u32[]{:S(2)}, u32[]{:S(2)}) collective-permute-start(bf16[1536,256]{1,0:T(8,128)(2,1)S(1)} %get-tuple-element.378.refs_3_), channel_id=1, source_target_pairs={{0,8},{4,12},{24,16},{28,20},{8,0},{12,4},{16,24},{20,28},{1,9},{5... | collective-permute-start | bytes 2359304 | tf_op jit(solution)/shard_map/ppermute | solution.py:476
  221.1 18.6 %collective-permute-start.36 = (bf16[1280,256]{1,0:T(8,128)(2,1)S(1)}, bf16[1280,256]{1,0:T(8,128)(2,1)S(1)}, u32[]{:S(2)}, u32[]{:S(2)}) collective-permute-start(bf16[1280,256]{1,0:T(8,128)(2,1)S(1)} %get-tuple-element.377.refs_1_), channel_id=1, source_target_pairs={{0,4},{4,0},{8,12},{12,8},{16,20},{20,16},{24,28},{28,24},{1,5},{5... | collective-permute-start | bytes 1966088 | tf_op jit(solution)/shard_map/ppermute | solution.py:475
  222.7 21.9 %collective-permute-start.38 = (bf16[1280,256]{1,0:T(8,128)(2,1)S(1)}, bf16[1280,256]{1,0:T(8,128)(2,1)S(1)}, u32[]{:S(2)}, u32[]{:S(2)}) collective-permute-start(bf16[1280,256]{1,0:T(8,128)(2,1)S(1)} %get-tuple-element.379.refs_4_), channel_id=1, source_target_pairs={{8,16},{12,20},{16,8},{20,12},{0,0},{4,4},{24,24},{28,28},{9,17},{... | collective-permute-start | bytes 1966088 | tf_op jit(solution)/shard_map/ppermute | solution.py:477
  239.7 26.5 %collective-permute-start.34 = (bf16[1536,256]{1,0:T(8,128)(2,1)S(1)}, bf16[1536,256]{1,0:T(8,128)(2,1)S(1)}, u32[]{:S(2)}, u32[]{:S(2)}) collective-permute-start(bf16[1536,256]{1,0:T(8,128)(2,1)S(1)} %get-tuple-element.375.refs_3_), channel_id=1, source_target_pairs={{0,8},{4,12},{24,16},{28,20},{8,0},{12,4},{16,24},{20,28},{1,9},{5... | collective-permute-start | bytes 2359304 | tf_op jit(solution)/shard_map/ppermute | solution.py:476
  247.3 24.1 %collective-permute-start.39 = (bf16[1536,256]{1,0:T(8,128)(2,1)S(1)}, bf16[1536,256]{1,0:T(8,128)(2,1)S(1)}, u32[]{:S(2)}, u32[]{:S(2)}) collective-permute-start(bf16[1536,256]{1,0:T(8,128)(2,1)S(1)} %get-tuple-element.393.refs_4_), channel_id=1, source_target_pairs={{8,16},{12,20},{16,8},{20,12},{0,0},{4,4},{24,24},{28,28},{9,17},{... | collective-permute-start | bytes 2359304 | tf_op jit(solution)/shard_map/ppermute | solution.py:477
  248.1 32.7 %collective-permute-start.41 = (bf16[1536,256]{1,0:T(8,128)(2,1)S(1)}, bf16[1536,256]{1,0:T(8,128)(2,1)S(1)}, u32[]{:S(2)}, u32[]{:S(2)}) collective-permute-start(bf16[1536,256]{1,0:T(8,128)(2,1)S(1)} %get-tuple-element.395.refs_3_), channel_id=1, source_target_pairs={{0,8},{4,12},{24,16},{28,20},{8,0},{12,4},{16,24},{20,28},{1,9},{5... | collective-permute-start | bytes 2359304 | tf_op jit(solution)/shard_map/ppermute | solution.py:476
  253.7 17.1 %collective-permute-start.40 = (bf16[1280,256]{1,0:T(8,128)(2,1)S(1)}, bf16[1280,256]{1,0:T(8,128)(2,1)S(1)}, u32[]{:S(2)}, u32[]{:S(2)}) collective-permute-start(bf16[1280,256]{1,0:T(8,128)(2,1)S(1)} %get-tuple-element.394.refs_1_), channel_id=1, source_target_pairs={{0,4},{4,0},{8,12},{12,8},{16,20},{20,16},{24,28},{28,24},{1,5},{5... | collective-permute-start | bytes 1966088 | tf_op jit(solution)/shard_map/ppermute | solution.py:475
  254.1 26.6 %collective-permute-start.31 = (f32[256,1024]{1,0:T(8,128)S(1)}, f32[256,1024]{1,0:T(8,128)S(1)}, u32[]{:S(2)}, u32[]{:S(2)}) collective-permute-start(f32[256,1024]{1,0:T(8,128)S(1)} %get-tuple-element.365), channel_id=1, source_target_pairs={{0,2},{1,3},{2,0},{3,1},{4,6},{5,7},{6,4},{7,5},{8,10},{9,11},{10,... | collective-permute-start | bytes 3145736 | tf_op jit(solution)/shard_map/ppermute | solution.py:429
  270.7 20.9 %collective-permute-start.47 = (bf16[1536,256]{1,0:T(8,128)(2,1)S(1)}, bf16[1536,256]{1,0:T(8,128)(2,1)S(1)}, u32[]{:S(2)}, u32[]{:S(2)}) collective-permute-start(bf16[1536,256]{1,0:T(8,128)(2,1)S(1)} %get-tuple-element.399.refs_4_), channel_id=1, source_target_pairs={{8,16},{12,20},{16,8},{20,12},{0,0},{4,4},{24,24},{28,28},{9,17},{... | collective-permute-start | bytes 2359304 | tf_op jit(solution)/shard_map/ppermute | solution.py:477
  271.4 23.5 %collective-permute-start.46 = (bf16[1536,256]{1,0:T(8,128)(2,1)S(1)}, bf16[1536,256]{1,0:T(8,128)(2,1)S(1)}, u32[]{:S(2)}, u32[]{:S(2)}) collective-permute-start(bf16[1536,256]{1,0:T(8,128)(2,1)S(1)} %get-tuple-element.398.refs_3_), channel_id=1, source_target_pairs={{0,8},{4,12},{24,16},{28,20},{8,0},{12,4},{16,24},{20,28},{1,9},{5... | collective-permute-start | bytes 2359304 | tf_op jit(solution)/shard_map/ppermute | solution.py:476
  282.2 19.8 %collective-permute-start.42 = (bf16[256,1024]{1,0:T(8,128)(2,1)S(1)}, bf16[256,1024]{1,0:T(8,128)(2,1)S(1)}, u32[]{:S(2)}, u32[]{:S(2)}) collective-permute-start(bf16[256,1024]{1,0:T(8,128)(2,1)S(1)} %get-tuple-element.396.refs_0_), channel_id=1, source_target_pairs={{0,1},{1,0},{2,3},{3,2},{4,5},{5,4},{6,7},{7,6},{8,9},{9,8},{10,11... | collective-permute-start | bytes 1572872 | tf_op jit(solution)/shard_map/ppermute | solution.py:429
  285.2 17.6 %collective-permute-start.48 = (bf16[1536,256]{1,0:T(8,128)(2,1)S(1)}, bf16[1536,256]{1,0:T(8,128)(2,1)S(1)}, u32[]{:S(2)}, u32[]{:S(2)}) collective-permute-start(bf16[1536,256]{1,0:T(8,128)(2,1)S(1)} %get-tuple-element.413.refs_4_), channel_id=1, source_target_pairs={{8,16},{12,20},{16,8},{20,12},{0,0},{4,4},{24,24},{28,28},{9,17},{... | collective-permute-start | bytes 2359304 | tf_op jit(solution)/shard_map/ppermute | solution.py:477
  290.9 26.3 %collective-permute-start.52 = (bf16[1536,256]{1,0:T(8,128)(2,1)S(1)}, bf16[1536,256]{1,0:T(8,128)(2,1)S(1)}, u32[]{:S(2)}, u32[]{:S(2)}) collective-permute-start(bf16[1536,256]{1,0:T(8,128)(2,1)S(1)} %get-tuple-element.418.refs_3_), channel_id=1, source_target_pairs={{0,4},{4,0},{8,12},{12,8},{16,20},{20,16},{24,28},{28,24},{1,5},{5... | collective-permute-start | bytes 2359304 | tf_op jit(solution)/shard_map/ppermute | solution.py:475
  291.6 25.6 %collective-permute-start.53 = (bf16[1536,256]{1,0:T(8,128)(2,1)S(1)}, bf16[1536,256]{1,0:T(8,128)(2,1)S(1)}, u32[]{:S(2)}, u32[]{:S(2)}) collective-permute-start(bf16[1536,256]{1,0:T(8,128)(2,1)S(1)} %get-tuple-element.420.refs_3_), channel_id=1, source_target_pairs={{0,8},{4,12},{24,16},{28,20},{8,0},{12,4},{16,24},{20,28},{1,9},{5... | collective-permute-start | bytes 2359304 | tf_op jit(solution)/shard_map/ppermute | solution.py:476
  302.0 21.5 %collective-permute-start.51 = (bf16[1536,256]{1,0:T(8,128)(2,1)S(1)}, bf16[1536,256]{1,0:T(8,128)(2,1)S(1)}, u32[]{:S(2)}, u32[]{:S(2)}) collective-permute-start(bf16[1536,256]{1,0:T(8,128)(2,1)S(1)} %get-tuple-element.417.refs_4_), channel_id=1, source_target_pairs={{8,16},{12,20},{16,8},{20,12},{0,0},{4,4},{24,24},{28,28},{9,17},{... | collective-permute-start | bytes 2359304 | tf_op jit(solution)/shard_map/ppermute | solution.py:477
  302.8 30.1 %collective-permute-start.50 = (bf16[1536,256]{1,0:T(8,128)(2,1)S(1)}, bf16[1536,256]{1,0:T(8,128)(2,1)S(1)}, u32[]{:S(2)}, u32[]{:S(2)}) collective-permute-start(bf16[1536,256]{1,0:T(8,128)(2,1)S(1)} %get-tuple-element.416.refs_3_), channel_id=1, source_target_pairs={{0,8},{4,12},{24,16},{28,20},{8,0},{12,4},{16,24},{20,28},{1,9},{5... | collective-permute-start | bytes 2359304 | tf_op jit(solution)/shard_map/ppermute | solution.py:476
  310.9 22.0 %collective-permute-start.49 = (bf16[1280,256]{1,0:T(8,128)(2,1)S(1)}, bf16[1280,256]{1,0:T(8,128)(2,1)S(1)}, u32[]{:S(2)}, u32[]{:S(2)}) collective-permute-start(bf16[1280,256]{1,0:T(8,128)(2,1)S(1)} %get-tuple-element.415.refs_3_), channel_id=1, source_target_pairs={{0,4},{4,0},{8,12},{12,8},{16,20},{20,16},{24,28},{28,24},{1,5},{5... | collective-permute-start | bytes 1966088 | tf_op jit(solution)/shard_map/ppermute | solution.py:475
  320.0 22.1 %collective-permute-start.57 = (bf16[1536,256]{1,0:T(8,128)(2,1)S(1)}, bf16[1536,256]{1,0:T(8,128)(2,1)S(1)}, u32[]{:S(2)}, u32[]{:S(2)}) collective-permute-start(bf16[1536,256]{1,0:T(8,128)(2,1)S(1)} %get-tuple-element.449.refs_4_), channel_id=1, source_target_pairs={{8,16},{12,20},{16,8},{20,12},{0,0},{4,4},{24,24},{28,28},{9,17},{... | collective-permute-start | bytes 2359304 | tf_op jit(solution)/shard_map/ppermute | solution.py:477
  321.0 29.4 %collective-permute-start.59 = (bf16[1536,256]{1,0:T(8,128)(2,1)S(1)}, bf16[1536,256]{1,0:T(8,128)(2,1)S(1)}, u32[]{:S(2)}, u32[]{:S(2)}) collective-permute-start(bf16[1536,256]{1,0:T(8,128)(2,1)S(1)} %get-tuple-element.452.refs_3_), channel_id=1, source_target_pairs={{0,8},{4,12},{24,16},{28,20},{8,0},{12,4},{16,24},{20,28},{1,9},{5... | collective-permute-start | bytes 2359304 | tf_op jit(solution)/shard_map/ppermute | solution.py:476
  323.5 26.9 %collective-permute-start.58 = (bf16[1280,256]{1,0:T(8,128)(2,1)S(1)}, bf16[1280,256]{1,0:T(8,128)(2,1)S(1)}, u32[]{:S(2)}, u32[]{:S(2)}) collective-permute-start(bf16[1280,256]{1,0:T(8,128)(2,1)S(1)} %get-tuple-element.451.refs_3_), channel_id=1, source_target_pairs={{0,4},{4,0},{8,12},{12,8},{16,20},{20,16},{24,28},{28,24},{1,5},{5... | collective-permute-start | bytes 1966088 | tf_op jit(solution)/shard_map/ppermute | solution.py:475
  335.3 21.5 %collective-permute-start.56 = (bf16[1280,256]{1,0:T(8,128)(2,1)S(1)}, bf16[1280,256]{1,0:T(8,128)(2,1)S(1)}, u32[]{:S(2)}, u32[]{:S(2)}) collective-permute-start(bf16[1280,256]{1,0:T(8,128)(2,1)S(1)} %get-tuple-element.439.refs_4_), channel_id=1, source_target_pairs={{8,16},{12,20},{16,8},{20,12},{0,0},{4,4},{24,24},{28,28},{9,17},{... | collective-permute-start | bytes 1966088 | tf_op jit(solution)/shard_map/ppermute | solution.py:477
  336.0 27.0 %collective-permute-start.55 = (bf16[1536,256]{1,0:T(8,128)(2,1)S(1)}, bf16[1536,256]{1,0:T(8,128)(2,1)S(1)}, u32[]{:S(2)}, u32[]{:S(2)}) collective-permute-start(bf16[1536,256]{1,0:T(8,128)(2,1)S(1)} %get-tuple-element.438.refs_3_), channel_id=1, source_target_pairs={{0,8},{4,12},{24,16},{28,20},{8,0},{12,4},{16,24},{20,28},{1,9},{5... | collective-permute-start | bytes 2359304 | tf_op jit(solution)/shard_map/ppermute | solution.py:476
  342.2 18.6 %collective-permute-start.54 = (bf16[1280,256]{1,0:T(8,128)(2,1)S(1)}, bf16[1280,256]{1,0:T(8,128)(2,1)S(1)}, u32[]{:S(2)}, u32[]{:S(2)}) collective-permute-start(bf16[1280,256]{1,0:T(8,128)(2,1)S(1)} %get-tuple-element.437.refs_1_.refs_3_), channel_id=1, source_target_pairs={{0,4},{4,0},{8,12},{12,8},{16,20},{20,16},{24,28},{28,24},{1,5},{5... | collective-permute-start | bytes 1966088 | tf_op jit(solution)/shard_map/ppermute | solution.py:475
  352.9 27.0 %collective-permute-start.65 = (bf16[1536,256]{1,0:T(8,128)(2,1)S(1)}, bf16[1536,256]{1,0:T(8,128)(2,1)S(1)}, u32[]{:S(2)}, u32[]{:S(2)}) collective-permute-start(bf16[1536,256]{1,0:T(8,128)(2,1)S(1)} %get-tuple-element.477.refs_3_), channel_id=1, source_target_pairs={{0,8},{4,12},{24,16},{28,20},{8,0},{12,4},{16,24},{20,28},{1,9},{5... | collective-permute-start | bytes 2359304 | tf_op jit(solution)/shard_map/ppermute | solution.py:476
  356.8 16.7 %collective-permute-start.64 = (bf16[1280,256]{1,0:T(8,128)(2,1)S(1)}, bf16[1280,256]{1,0:T(8,128)(2,1)S(1)}, u32[]{:S(2)}, u32[]{:S(2)}) collective-permute-start(bf16[1280,256]{1,0:T(8,128)(2,1)S(1)} %get-tuple-element.476.refs_1_.refs_3_), channel_id=1, source_target_pairs={{0,4},{4,0},{8,12},{12,8},{16,20},{20,16},{24,28},{28,24},{1,5},{5... | collective-permute-start | bytes 1966088 | tf_op jit(solution)/shard_map/ppermute | solution.py:475
  365.2 20.6 %collective-permute-start.62 = (bf16[1024,256]{1,0:T(8,128)(2,1)S(1)}, bf16[1024,256]{1,0:T(8,128)(2,1)S(1)}, u32[]{:S(2)}, u32[]{:S(2)}) collective-permute-start(bf16[1024,256]{1,0:T(8,128)(2,1)S(1)} %get-tuple-element.464.refs_4_), channel_id=1, source_target_pairs={{8,16},{12,20},{16,8},{20,12},{0,0},{4,4},{24,24},{28,28},{9,17},{... | collective-permute-start | bytes 1572872 | tf_op jit(solution)/shard_map/ppermute | solution.py:477
  365.9 31.5 %collective-permute-start.61 = (bf16[1536,256]{1,0:T(8,128)(2,1)S(1)}, bf16[1536,256]{1,0:T(8,128)(2,1)S(1)}, u32[]{:S(2)}, u32[]{:S(2)}) collective-permute-start(bf16[1536,256]{1,0:T(8,128)(2,1)S(1)} %get-tuple-element.463.refs_3_), channel_id=1, source_target_pairs={{0,8},{4,12},{24,16},{28,20},{8,0},{12,4},{16,24},{20,28},{1,9},{5... | collective-permute-start | bytes 2359304 | tf_op jit(solution)/shard_map/ppermute | solution.py:476
  382.0 31.6 %collective-permute-start.71 = (bf16[1536,256]{1,0:T(8,128)(2,1)S(1)}, bf16[1536,256]{1,0:T(8,128)(2,1)S(1)}, u32[]{:S(2)}, u32[]{:S(2)}) collective-permute-start(bf16[1536,256]{1,0:T(8,128)(2,1)S(1)} %get-tuple-element.497.refs_3_), channel_id=1, source_target_pairs={{0,8},{4,12},{24,16},{28,20},{8,0},{12,4},{16,24},{20,28},{1,9},{5... | collective-permute-start | bytes 2359304 | tf_op jit(solution)/shard_map/ppermute | solution.py:476
  384.3 17.2 %collective-permute-start.69 = (bf16[1024,256]{1,0:T(8,128)(2,1)S(1)}, bf16[1024,256]{1,0:T(8,128)(2,1)S(1)}, u32[]{:S(2)}, u32[]{:S(2)}) collective-permute-start(bf16[1024,256]{1,0:T(8,128)(2,1)S(1)} %get-tuple-element.494.refs_4_), channel_id=1, source_target_pairs={{8,16},{12,20},{16,8},{20,12},{0,0},{4,4},{24,24},{28,28},{9,17},{... | collective-permute-start | bytes 1572872 | tf_op jit(solution)/shard_map/ppermute | solution.py:477
  385.8 18.9 %collective-permute-start.70 = (bf16[768,256]{1,0:T(8,128)(2,1)S(1)}, bf16[768,256]{1,0:T(8,128)(2,1)S(1)}, u32[]{:S(2)}, u32[]{:S(2)}) collective-permute-start(bf16[768,256]{1,0:T(8,128)(2,1)S(1)} %get-tuple-element.496.refs_1_.refs_3_), channel_id=1, source_target_pairs={{0,4},{4,0},{8,12},{12,8},{16,20},{20,16},{24,28},{28,24},{1,5},{5... | collective-permute-start | bytes 1179656 | tf_op jit(solution)/shard_map/ppermute | solution.py:475
  399.1 31.2 %collective-permute-start.67 = (bf16[1280,256]{1,0:T(8,128)(2,1)S(1)}, bf16[1280,256]{1,0:T(8,128)(2,1)S(1)}, u32[]{:S(2)}, u32[]{:S(2)}) collective-permute-start(bf16[1280,256]{1,0:T(8,128)(2,1)S(1)} %get-tuple-element.486.refs_3_), channel_id=1, source_target_pairs={{0,8},{4,12},{24,16},{28,20},{8,0},{12,4},{16,24},{20,28},{1,9},{5... | collective-permute-start | bytes 1966088 | tf_op jit(solution)/shard_map/ppermute | solution.py:476
  415.3 26.4 %collective-permute-start.77 = (bf16[1280,256]{1,0:T(8,128)(2,1)S(1)}, bf16[1280,256]{1,0:T(8,128)(2,1)S(1)}, u32[]{:S(2)}, u32[]{:S(2)}) collective-permute-start(bf16[1280,256]{1,0:T(8,128)(2,1)S(1)} %get-tuple-element.515.refs_3_), channel_id=1, source_target_pairs={{0,8},{4,12},{24,16},{28,20},{8,0},{12,4},{16,24},{20,28},{1,9},{5... | collective-permute-start | bytes 1966088 | tf_op jit(solution)/shard_map/ppermute | solution.py:476
  418.7 18.4 %collective-permute-start.76 = (bf16[768,256]{1,0:T(8,128)(2,1)S(1)}, bf16[768,256]{1,0:T(8,128)(2,1)S(1)}, u32[]{:S(2)}, u32[]{:S(2)}) collective-permute-start(bf16[768,256]{1,0:T(8,128)(2,1)S(1)} %get-tuple-element.514.refs_1_.refs_3_), channel_id=1, source_target_pairs={{0,4},{4,0},{8,12},{12,8},{16,20},{20,16},{24,28},{28,24},{1,5},{5... | collective-permute-start | bytes 1179656 | tf_op jit(solution)/shard_map/ppermute | solution.py:475
  431.6 20.4 %collective-permute-start.73 = (bf16[768,256]{1,0:T(8,128)(2,1)S(1)}, bf16[768,256]{1,0:T(8,128)(2,1)S(1)}, u32[]{:S(2)}, u32[]{:S(2)}) collective-permute-start(bf16[768,256]{1,0:T(8,128)(2,1)S(1)} %get-tuple-element.506.refs_3_), channel_id=1, source_target_pairs={{0,8},{4,12},{24,16},{28,20},{8,0},{12,4},{16,24},{20,28},{1,9},{5... | collective-permute-start | bytes 1179656 | tf_op jit(solution)/shard_map/ppermute | solution.py:476
  443.0 19.5 %collective-permute-start.80 = (bf16[768,256]{1,0:T(8,128)(2,1)S(1)}, bf16[768,256]{1,0:T(8,128)(2,1)S(1)}, u32[]{:S(2)}, u32[]{:S(2)}) collective-permute-start(bf16[768,256]{1,0:T(8,128)(2,1)S(1)} %get-tuple-element.523.refs_3_), channel_id=1, source_target_pairs={{0,8},{4,12},{24,16},{28,20},{8,0},{12,4},{16,24},{20,28},{1,9},{5... | collective-permute-start | bytes 1179656 | tf_op jit(solution)/shard_map/ppermute | solution.py:476
  446.3 16.2 %collective-permute-start.79 = (bf16[256,256]{1,0:T(8,128)(2,1)S(1)}, bf16[256,256]{1,0:T(8,128)(2,1)S(1)}, u32[]{:S(2)}, u32[]{:S(2)}) collective-permute-start(bf16[256,256]{1,0:T(8,128)(2,1)S(1)} %get-tuple-element.522.refs_3_), channel_id=1, source_target_pairs={{0,4},{4,0},{8,12},{12,8},{16,20},{20,16},{24,28},{28,24},{1,5},{5... | collective-permute-start | bytes 393224 | tf_op jit(solution)/shard_map/ppermute | solution.py:475
  (67 other events, 885.2 us)
Sparse Core Ops, SparseCore 0:
  9.5 109.3 all-gather.1

commit v3 on v2

--- a/solution.py
+++ b/solution.py
@@ -6,7 +6,7 @@
 from jax.sharding import PartitionSpec as P
 
 SEQ_LEN = 256
-EXTRA = {0: 1, 1: 1, 2: 1, 3: 1, 4: 1, 9: 1, 10: 1, 11: 1, 12: 1, 13: 2, 14: 1}
+EXTRA = {0: 1, 1: 1, 2: 1, 3: 1, 4: 1}
 PARTS = 4
 WIDTH = 256
 BF16 = jnp.bfloat16
@@ -78,7 +78,7 @@
     units += [[(1, i), (1, i + 1)] for i in range(0, lead, 2)]
     rest = [(half, i) for i in range(lead, count) for half in (0, 1)]
     while rest:
-        size = 2 if len(rest) > 4 else 1
+        size = 2 if len(rest) > 8 else 1
         units.append(rest[:size])
         rest = rest[size:]
     return units

time: 496 us -> 488 us (0.984)
  waiting for transfers between devices: 94.2 us -> 67.6 us
  starting transfers between devices: 146 us -> 161 us
  Pallas kernels: 207 us -> 215 us
    ppermute x27 -> x29, waiting for transfers between devices: 71.2 us -> 48.5 us  [pipelined(): lax.ppermute(v, 'feat', inward[0] + outward[0])]
    ppermute x27 -> x29, starting transfers between devices: 93.6 us -> 105 us  [pipelined(): lax.ppermute(v, 'feat', inward[0] + outward[0])]
    pallas_call x65 -> x69, Pallas kernels: 207 us -> 215 us  [call(): pl.pallas_call(kernel, grid_spec=pltpu.PrefetchScalarGridSpec(num_scalar_...]
    ppermute x8, waiting for transfers between devices: 5.99 us -> 1 us  [swap_ex(): return lax.ppermute(value, 'ex', [(i, i ^ bit) for i in range(ex)])]
    unnamed x90 -> x86, local copies, waits for them, and re-layouts: 25 us -> 21.2 us
    ppermute x23 -> x25, starting transfers between devices: 18.2 us -> 19.6 us  [pipelined(): lax.ppermute(v, 'feat', middle + stay)]
    ppermute x27 -> x29, waiting for transfers between devices: 16.2 us -> 17.4 us  [pipelined(): lax.ppermute(v, 'feat', y_swap)]
    ppermute x27 -> x29, starting transfers between devices: 29.3 us -> 29.8 us  [pipelined(): lax.ppermute(v, 'feat', y_swap)]
  transfers between devices with their start and end apart: 86 -> 92, of which waited for: 15 -> 15; matrix products, arithmetic and copies ran while one was open for 0% -> 0% of each run, Pallas kernels for 40% -> 43%
where the time goes in v3:
time: 488 us; the launch traced here: 479 us
  Pallas kernels  215 us (44%)
  starting transfers between devices  161 us (33%)
  waiting for transfers between devices  67.6 us (14%)
  local copies, waits for them, and re-layouts  21.2 us (4%)
  between operations  15.2 us (3%)
    pallas_call x69, Pallas kernels, call(): pl.pallas_call(kernel, grid_spec=pltpu.PrefetchScalarGridSpec(num_scalar_...  215 us
    ppermute x29, starting transfers between devices, pipelined(): lax.ppermute(v, 'feat', inward[0] + outward[0])  105 us
    ppermute x29, waiting for transfers between devices, pipelined(): lax.ppermute(v, 'feat', inward[0] + outward[0])  48.5 us
    ppermute x29, starting transfers between devices, pipelined(): lax.ppermute(v, 'feat', y_swap)  29.8 us
    unnamed x86, local copies, waits for them, and re-layouts  21.2 us
    ppermute x25, starting transfers between devices, pipelined(): lax.ppermute(v, 'feat', middle + stay)  19.6 us
    ppermute x29, waiting for transfers between devices, pipelined(): lax.ppermute(v, 'feat', y_swap)  17.4 us
  transfers between devices with their start and end apart: 92, of which 15 were waited for; matrix products, arithmetic and copies ran while one was open for 0% of the time, Pallas kernels for 43%

profile of v3, /device:TPU:0, one launch (start us, length us, event | category | flops | bytes accessed | tf_op | source)
XLA Modules:
  0.0 479.4 jit_solution(17355129242733216273)
XLA Ops:
  13.6 4.3 shard_map.46
  18.7 3.0 collective-permute-start.4
  23.2 4.3 shard_map.48
  29.1 4.3 shard_map.50
  33.4 6.6 %collective-permute-done.4.refs_1_ = bf16[512,256]{1,0:T(8,128)(2,1)S(1)} collective-permute-done((bf16[512,256]{1,0:T(8,128)(2,1)S(1)}, bf16[512,256]{1,0:T(8,128)(2,1)S(1)}, u32[]{:S(2)}, u32[]{:S(2)}) %collective-permute-start.4) | collective-permute-done | bytes 262176 | tf_op jit(solution)/shard_map/ppermute | solution.py:476
  43.6 4.3 shard_map.52
  57.5 4.5 collective-permute-start.6
  62.0 4.3 shard_map.55
  66.3 16.0 %collective-permute-done.9.refs_1_ = bf16[768,256]{1,0:T(8,128)(2,1)S(1)} collective-permute-done((bf16[768,256]{1,0:T(8,128)(2,1)S(1)}, bf16[768,256]{1,0:T(8,128)(2,1)S(1)}, u32[]{:S(2)}, u32[]{:S(2)}) %collective-permute-start.9) | collective-permute-done | bytes 393248 | tf_op jit(solution)/shard_map/ppermute | solution.py:476
  84.4 5.6 %collective-permute-start.17 = (bf16[768,256]{1,0:T(8,128)(2,1)S(1)}, bf16[768,256]{1,0:T(8,128)(2,1)S(1)}, u32[]{:S(2)}, u32[]{:S(2)}) collective-permute-start(bf16[768,256]{1,0:T(8,128)(2,1)S(1)} %get-tuple-element.338), channel_id=1, source_target_pairs={{0,8},{4,12},{24,16},{28,20},{8,0},{12,4},{16,24},{20,28},{1,9},{5... | collective-permute-start | bytes 1179656 | tf_op jit(solution)/shard_map/ppermute | solution.py:476
  91.6 4.3 shard_map.57
  96.0 8.9 %collective-permute-done.6.refs_1_ = bf16[768,256]{1,0:T(8,128)(2,1)S(1)} collective-permute-done((bf16[768,256]{1,0:T(8,128)(2,1)S(1)}, bf16[768,256]{1,0:T(8,128)(2,1)S(1)}, u32[]{:S(2)}, u32[]{:S(2)}) %collective-permute-start.6) | collective-permute-done | bytes 393248 | tf_op jit(solution)/shard_map/ppermute | solution.py:476
  106.9 6.1 %collective-permute-start.13 = (bf16[768,256]{1,0:T(8,128)(2,1)S(1)}, bf16[768,256]{1,0:T(8,128)(2,1)S(1)}, u32[]{:S(2)}, u32[]{:S(2)}) collective-permute-start(bf16[768,256]{1,0:T(8,128)(2,1)S(1)} %get-tuple-element.334), channel_id=1, source_target_pairs={{0,8},{4,12},{24,16},{28,20},{8,0},{12,4},{16,24},{20,28},{1,9},{5... | collective-permute-start | bytes 1179656 | tf_op jit(solution)/shard_map/ppermute | solution.py:476
  114.6 7.0 %shard_map.59 = (bf16[512,1024]{1,0:T(8,128)(2,1)S(1)}, f32[8,128]{1,0:T(8,128)S(1)}) custom-call(s32[4]{0:T(128)S(1)} %pad_add_fusion.flags, bf16[256,3584]{1,0:T(8,128)(2,1)S(1)} %get-tuple-element.336.refs_0_.refs_2_, bf16[256,3584]{1,0:T(8,128)(2,1)S(1)} %collective-permute-done.15.refs_1_.refs_3_, bf16[3584,7168]{1,0:T(8,128)(2,1)} %refs_2_.33, ...), custom_call_target="tpu_custom_call" | custom-call | flops 3758096384 | bytes 13107200 | tf_op jit(solution)/shard_map/pallas_call | solution.py:63
  127.2 7.1 %shard_map.61 = (bf16[512,1024]{1,0:T(8,128)(2,1)S(1)}, f32[8,128]{1,0:T(8,128)S(1)}) custom-call(s32[4]{0:T(128)S(1)} %pad_add_fusion.flags, bf16[256,3584]{1,0:T(8,128)(2,1)S(1)} %get-tuple-element.336.refs_0_.refs_2_, bf16[256,3584]{1,0:T(8,128)(2,1)S(1)} %collective-permute-done.15.refs_1_.refs_3_, bf16[3584,7168]{1,0:T(8,128)(2,1)} %refs_2_.33, ...), custom_call_target="tpu_custom_call" | custom-call | flops 3758096384 | bytes 13107200 | tf_op jit(solution)/shard_map/pallas_call | solution.py:63
  141.4 7.1 %shard_map.63 = (bf16[512,1024]{1,0:T(8,128)(2,1)S(1)}, f32[8,128]{1,0:T(8,128)S(1)}) custom-call(s32[4]{0:T(128)S(1)} %pad_add_fusion.flags, bf16[256,3584]{1,0:T(8,128)(2,1)S(1)} %get-tuple-element.336.refs_0_.refs_2_, bf16[256,3584]{1,0:T(8,128)(2,1)S(1)} %collective-permute-done.15.refs_1_.refs_3_, bf16[3584,7168]{1,0:T(8,128)(2,1)} %refs_2_.33, ...), custom_call_target="tpu_custom_call" | custom-call | flops 3758096384 | bytes 13107200 | tf_op jit(solution)/shard_map/pallas_call | solution.py:63
  151.8 10.5 %shard_map.65 = (bf16[1024,1024]{1,0:T(8,128)(2,1)S(1)}, f32[8,128]{1,0:T(8,128)S(1)}) custom-call(s32[4]{0:T(128)S(1)} %pad_add_fusion.flags, bf16[256,3584]{1,0:T(8,128)(2,1)S(1)} %copy-done.1, bf16[256,3584]{1,0:T(8,128)(2,1)S(1)} %copy-done.4, bf16[256,3584]{1,0:T(8,128)(2,1)S(1)} %get-tuple-element.336.refs_0_.refs_2_, ...), custom_call_target="tpu_custom_call" | custom-call | flops 7516192768 | bytes 18874368 | tf_op jit(solution)/shard_map/pallas_call | solution.py:63
  171.8 2.8 copy-done.41
  176.7 6.5 %shard_map.67 = (f32[512,1024]{1,0:T(8,128)S(1)}, f32[512,1024]{1,0:T(8,128)S(1)}, f32[8,128]{1,0:T(8,128)S(1)}) custom-call(s32[4]{0:T(128)S(1)} %pad_add_fusion.flags, bf16[1024,2048]{1,0:T(8,128)(2,1)S(1)} %copy-done.42, bf16[2048,1024]{1,0:T(8,128)(2,1)S(1)} %copy-done.41, f32[8,128]{1,0:T(8,128)S(1)} %get-tuple-element.374.refs_2_, ...), custom_call_target="tpu_custom_call" | custom-call | flops 4294967296 | bytes 12582912 | tf_op jit(solution)/shard_map/pallas_call | solution.py:63
  183.3 2.8 collective-permute-start.28
  189.5 10.8 %collective-permute-done.27.refs_0_.refs_2_ = bf16[1024,256]{1,0:T(8,128)(2,1)S(1)} collective-permute-done((bf16[1024,256]{1,0:T(8,128)(2,1)}, bf16[1024,256]{1,0:T(8,128)(2,1)S(1)}, u32[]{:S(2)}, u32[]{:S(2)}) %collective-permute-start.27) | collective-permute-done | bytes 524320 | tf_op jit(solution)/shard_map/ppermute | solution.py:475
  200.7 4.0 collective-permute-done.28.refs_1_
  211.9 2.8 shard_map.68
  219.4 10.7 %shard_map.70 = (bf16[1024,1024]{1,0:T(8,128)(2,1)S(1)}, f32[8,128]{1,0:T(8,128)S(1)}) custom-call(s32[4]{0:T(128)S(1)} %pad_add_fusion.flags, bf16[256,3584]{1,0:T(8,128)(2,1)S(1)} %copy-done.2, bf16[256,3584]{1,0:T(8,128)(2,1)S(1)} %copy-done.5, bf16[256,3584]{1,0:T(8,128)(2,1)S(1)} %copy-done.7, bf16[256,3584]{1,0:T(8,128)(2,1)S(1)} %copy-done.9, ...), custom_call_target="tpu_custom_call" | custom-call | flops 7516192768 | bytes 18874368 | tf_op jit(solution)/shard_map/pallas_call | solution.py:63
  230.2 2.8 shard_map.71
  237.1 4.7 collective-permute-start.34
  241.8 2.9 shard_map.72
  245.9 5.7 %collective-permute-done.33.refs_0_.refs_2_ = bf16[1280,256]{1,0:T(8,128)(2,1)S(1)} collective-permute-done((bf16[1280,256]{1,0:T(8,128)(2,1)S(1)}, bf16[1280,256]{1,0:T(8,128)(2,1)S(1)}, u32[]{:S(2)}, u32[]{:S(2)}) %collective-permute-start.33) | collective-permute-done | bytes 655392 | tf_op jit(solution)/shard_map/ppermute | solution.py:475
  251.6 5.0 %collective-permute-start.47 = (bf16[1536,256]{1,0:T(8,128)(2,1)S(1)}, bf16[1536,256]{1,0:T(8,128)(2,1)S(1)}, u32[]{:S(2)}, u32[]{:S(2)}) collective-permute-start(bf16[1536,256]{1,0:T(8,128)(2,1)S(1)} %get-tuple-element.423.refs_3_), channel_id=1, source_target_pairs={{0,8},{4,12},{24,16},{28,20},{8,0},{12,4},{16,24},{20,28},{1,9},{5... | collective-permute-start | bytes 2359304 | tf_op jit(solution)/shard_map/ppermute | solution.py:476
  256.6 4.3 shard_map.73
  264.8 8.7 %collective-permute-start.44 = (bf16[1024,256]{1,0:T(8,128)(2,1)S(1)}, bf16[1024,256]{1,0:T(8,128)(2,1)S(1)}, u32[]{:S(2)}, u32[]{:S(2)}) collective-permute-start(bf16[1024,256]{1,0:T(8,128)(2,1)S(1)} %get-tuple-element.420.refs_3_), channel_id=1, source_target_pairs={{0,8},{4,12},{24,16},{28,20},{8,0},{12,4},{16,24},{20,28},{1,9},{5... | collective-permute-start | bytes 1572872 | tf_op jit(solution)/shard_map/ppermute | solution.py:476
  276.0 4.3 shard_map.76
  280.3 2.7 shard_map.77
  287.7 4.3 shard_map.78
  295.0 10.7 %collective-permute-start.50 = (bf16[1536,256]{1,0:T(8,128)(2,1)S(1)}, bf16[1536,256]{1,0:T(8,128)(2,1)S(1)}, u32[]{:S(2)}, u32[]{:S(2)}) collective-permute-start(bf16[1536,256]{1,0:T(8,128)(2,1)S(1)} %get-tuple-element.442.refs_3_), channel_id=1, source_target_pairs={{0,8},{4,12},{24,16},{28,20},{8,0},{12,4},{16,24},{20,28},{1,9},{5... | collective-permute-start | bytes 2359304 | tf_op jit(solution)/shard_map/ppermute | solution.py:476
  309.0 4.3 shard_map.81
  319.9 3.2 shard_map.83
  323.1 4.3 shard_map.84
  330.4 3.8 collective-permute-start.55
  334.4 3.2 shard_map.86
  337.5 4.3 shard_map.87
  344.9 3.7 collective-permute-start.65
  350.0 3.1 shard_map.89
  353.2 4.3 shard_map.90
  360.7 4.5 collective-permute-start.61
  366.7 3.1 shard_map.92
  369.8 4.3 shard_map.93
  381.5 3.2 shard_map.95
  384.7 4.1 collective-permute-done.61.refs_1_
  391.3 4.5 collective-permute-start.67
  395.8 3.1 shard_map.97
  399.0 3.8 collective-permute-done.71.refs_1_
  406.8 4.5 collective-permute-start.77
  411.9 3.1 shard_map.99
  417.1 3.5 collective-permute-start.73
  420.7 3.1 shard_map.101
  428.2 3.1 shard_map.103
  432.9 3.9 collective-permute-start.79
  436.8 3.2 shard_map.105
  446.1 3.2 shard_map.107
  450.3 7.2 %collective-permute-start.89 = (bf16[512,256]{1,0:T(8,128)(2,1)S(1)}, bf16[512,256]{1,0:T(8,128)(2,1)S(1)}, u32[]{:S(2)}, u32[]{:S(2)}) collective-permute-start(bf16[512,256]{1,0:T(8,128)(2,1)S(1)} %get-tuple-element.584.refs_2_), channel_id=1, source_target_pairs={{0,8},{4,12},{24,16},{28,20},{8,0},{12,4},{16,24},{20,28},{1,9},{5... | collective-permute-start | bytes 786440 | tf_op jit(solution)/shard_map/ppermute | solution.py:476
  457.4 3.2 shard_map.109
  463.8 3.1 shard_map.111
  468.9 3.2 shard_map.114
  (278 shorter events, 150.2 us)
Async XLA Ops:
  6.5 164.0 %all-gather.2.cloned.1.call-start = ((), (), s32[]{:S(2)}) async-start(), calls=%async_computation | async-start | bytes 4718592 | tf_op jit(solution)/shard_map/all_gather | solution.py:481
  7.8 43.9 %collective-permute-start.11 = (bf16[256,3584]{1,0:T(8,128)(2,1)}, bf16[256,3584]{1,0:T(8,128)(2,1)}, u32[]{:S(2)}, u32[]{:S(2)}) collective-permute-start(bf16[256,3584]{1,0:T(8,128)(2,1)} %refs_0_.23), channel_id=1, source_target_pairs={{0,2},{1,3},{2,0},{3,1},{4,6},{5,7},{6,4},{7,5},{8,10},{9,11},{10,... | collective-permute-start | bytes 5505032 | tf_op jit(solution)/shard_map/ppermute | solution.py:429
  18.7 21.3 %collective-permute-start.4 = (bf16[512,256]{1,0:T(8,128)(2,1)S(1)}, bf16[512,256]{1,0:T(8,128)(2,1)S(1)}, u32[]{:S(2)}, u32[]{:S(2)}) collective-permute-start(bf16[512,256]{1,0:T(8,128)(2,1)S(1)} %get-tuple-element.309), channel_id=1, source_target_pairs={{0,8},{4,12},{24,16},{28,20},{8,0},{12,4},{16,24},{20,28},{1,9},{5... | collective-permute-start | bytes 786440 | tf_op jit(solution)/shard_map/ppermute | solution.py:476
  29.0 21.5 %collective-permute-start.2 = (bf16[512,256]{1,0:T(8,128)(2,1)S(1)}, bf16[512,256]{1,0:T(8,128)(2,1)S(1)}, u32[]{:S(2)}, u32[]{:S(2)}) collective-permute-start(bf16[512,256]{1,0:T(8,128)(2,1)S(1)} %get-tuple-element.307), channel_id=1, source_target_pairs={{0,8},{4,12},{24,16},{28,20},{8,0},{12,4},{16,24},{20,28},{1,9},{5... | collective-permute-start | bytes 786440 | tf_op jit(solution)/shard_map/ppermute | solution.py:476
  53.8 59.2 %collective-permute-start.15 = (bf16[256,3584]{1,0:T(8,128)(2,1)S(1)}, bf16[256,3584]{1,0:T(8,128)(2,1)S(1)}, u32[]{:S(2)}, u32[]{:S(2)}) collective-permute-start(bf16[256,3584]{1,0:T(8,128)(2,1)S(1)} %get-tuple-element.336.refs_0_.refs_2_), channel_id=1, source_target_pairs={{0,1},{1,0},{2,3},{3,2},{4,5},{5,4},{6,7},{7,6},{8,9},{9,8},{10,11... | collective-permute-start | bytes 5505032 | tf_op jit(solution)/shard_map/ppermute | solution.py:429
  53.9 28.5 %collective-permute-start.9 = (bf16[768,256]{1,0:T(8,128)(2,1)S(1)}, bf16[768,256]{1,0:T(8,128)(2,1)S(1)}, u32[]{:S(2)}, u32[]{:S(2)}) collective-permute-start(bf16[768,256]{1,0:T(8,128)(2,1)S(1)} %get-tuple-element.320), channel_id=1, source_target_pairs={{0,8},{4,12},{24,16},{28,20},{8,0},{12,4},{16,24},{20,28},{1,9},{5... | collective-permute-start | bytes 1179656 | tf_op jit(solution)/shard_map/ppermute | solution.py:476
  55.4 29.1 %collective-permute-start.5 = (bf16[256,256]{1,0:T(8,128)(2,1)S(1)}, bf16[256,256]{1,0:T(8,128)(2,1)S(1)}, u32[]{:S(2)}, u32[]{:S(2)}) collective-permute-start(bf16[256,256]{1,0:T(8,128)(2,1)S(1)} %get-tuple-element.316), channel_id=1, source_target_pairs={{0,4},{4,0},{8,12},{12,8},{16,20},{20,16},{24,28},{28,24},{1,5},{5... | collective-permute-start | bytes 393224 | tf_op jit(solution)/shard_map/ppermute | solution.py:475
  56.9 33.2 %collective-permute-start.7 = (bf16[256,256]{1,0:T(8,128)(2,1)S(1)}, bf16[256,256]{1,0:T(8,128)(2,1)S(1)}, u32[]{:S(2)}, u32[]{:S(2)}) collective-permute-start(bf16[256,256]{1,0:T(8,128)(2,1)S(1)} %get-tuple-element.318), channel_id=1, source_target_pairs={{8,16},{12,20},{16,8},{20,12},{0,0},{4,4},{24,24},{28,28},{9,17},{... | collective-permute-start | bytes 393224 | tf_op jit(solution)/shard_map/ppermute | solution.py:477
  57.5 47.3 %collective-permute-start.6 = (bf16[768,256]{1,0:T(8,128)(2,1)S(1)}, bf16[768,256]{1,0:T(8,128)(2,1)S(1)}, u32[]{:S(2)}, u32[]{:S(2)}) collective-permute-start(bf16[768,256]{1,0:T(8,128)(2,1)S(1)} %get-tuple-element.317), channel_id=1, source_target_pairs={{0,8},{4,12},{24,16},{28,20},{8,0},{12,4},{16,24},{20,28},{1,9},{5... | collective-permute-start | bytes 1179656 | tf_op jit(solution)/shard_map/ppermute | solution.py:476
  83.8 23.2 %collective-permute-start.18 = (bf16[512,256]{1,0:T(8,128)(2,1)S(1)}, bf16[512,256]{1,0:T(8,128)(2,1)S(1)}, u32[]{:S(2)}, u32[]{:S(2)}) collective-permute-start(bf16[512,256]{1,0:T(8,128)(2,1)S(1)} %get-tuple-element.339), channel_id=1, source_target_pairs={{8,16},{12,20},{16,8},{20,12},{0,0},{4,4},{24,24},{28,28},{9,17},{... | collective-permute-start | bytes 786440 | tf_op jit(solution)/shard_map/ppermute | solution.py:477
  84.4 37.2 %collective-permute-start.17 = (bf16[768,256]{1,0:T(8,128)(2,1)S(1)}, bf16[768,256]{1,0:T(8,128)(2,1)S(1)}, u32[]{:S(2)}, u32[]{:S(2)}) collective-permute-start(bf16[768,256]{1,0:T(8,128)(2,1)S(1)} %get-tuple-element.338), channel_id=1, source_target_pairs={{0,8},{4,12},{24,16},{28,20},{8,0},{12,4},{16,24},{20,28},{1,9},{5... | collective-permute-start | bytes 1179656 | tf_op jit(solution)/shard_map/ppermute | solution.py:476
  90.1 31.6 %collective-permute-start.16 = (bf16[512,256]{1,0:T(8,128)(2,1)S(1)}, bf16[512,256]{1,0:T(8,128)(2,1)S(1)}, u32[]{:S(2)}, u32[]{:S(2)}) collective-permute-start(bf16[512,256]{1,0:T(8,128)(2,1)S(1)} %get-tuple-element.337), channel_id=1, source_target_pairs={{0,4},{4,0},{8,12},{12,8},{16,20},{20,16},{24,28},{28,24},{1,5},{5... | collective-permute-start | bytes 786440 | tf_op jit(solution)/shard_map/ppermute | solution.py:475
  106.2 20.6 %collective-permute-start.14 = (bf16[512,256]{1,0:T(8,128)(2,1)S(1)}, bf16[512,256]{1,0:T(8,128)(2,1)S(1)}, u32[]{:S(2)}, u32[]{:S(2)}) collective-permute-start(bf16[512,256]{1,0:T(8,128)(2,1)S(1)} %get-tuple-element.335), channel_id=1, source_target_pairs={{8,16},{12,20},{16,8},{20,12},{0,0},{4,4},{24,24},{28,28},{9,17},{... | collective-permute-start | bytes 786440 | tf_op jit(solution)/shard_map/ppermute | solution.py:477
  106.9 27.4 %collective-permute-start.13 = (bf16[768,256]{1,0:T(8,128)(2,1)S(1)}, bf16[768,256]{1,0:T(8,128)(2,1)S(1)}, u32[]{:S(2)}, u32[]{:S(2)}) collective-permute-start(bf16[768,256]{1,0:T(8,128)(2,1)S(1)} %get-tuple-element.334), channel_id=1, source_target_pairs={{0,8},{4,12},{24,16},{28,20},{8,0},{12,4},{16,24},{20,28},{1,9},{5... | collective-permute-start | bytes 1179656 | tf_op jit(solution)/shard_map/ppermute | solution.py:476
  113.0 21.3 %collective-permute-start.12 = (bf16[512,256]{1,0:T(8,128)(2,1)S(1)}, bf16[512,256]{1,0:T(8,128)(2,1)S(1)}, u32[]{:S(2)}, u32[]{:S(2)}) collective-permute-start(bf16[512,256]{1,0:T(8,128)(2,1)S(1)} %get-tuple-element.333), channel_id=1, source_target_pairs={{0,4},{4,0},{8,12},{12,8},{16,20},{20,16},{24,28},{28,24},{1,5},{5... | collective-permute-start | bytes 786440 | tf_op jit(solution)/shard_map/ppermute | solution.py:475
  124.2 24.2 %collective-permute-start.23 = (bf16[1280,256]{1,0:T(8,128)(2,1)S(1)}, bf16[1280,256]{1,0:T(8,128)(2,1)S(1)}, u32[]{:S(2)}, u32[]{:S(2)}) collective-permute-start(bf16[1280,256]{1,0:T(8,128)(2,1)S(1)} %get-tuple-element.358.refs_3_), channel_id=1, source_target_pairs={{0,8},{4,12},{24,16},{28,20},{8,0},{12,4},{16,24},{20,28},{1,9},{5... | collective-permute-start | bytes 1966088 | tf_op jit(solution)/shard_map/ppermute | solution.py:476
  126.8 21.7 %collective-permute-start.22 = (bf16[768,256]{1,0:T(8,128)(2,1)S(1)}, bf16[768,256]{1,0:T(8,128)(2,1)S(1)}, u32[]{:S(2)}, u32[]{:S(2)}) collective-permute-start(bf16[768,256]{1,0:T(8,128)(2,1)S(1)} %get-tuple-element.357), channel_id=1, source_target_pairs={{0,4},{4,0},{8,12},{12,8},{16,20},{20,16},{24,28},{28,24},{1,5},{5... | collective-permute-start | bytes 1179656 | tf_op jit(solution)/shard_map/ppermute | solution.py:475
  137.3 25.0 %collective-permute-start.20 = (bf16[1280,256]{1,0:T(8,128)(2,1)S(1)}, bf16[1280,256]{1,0:T(8,128)(2,1)S(1)}, u32[]{:S(2)}, u32[]{:S(2)}) collective-permute-start(bf16[1280,256]{1,0:T(8,128)(2,1)S(1)} %get-tuple-element.355.refs_3_), channel_id=1, source_target_pairs={{0,8},{4,12},{24,16},{28,20},{8,0},{12,4},{16,24},{20,28},{1,9},{5... | collective-permute-start | bytes 1966088 | tf_op jit(solution)/shard_map/ppermute | solution.py:476
  139.8 22.6 %collective-permute-start.19 = (bf16[768,256]{1,0:T(8,128)(2,1)S(1)}, bf16[768,256]{1,0:T(8,128)(2,1)S(1)}, u32[]{:S(2)}, u32[]{:S(2)}) collective-permute-start(bf16[768,256]{1,0:T(8,128)(2,1)S(1)} %get-tuple-element.354), channel_id=1, source_target_pairs={{0,4},{4,0},{8,12},{12,8},{16,20},{20,16},{24,28},{28,24},{1,5},{5... | collective-permute-start | bytes 1179656 | tf_op jit(solution)/shard_map/ppermute | solution.py:475
  151.0 18.7 %collective-permute-start.25 = (bf16[1024,256]{1,0:T(8,128)(2,1)S(1)}, bf16[1024,256]{1,0:T(8,128)(2,1)S(1)}, u32[]{:S(2)}, u32[]{:S(2)}) collective-permute-start(bf16[1024,256]{1,0:T(8,128)(2,1)S(1)} %get-tuple-element.375.refs_4_), channel_id=1, source_target_pairs={{8,16},{12,20},{16,8},{20,12},{0,0},{4,4},{24,24},{28,28},{9,17},{... | collective-permute-start | bytes 1572872 | tf_op jit(solution)/shard_map/ppermute | solution.py:477
  183.2 34.1 %collective-permute-start.26 = (f32[512,1024]{1,0:T(8,128)S(1)}, f32[512,1024]{1,0:T(8,128)S(1)}, u32[]{:S(2)}, u32[]{:S(2)}) collective-permute-start(f32[512,1024]{1,0:T(8,128)S(1)} %get-tuple-element.377), channel_id=1, source_target_pairs={{0,1},{1,0},{2,3},{3,2},{4,5},{5,4},{6,7},{7,6},{8,9},{9,8},{10,11... | collective-permute-start | bytes 6291464 | tf_op jit(solution)/shard_map/ppermute | solution.py:429
  183.3 21.4 %collective-permute-start.28 = (bf16[1536,256]{1,0:T(8,128)(2,1)}, bf16[1536,256]{1,0:T(8,128)(2,1)S(1)}, u32[]{:S(2)}, u32[]{:S(2)}) collective-permute-start(bf16[1536,256]{1,0:T(8,128)(2,1)} %copy-done.12), channel_id=1, source_target_pairs={{0,8},{4,12},{24,16},{28,20},{8,0},{12,4},{16,24},{20,28},{1,9},{5... | collective-permute-start | bytes 2359304 | tf_op jit(solution)/shard_map/ppermute | solution.py:476
  186.5 30.4 %collective-permute-start.29 = (bf16[1024,256]{1,0:T(8,128)(2,1)}, bf16[1024,256]{1,0:T(8,128)(2,1)S(1)}, u32[]{:S(2)}, u32[]{:S(2)}) collective-permute-start(bf16[1024,256]{1,0:T(8,128)(2,1)} %copy-done.18), channel_id=1, source_target_pairs={{8,16},{12,20},{16,8},{20,12},{0,0},{4,4},{24,24},{28,28},{9,17},{... | collective-permute-start | bytes 1572872 | tf_op jit(solution)/shard_map/ppermute | solution.py:477
  188.2 41.9 %collective-permute-start.32 = (bf16[1536,256]{1,0:T(8,128)(2,1)}, bf16[1536,256]{1,0:T(8,128)(2,1)S(1)}, u32[]{:S(2)}, u32[]{:S(2)}) collective-permute-start(bf16[1536,256]{1,0:T(8,128)(2,1)} %copy-done.10), channel_id=1, source_target_pairs={{0,8},{4,12},{24,16},{28,20},{8,0},{12,4},{16,24},{20,28},{1,9},{5... | collective-permute-start | bytes 2359304 | tf_op jit(solution)/shard_map/ppermute | solution.py:476
  200.3 29.9 %collective-permute-start.31 = (bf16[1024,256]{1,0:T(8,128)(2,1)}, bf16[1024,256]{1,0:T(8,128)(2,1)S(1)}, u32[]{:S(2)}, u32[]{:S(2)}) collective-permute-start(bf16[1024,256]{1,0:T(8,128)(2,1)} %copy-done.16), channel_id=1, source_target_pairs={{0,4},{4,0},{8,12},{12,8},{16,20},{20,16},{24,28},{28,24},{1,5},{5... | collective-permute-start | bytes 1572872 | tf_op jit(solution)/shard_map/ppermute | solution.py:475
  214.7 27.1 %collective-permute-start.37 = (bf16[1536,256]{1,0:T(8,128)(2,1)S(1)}, bf16[1536,256]{1,0:T(8,128)(2,1)S(1)}, u32[]{:S(2)}, u32[]{:S(2)}) collective-permute-start(bf16[1536,256]{1,0:T(8,128)(2,1)S(1)} %get-tuple-element.402.refs_3_), channel_id=1, source_target_pairs={{0,8},{4,12},{24,16},{28,20},{8,0},{12,4},{16,24},{20,28},{1,9},{5... | collective-permute-start | bytes 2359304 | tf_op jit(solution)/shard_map/ppermute | solution.py:476
  216.9 18.6 %collective-permute-start.36 = (bf16[1280,256]{1,0:T(8,128)(2,1)S(1)}, bf16[1280,256]{1,0:T(8,128)(2,1)S(1)}, u32[]{:S(2)}, u32[]{:S(2)}) collective-permute-start(bf16[1280,256]{1,0:T(8,128)(2,1)S(1)} %get-tuple-element.401.refs_1_), channel_id=1, source_target_pairs={{0,4},{4,0},{8,12},{12,8},{16,20},{20,16},{24,28},{28,24},{1,5},{5... | collective-permute-start | bytes 1966088 | tf_op jit(solution)/shard_map/ppermute | solution.py:475
  217.3 19.7 %collective-permute-start.38 = (bf16[1280,256]{1,0:T(8,128)(2,1)S(1)}, bf16[1280,256]{1,0:T(8,128)(2,1)S(1)}, u32[]{:S(2)}, u32[]{:S(2)}) collective-permute-start(bf16[1280,256]{1,0:T(8,128)(2,1)S(1)} %get-tuple-element.403.refs_4_), channel_id=1, source_target_pairs={{8,16},{12,20},{16,8},{20,12},{0,0},{4,4},{24,24},{28,28},{9,17},{... | collective-permute-start | bytes 1966088 | tf_op jit(solution)/shard_map/ppermute | solution.py:477
  233.9 17.7 %collective-permute-start.33 = (bf16[1280,256]{1,0:T(8,128)(2,1)S(1)}, bf16[1280,256]{1,0:T(8,128)(2,1)S(1)}, u32[]{:S(2)}, u32[]{:S(2)}) collective-permute-start(bf16[1280,256]{1,0:T(8,128)(2,1)S(1)} %get-tuple-element.398.refs_1_), channel_id=1, source_target_pairs={{0,4},{4,0},{8,12},{12,8},{16,20},{20,16},{24,28},{28,24},{1,5},{5... | collective-permute-start | bytes 1966088 | tf_op jit(solution)/shard_map/ppermute | solution.py:475
  235.5 29.3 %collective-permute-start.30 = (f32[256,1024]{1,0:T(8,128)S(1)}, f32[256,1024]{1,0:T(8,128)S(1)}, u32[]{:S(2)}, u32[]{:S(2)}) collective-permute-start(f32[256,1024]{1,0:T(8,128)S(1)} %get-tuple-element.388), channel_id=1, source_target_pairs={{0,2},{1,3},{2,0},{3,1},{4,6},{5,7},{6,4},{7,5},{8,10},{9,11},{10,... | collective-permute-start | bytes 3145736 | tf_op jit(solution)/shard_map/ppermute | solution.py:429
  237.1 23.9 %collective-permute-start.34 = (bf16[1536,256]{1,0:T(8,128)(2,1)S(1)}, bf16[1536,256]{1,0:T(8,128)(2,1)S(1)}, u32[]{:S(2)}, u32[]{:S(2)}) collective-permute-start(bf16[1536,256]{1,0:T(8,128)(2,1)S(1)} %get-tuple-element.399.refs_3_), channel_id=1, source_target_pairs={{0,8},{4,12},{24,16},{28,20},{8,0},{12,4},{16,24},{20,28},{1,9},{5... | collective-permute-start | bytes 2359304 | tf_op jit(solution)/shard_map/ppermute | solution.py:476
  244.7 19.6 %collective-permute-start.39 = (bf16[1536,256]{1,0:T(8,128)(2,1)S(1)}, bf16[1536,256]{1,0:T(8,128)(2,1)S(1)}, u32[]{:S(2)}, u32[]{:S(2)}) collective-permute-start(bf16[1536,256]{1,0:T(8,128)(2,1)S(1)} %get-tuple-element.417.refs_4_), channel_id=1, source_target_pairs={{8,16},{12,20},{16,8},{20,12},{0,0},{4,4},{24,24},{28,28},{9,17},{... | collective-permute-start | bytes 2359304 | tf_op jit(solution)/shard_map/ppermute | solution.py:477
  245.4 29.0 %collective-permute-start.46 = (bf16[1280,256]{1,0:T(8,128)(2,1)S(1)}, bf16[1280,256]{1,0:T(8,128)(2,1)S(1)}, u32[]{:S(2)}, u32[]{:S(2)}) collective-permute-start(bf16[1280,256]{1,0:T(8,128)(2,1)S(1)} %get-tuple-element.422.refs_1_), channel_id=1, source_target_pairs={{0,4},{4,0},{8,12},{12,8},{16,20},{20,16},{24,28},{28,24},{1,5},{5... | collective-permute-start | bytes 1966088 | tf_op jit(solution)/shard_map/ppermute | solution.py:475
  251.6 28.7 %collective-permute-start.47 = (bf16[1536,256]{1,0:T(8,128)(2,1)S(1)}, bf16[1536,256]{1,0:T(8,128)(2,1)S(1)}, u32[]{:S(2)}, u32[]{:S(2)}) collective-permute-start(bf16[1536,256]{1,0:T(8,128)(2,1)S(1)} %get-tuple-element.423.refs_3_), channel_id=1, source_target_pairs={{0,8},{4,12},{24,16},{28,20},{8,0},{12,4},{16,24},{20,28},{1,9},{5... | collective-permute-start | bytes 2359304 | tf_op jit(solution)/shard_map/ppermute | solution.py:476
  263.5 23.6 %collective-permute-start.45 = (bf16[1536,256]{1,0:T(8,128)(2,1)S(1)}, bf16[1536,256]{1,0:T(8,128)(2,1)S(1)}, u32[]{:S(2)}, u32[]{:S(2)}) collective-permute-start(bf16[1536,256]{1,0:T(8,128)(2,1)S(1)} %get-tuple-element.421.refs_4_), channel_id=1, source_target_pairs={{8,16},{12,20},{16,8},{20,12},{0,0},{4,4},{24,24},{28,28},{9,17},{... | collective-permute-start | bytes 2359304 | tf_op jit(solution)/shard_map/ppermute | solution.py:477
  264.3 19.5 %collective-permute-start.43 = (bf16[1024,256]{1,0:T(8,128)(2,1)S(1)}, bf16[1024,256]{1,0:T(8,128)(2,1)S(1)}, u32[]{:S(2)}, u32[]{:S(2)}) collective-permute-start(bf16[1024,256]{1,0:T(8,128)(2,1)S(1)} %get-tuple-element.419.refs_1_), channel_id=1, source_target_pairs={{0,4},{4,0},{8,12},{12,8},{16,20},{20,16},{24,28},{28,24},{1,5},{5... | collective-permute-start | bytes 1572872 | tf_op jit(solution)/shard_map/ppermute | solution.py:475
  264.8 20.6 %collective-permute-start.44 = (bf16[1024,256]{1,0:T(8,128)(2,1)S(1)}, bf16[1024,256]{1,0:T(8,128)(2,1)S(1)}, u32[]{:S(2)}, u32[]{:S(2)}) collective-permute-start(bf16[1024,256]{1,0:T(8,128)(2,1)S(1)} %get-tuple-element.420.refs_3_), channel_id=1, source_target_pairs={{0,8},{4,12},{24,16},{28,20},{8,0},{12,4},{16,24},{20,28},{1,9},{5... | collective-permute-start | bytes 1572872 | tf_op jit(solution)/shard_map/ppermute | solution.py:476
  285.4 27.9 %collective-permute-start.53 = (bf16[1536,256]{1,0:T(8,128)(2,1)S(1)}, bf16[1536,256]{1,0:T(8,128)(2,1)S(1)}, u32[]{:S(2)}, u32[]{:S(2)}) collective-permute-start(bf16[1536,256]{1,0:T(8,128)(2,1)S(1)} %get-tuple-element.446.refs_3_), channel_id=1, source_target_pairs={{0,8},{4,12},{24,16},{28,20},{8,0},{12,4},{16,24},{20,28},{1,9},{5... | collective-permute-start | bytes 2359304 | tf_op jit(solution)/shard_map/ppermute | solution.py:476
  287.1 18.6 %collective-permute-start.42 = (bf16[256,1024]{1,0:T(8,128)(2,1)S(1)}, bf16[256,1024]{1,0:T(8,128)(2,1)S(1)}, u32[]{:S(2)}, u32[]{:S(2)}) collective-permute-start(bf16[256,1024]{1,0:T(8,128)(2,1)S(1)} %collective-permute-done.41.refs_2_), channel_id=1, source_target_pairs={{0,1},{1,0},{2,3},{3,2},{4,5},{5,4},{6,7},{7,6},{8,9},{9,8},{10,11... | collective-permute-start | bytes 1572872 | tf_op jit(solution)/shard_map/ppermute | solution.py:429
  287.1 26.2 %collective-permute-start.52 = (bf16[1280,256]{1,0:T(8,128)(2,1)S(1)}, bf16[1280,256]{1,0:T(8,128)(2,1)S(1)}, u32[]{:S(2)}, u32[]{:S(2)}) collective-permute-start(bf16[1280,256]{1,0:T(8,128)(2,1)S(1)} %get-tuple-element.444.refs_3_), channel_id=1, source_target_pairs={{0,4},{4,0},{8,12},{12,8},{16,20},{20,16},{24,28},{28,24},{1,5},{5... | collective-permute-start | bytes 1966088 | tf_op jit(solution)/shard_map/ppermute | solution.py:475
  294.3 25.0 %collective-permute-start.51 = (bf16[1280,256]{1,0:T(8,128)(2,1)S(1)}, bf16[1280,256]{1,0:T(8,128)(2,1)S(1)}, u32[]{:S(2)}, u32[]{:S(2)}) collective-permute-start(bf16[1280,256]{1,0:T(8,128)(2,1)S(1)} %get-tuple-element.443.refs_4_), channel_id=1, source_target_pairs={{8,16},{12,20},{16,8},{20,12},{0,0},{4,4},{24,24},{28,28},{9,17},{... | collective-permute-start | bytes 1966088 | tf_op jit(solution)/shard_map/ppermute | solution.py:477
  295.0 32.4 %collective-permute-start.50 = (bf16[1536,256]{1,0:T(8,128)(2,1)S(1)}, bf16[1536,256]{1,0:T(8,128)(2,1)S(1)}, u32[]{:S(2)}, u32[]{:S(2)}) collective-permute-start(bf16[1536,256]{1,0:T(8,128)(2,1)S(1)} %get-tuple-element.442.refs_3_), channel_id=1, source_target_pairs={{0,8},{4,12},{24,16},{28,20},{8,0},{12,4},{16,24},{20,28},{1,9},{5... | collective-permute-start | bytes 2359304 | tf_op jit(solution)/shard_map/ppermute | solution.py:476
  305.7 21.7 %collective-permute-start.49 = (bf16[1280,256]{1,0:T(8,128)(2,1)S(1)}, bf16[1280,256]{1,0:T(8,128)(2,1)S(1)}, u32[]{:S(2)}, u32[]{:S(2)}) collective-permute-start(bf16[1280,256]{1,0:T(8,128)(2,1)S(1)} %get-tuple-element.441.refs_3_), channel_id=1, source_target_pairs={{0,4},{4,0},{8,12},{12,8},{16,20},{20,16},{24,28},{28,24},{1,5},{5... | collective-permute-start | bytes 1966088 | tf_op jit(solution)/shard_map/ppermute | solution.py:475
  315.8 18.5 %collective-permute-start.57 = (bf16[1280,256]{1,0:T(8,128)(2,1)S(1)}, bf16[1280,256]{1,0:T(8,128)(2,1)S(1)}, u32[]{:S(2)}, u32[]{:S(2)}) collective-permute-start(bf16[1280,256]{1,0:T(8,128)(2,1)S(1)} %get-tuple-element.471.refs_4_), channel_id=1, source_target_pairs={{8,16},{12,20},{16,8},{20,12},{0,0},{4,4},{24,24},{28,28},{9,17},{... | collective-permute-start | bytes 1966088 | tf_op jit(solution)/shard_map/ppermute | solution.py:477
  316.7 25.2 %collective-permute-start.59 = (bf16[1536,256]{1,0:T(8,128)(2,1)S(1)}, bf16[1536,256]{1,0:T(8,128)(2,1)S(1)}, u32[]{:S(2)}, u32[]{:S(2)}) collective-permute-start(bf16[1536,256]{1,0:T(8,128)(2,1)S(1)} %get-tuple-element.474.refs_3_), channel_id=1, source_target_pairs={{0,8},{4,12},{24,16},{28,20},{8,0},{12,4},{16,24},{20,28},{1,9},{5... | collective-permute-start | bytes 2359304 | tf_op jit(solution)/shard_map/ppermute | solution.py:476
  319.3 22.6 %collective-permute-start.58 = (bf16[1280,256]{1,0:T(8,128)(2,1)S(1)}, bf16[1280,256]{1,0:T(8,128)(2,1)S(1)}, u32[]{:S(2)}, u32[]{:S(2)}) collective-permute-start(bf16[1280,256]{1,0:T(8,128)(2,1)S(1)} %get-tuple-element.473.refs_3_), channel_id=1, source_target_pairs={{0,4},{4,0},{8,12},{12,8},{16,20},{20,16},{24,28},{28,24},{1,5},{5... | collective-permute-start | bytes 1966088 | tf_op jit(solution)/shard_map/ppermute | solution.py:475
  329.7 18.9 %collective-permute-start.56 = (bf16[1024,256]{1,0:T(8,128)(2,1)S(1)}, bf16[1024,256]{1,0:T(8,128)(2,1)S(1)}, u32[]{:S(2)}, u32[]{:S(2)}) collective-permute-start(bf16[1024,256]{1,0:T(8,128)(2,1)S(1)} %get-tuple-element.465.refs_4_), channel_id=1, source_target_pairs={{8,16},{12,20},{16,8},{20,12},{0,0},{4,4},{24,24},{28,28},{9,17},{... | collective-permute-start | bytes 1572872 | tf_op jit(solution)/shard_map/ppermute | solution.py:477
  330.4 27.4 %collective-permute-start.55 = (bf16[1536,256]{1,0:T(8,128)(2,1)S(1)}, bf16[1536,256]{1,0:T(8,128)(2,1)S(1)}, u32[]{:S(2)}, u32[]{:S(2)}) collective-permute-start(bf16[1536,256]{1,0:T(8,128)(2,1)S(1)} %get-tuple-element.464.refs_3_), channel_id=1, source_target_pairs={{0,8},{4,12},{24,16},{28,20},{8,0},{12,4},{16,24},{20,28},{1,9},{5... | collective-permute-start | bytes 2359304 | tf_op jit(solution)/shard_map/ppermute | solution.py:476
  334.3 23.2 %collective-permute-start.54 = (bf16[1024,256]{1,0:T(8,128)(2,1)S(1)}, bf16[1024,256]{1,0:T(8,128)(2,1)S(1)}, u32[]{:S(2)}, u32[]{:S(2)}) collective-permute-start(bf16[1024,256]{1,0:T(8,128)(2,1)S(1)} %get-tuple-element.463.refs_1_.refs_3_), channel_id=1, source_target_pairs={{0,4},{4,0},{8,12},{12,8},{16,20},{20,16},{24,28},{28,24},{1,5},{5... | collective-permute-start | bytes 1572872 | tf_op jit(solution)/shard_map/ppermute | solution.py:475
  344.2 21.1 %collective-permute-start.63 = (bf16[1024,256]{1,0:T(8,128)(2,1)S(1)}, bf16[1024,256]{1,0:T(8,128)(2,1)S(1)}, u32[]{:S(2)}, u32[]{:S(2)}) collective-permute-start(bf16[1024,256]{1,0:T(8,128)(2,1)S(1)} %get-tuple-element.502.refs_4_), channel_id=1, source_target_pairs={{8,16},{12,20},{16,8},{20,12},{0,0},{4,4},{24,24},{28,28},{9,17},{... | collective-permute-start | bytes 1572872 | tf_op jit(solution)/shard_map/ppermute | solution.py:477
  344.9 29.8 %collective-permute-start.65 = (bf16[1536,256]{1,0:T(8,128)(2,1)S(1)}, bf16[1536,256]{1,0:T(8,128)(2,1)S(1)}, u32[]{:S(2)}, u32[]{:S(2)}) collective-permute-start(bf16[1536,256]{1,0:T(8,128)(2,1)S(1)} %get-tuple-element.505.refs_3_), channel_id=1, source_target_pairs={{0,8},{4,12},{24,16},{28,20},{8,0},{12,4},{16,24},{20,28},{1,9},{5... | collective-permute-start | bytes 2359304 | tf_op jit(solution)/shard_map/ppermute | solution.py:476
  348.6 25.6 %collective-permute-start.64 = (bf16[1024,256]{1,0:T(8,128)(2,1)S(1)}, bf16[1024,256]{1,0:T(8,128)(2,1)S(1)}, u32[]{:S(2)}, u32[]{:S(2)}) collective-permute-start(bf16[1024,256]{1,0:T(8,128)(2,1)S(1)} %get-tuple-element.504.refs_1_.refs_3_), channel_id=1, source_target_pairs={{0,4},{4,0},{8,12},{12,8},{16,20},{20,16},{24,28},{28,24},{1,5},{5... | collective-permute-start | bytes 1572872 | tf_op jit(solution)/shard_map/ppermute | solution.py:475
  360.0 20.5 %collective-permute-start.62 = (bf16[768,256]{1,0:T(8,128)(2,1)S(1)}, bf16[768,256]{1,0:T(8,128)(2,1)S(1)}, u32[]{:S(2)}, u32[]{:S(2)}) collective-permute-start(bf16[768,256]{1,0:T(8,128)(2,1)S(1)} %get-tuple-element.492.refs_4_), channel_id=1, source_target_pairs={{8,16},{12,20},{16,8},{20,12},{0,0},{4,4},{24,24},{28,28},{9,17},{... | collective-permute-start | bytes 1179656 | tf_op jit(solution)/shard_map/ppermute | solution.py:477
  360.7 28.1 %collective-permute-start.61 = (bf16[1280,256]{1,0:T(8,128)(2,1)S(1)}, bf16[1280,256]{1,0:T(8,128)(2,1)S(1)}, u32[]{:S(2)}, u32[]{:S(2)}) collective-permute-start(bf16[1280,256]{1,0:T(8,128)(2,1)S(1)} %get-tuple-element.491.refs_3_), channel_id=1, source_target_pairs={{0,8},{4,12},{24,16},{28,20},{8,0},{12,4},{16,24},{20,28},{1,9},{5... | collective-permute-start | bytes 1966088 | tf_op jit(solution)/shard_map/ppermute | solution.py:476
  365.3 19.4 %collective-permute-start.60 = (bf16[1024,256]{1,0:T(8,128)(2,1)S(1)}, bf16[1024,256]{1,0:T(8,128)(2,1)S(1)}, u32[]{:S(2)}, u32[]{:S(2)}) collective-permute-start(bf16[1024,256]{1,0:T(8,128)(2,1)S(1)} %get-tuple-element.490.refs_1_.refs_3_), channel_id=1, source_target_pairs={{0,4},{4,0},{8,12},{12,8},{16,20},{20,16},{24,28},{28,24},{1,5},{5... | collective-permute-start | bytes 1572872 | tf_op jit(solution)/shard_map/ppermute | solution.py:475
  376.9 25.9 %collective-permute-start.71 = (bf16[1280,256]{1,0:T(8,128)(2,1)S(1)}, bf16[1280,256]{1,0:T(8,128)(2,1)S(1)}, u32[]{:S(2)}, u32[]{:S(2)}) collective-permute-start(bf16[1280,256]{1,0:T(8,128)(2,1)S(1)} %get-tuple-element.529.refs_3_), channel_id=1, source_target_pairs={{0,8},{4,12},{24,16},{28,20},{8,0},{12,4},{16,24},{20,28},{1,9},{5... | collective-permute-start | bytes 1966088 | tf_op jit(solution)/shard_map/ppermute | solution.py:476
  379.1 19.9 %collective-permute-start.70 = (bf16[1024,256]{1,0:T(8,128)(2,1)S(1)}, bf16[1024,256]{1,0:T(8,128)(2,1)S(1)}, u32[]{:S(2)}, u32[]{:S(2)}) collective-permute-start(bf16[1024,256]{1,0:T(8,128)(2,1)S(1)} %get-tuple-element.528.refs_1_.refs_3_), channel_id=1, source_target_pairs={{0,4},{4,0},{8,12},{12,8},{16,20},{20,16},{24,28},{28,24},{1,5},{5... | collective-permute-start | bytes 1572872 | tf_op jit(solution)/shard_map/ppermute | solution.py:475
  390.6 20.7 %collective-permute-start.68 = (bf16[768,256]{1,0:T(8,128)(2,1)S(1)}, bf16[768,256]{1,0:T(8,128)(2,1)S(1)}, u32[]{:S(2)}, u32[]{:S(2)}) collective-permute-start(bf16[768,256]{1,0:T(8,128)(2,1)S(1)} %get-tuple-element.517.refs_4_), channel_id=1, source_target_pairs={{8,16},{12,20},{16,8},{20,12},{0,0},{4,4},{24,24},{28,28},{9,17},{... | collective-permute-start | bytes 1179656 | tf_op jit(solution)/shard_map/ppermute | solution.py:477
  391.3 23.8 %collective-permute-start.67 = (bf16[768,256]{1,0:T(8,128)(2,1)S(1)}, bf16[768,256]{1,0:T(8,128)(2,1)S(1)}, u32[]{:S(2)}, u32[]{:S(2)}) collective-permute-start(bf16[768,256]{1,0:T(8,128)(2,1)S(1)} %get-tuple-element.516.refs_3_), channel_id=1, source_target_pairs={{0,8},{4,12},{24,16},{28,20},{8,0},{12,4},{16,24},{20,28},{1,9},{5... | collective-permute-start | bytes 1179656 | tf_op jit(solution)/shard_map/ppermute | solution.py:476
  406.8 17.0 %collective-permute-start.77 = (bf16[768,256]{1,0:T(8,128)(2,1)S(1)}, bf16[768,256]{1,0:T(8,128)(2,1)S(1)}, u32[]{:S(2)}, u32[]{:S(2)}) collective-permute-start(bf16[768,256]{1,0:T(8,128)(2,1)S(1)} %get-tuple-element.549.refs_3_), channel_id=1, source_target_pairs={{0,8},{4,12},{24,16},{28,20},{8,0},{12,4},{16,24},{20,28},{1,9},{5... | collective-permute-start | bytes 1179656 | tf_op jit(solution)/shard_map/ppermute | solution.py:476
  432.9 16.4 %collective-permute-start.79 = (bf16[768,256]{1,0:T(8,128)(2,1)S(1)}, bf16[768,256]{1,0:T(8,128)(2,1)S(1)}, u32[]{:S(2)}, u32[]{:S(2)}) collective-permute-start(bf16[768,256]{1,0:T(8,128)(2,1)S(1)} %get-tuple-element.558.refs_3_), channel_id=1, source_target_pairs={{0,8},{4,12},{24,16},{28,20},{8,0},{12,4},{16,24},{20,28},{1,9},{5... | collective-permute-start | bytes 1179656 | tf_op jit(solution)/shard_map/ppermute | solution.py:476
  441.1 19.5 %collective-permute-start.86 = (bf16[768,256]{1,0:T(8,128)(2,1)S(1)}, bf16[768,256]{1,0:T(8,128)(2,1)S(1)}, u32[]{:S(2)}, u32[]{:S(2)}) collective-permute-start(bf16[768,256]{1,0:T(8,128)(2,1)S(1)} %get-tuple-element.576.refs_3_), channel_id=1, source_target_pairs={{0,8},{4,12},{24,16},{28,20},{8,0},{12,4},{16,24},{20,28},{1,9},{5... | collective-permute-start | bytes 1179656 | tf_op jit(solution)/shard_map/ppermute | solution.py:476
  444.2 16.4 %collective-permute-start.85 = (bf16[256,256]{1,0:T(8,128)(2,1)S(1)}, bf16[256,256]{1,0:T(8,128)(2,1)S(1)}, u32[]{:S(2)}, u32[]{:S(2)}) collective-permute-start(bf16[256,256]{1,0:T(8,128)(2,1)S(1)} %get-tuple-element.575.refs_3_), channel_id=1, source_target_pairs={{0,4},{4,0},{8,12},{12,8},{16,20},{20,16},{24,28},{28,24},{1,5},{5... | collective-permute-start | bytes 393224 | tf_op jit(solution)/shard_map/ppermute | solution.py:475
  450.3 16.6 %collective-permute-start.89 = (bf16[512,256]{1,0:T(8,128)(2,1)S(1)}, bf16[512,256]{1,0:T(8,128)(2,1)S(1)}, u32[]{:S(2)}, u32[]{:S(2)}) collective-permute-start(bf16[512,256]{1,0:T(8,128)(2,1)S(1)} %get-tuple-element.584.refs_2_), channel_id=1, source_target_pairs={{0,8},{4,12},{24,16},{28,20},{8,0},{12,4},{16,24},{20,28},{1,9},{5... | collective-permute-start | bytes 786440 | tf_op jit(solution)/shard_map/ppermute | solution.py:476
  (71 other events, 954.8 us)
Sparse Core Ops, SparseCore 0:
  9.5 109.2 all-gather.1
